TPU v7x, 32 devices: a whole 2x2x4 slice. The times are simulated.
32 devices in a mesh: dom: 32 (over z, y, x, core).
Axes of the slice: x: 2, y: 2, z: 4, core: 2. Of those that a mesh axis runs over, the one named last changes fastest.
Arguments:
- dofs: float32 [9, 35, 4096], P(None, None, 'dom'), may hold values from -6 to 6
- star: float32 [3, 9, 9, 4096], P(None, None, None, 'dom'), may hold values from -0.8 to 0.8
- flux_local: float32 [4, 9, 9, 4096], P(None, None, None, 'dom'), may hold values from -0.2 to 0.2
- flux_neigh: float32 [4, 9, 9, 4096], P(None, None, None, 'dom'), may hold values from -0.2 to 0.2
- neighbour: int32 [4, 4096], P(None, 'dom'), may hold values from 0 to 4095, as said below
- neighbour_face: int32 [4, 4096], P(None, 'dom'), may hold values from 0 to 3, as said below
- orientation: int32 [4, 4096], P(None, 'dom'), may hold values from 0 to 2, as said below
- face_kind: int32 [4, 4096], P(None, 'dom'), may hold values from 0 to 2
- cluster: int32 [4096], P('dom'), may hold values from 0 to 2, as said below
- deriv_stiff: float32 [3, 35, 35], replicated, may hold values from -1 to 1
- update_stiff: float32 [3, 35, 35], replicated, may hold values from -0.3125 to 0.3125
- face_proj: float32 [4, 15, 35], replicated, may hold values from -1 to 1
- face_lift: float32 [4, 35, 15], replicated, may hold values from -1.5 to 1.5
- orient_map: float32 [3, 15, 15], replicated, may hold values from -1.5 to 1.5
Outputs:
- advanced: float32 [9, 35, 4096], P(None, None, 'dom')
Inputs may be any that keep to these rules, and one draw needn't show every extreme that they name: Each partition (a block of 128 consecutive elements) holds exactly 32 elements of cluster 0, 32 of cluster 1 and 64 of cluster 2. The face relation is symmetric: if face f of element e has neighbour n and neighbour_face g, then face g of n has neighbour e and neighbour_face f, with the same orientation. Across an interior face the neighbour lies in the same partition or in a partition one or two apart along the loop of partitions, wrapping at the ends. Two partitions one apart share at most 64 faces and two partitions two apart at most 32; both bounds are reached. A face of kind 1 or 2 names its own element and its own face. `neighbour_face`: see neighbour. `orientation`: equal on both sides of an interior face; 0 on faces of kinds 1 and 2.
All inputs are finite; a program needn't handle non-finite values.
Results may differ from a plain program's by a relative error of at most 0.0003.
Values sent between devices are 32-bit elements; how exact they have to be, the bound alone decides.
No kernel may reach another device: no remote copies, remote signals or barrier semaphores. Data moves between devices by JAX's collectives and lax.ppermute only.
A program may use at most 128 MiB of HBM per device.

v0:
```python
import math

import jax
import jax.numpy as jnp
from jax import lax
from jax.sharding import PartitionSpec as P

ELEM_DEV = 128
FAST_DEV = 32
MIDDLE_DEV = 32
CAP_NEAR = 64
CAP_FAR = 32
QUANTITIES = 9
FACE_BASIS = 15
ORDER = 5
SLOTS = 4


HIGHEST = lax.Precision.HIGHEST
OFFSETS = (1, -1, 2, -2)


def from_behind(shard, axis, by):
    devices = lax.axis_size(axis)
    return lax.ppermute(shard, axis, [(i, (i + by) % devices) for i in range(devices)])


def taylor_terms(initial, star, deriv_stiff):
    terms = [initial]
    current = initial
    for degree in range(1, ORDER):
        contracted = jnp.einsum("dxy,pye->dpxe", deriv_stiff, current, precision=HIGHEST)
        current = -jnp.einsum("dqpe,dpxe->qxe", star, contracted, precision=HIGHEST)
        terms.append(current)
    return jnp.stack(terms)


def slot_weights(slot_offset):
    weights_list = []
    for degree in range(ORDER):
        upper = jnp.power(slot_offset + 1.0, degree + 1)
        lower = jnp.power(slot_offset, degree + 1)
        weights_list.append((upper - lower) / math.factorial(degree + 1))
    return jnp.stack(weights_list)


def step_weights(step_span):
    return jnp.stack(
        [jnp.power(step_span, degree + 1) / math.factorial(degree + 1) for degree in range(ORDER)]
    )


def weighted_sum(terms, weights):
    return jnp.sum(terms * weights[:, None, None, :], axis=0)


def update_state(
    fields,
    taylor,
    collected,
    star,
    flux_local,
    flux_neigh,
    orientation,
    face_kind,
    step_span,
    update_stiff,
    face_proj,
    face_lift,
    orient_map,
):
    step_integral = weighted_sum(taylor, step_weights(step_span))
    contracted = jnp.einsum("pye,dyx->dpxe", step_integral, update_stiff, precision=HIGHEST)
    volume = jnp.einsum("dqpe,dpxe->qxe", star, contracted, precision=HIGHEST)
    own_faces = jnp.einsum("fmb,qbe->qmfe", face_proj, step_integral, precision=HIGHEST)
    rotated = jnp.zeros_like(collected)
    for rotation in range(3):
        selected = (orientation == rotation).astype(jnp.float32)
        rotated = rotated + selected * jnp.einsum(
            "mn,qnfe->qmfe", orient_map[rotation], collected, precision=HIGHEST
        )
    mirror_signs = jnp.where(jnp.arange(QUANTITIES) < 6, -1.0, 1.0).astype(jnp.float32)
    mirrored = mirror_signs[:, None, None, None] * own_faces
    outside = jnp.where(
        face_kind == 0, rotated, jnp.where(face_kind == 1, mirrored, jnp.zeros_like(mirrored))
    )
    face_terms = jnp.einsum("fqpe,pmfe->qmfe", flux_local, own_faces, precision=HIGHEST)
    face_terms = face_terms + jnp.einsum("fqpe,pmfe->qmfe", flux_neigh, outside, precision=HIGHEST)
    lifted = jnp.einsum("fbm,qmfe->qbe", face_lift, face_terms, precision=HIGHEST)
    return fields + volume - lifted


def body(
    dofs,
    star,
    flux_local,
    flux_neigh,
    neighbour,
    neighbour_face,
    orientation,
    face_kind,
    cluster,
    deriv_stiff,
    update_stiff,
    face_proj,
    face_lift,
    orient_map,
):
    local_count = dofs.shape[2]
    devices = lax.axis_size("dom")
    my_index = lax.axis_index("dom")
    everyone = local_count * devices
    face_count = 4 * local_count
    owner_part = neighbour // local_count
    local_id = neighbour - owner_part * local_count
    distance = jnp.mod(owner_part - my_index, devices)
    interior = face_kind == 0
    capacity = (CAP_NEAR, CAP_NEAR, CAP_FAR, CAP_FAR)
    column_base = (0, CAP_NEAR, 2 * CAP_NEAR, 2 * CAP_NEAR + CAP_FAR)
    send_group = jnp.full(neighbour.shape, 4, jnp.int32)
    recv_group = jnp.full(neighbour.shape, 4, jnp.int32)
    for partner in range(4):
        send_group = jnp.where(
            interior & (distance == OFFSETS[partner] % devices), partner, send_group
        )
        recv_group = jnp.where(
            interior & (distance == -OFFSETS[partner] % devices), partner, recv_group
        )
    send_flat = send_group.reshape(-1)
    recv_flat = recv_group.reshape(-1)
    own_key = (
        jnp.arange(local_count, dtype=jnp.int32)[None, :] * 4
        + jnp.arange(4, dtype=jnp.int32)[:, None]
    ).reshape(-1)
    send_order = jnp.argsort(send_flat * face_count + own_key, stable=True)
    send_sizes = jnp.stack(
        [jnp.sum((send_flat == partner).astype(jnp.int32)) for partner in range(4)]
    )
    send_first = jnp.cumsum(send_sizes) - send_sizes
    send_index = []
    for partner in range(4):
        wanted = jnp.minimum(
            send_first[partner] + jnp.arange(capacity[partner], dtype=jnp.int32), face_count - 1
        )
        send_index.append(jnp.take(send_order, wanted))
    far_key = (neighbour * 4 + neighbour_face).reshape(-1)
    recv_order = jnp.argsort(recv_flat * (4 * everyone) + far_key, stable=True)
    recv_rank = jnp.argsort(recv_order, stable=True)
    recv_sizes = jnp.stack(
        [jnp.sum((recv_flat == partner).astype(jnp.int32)) for partner in range(4)]
    )
    recv_first = jnp.cumsum(recv_sizes) - recv_sizes
    start_of = jnp.zeros_like(recv_flat)
    base_of = jnp.zeros_like(recv_flat)
    for partner in range(4):
        start_of = jnp.where(recv_flat == partner, recv_first[partner], start_of)
        base_of = jnp.where(recv_flat == partner, column_base[partner], base_of)
    remote_source = face_count + base_of + recv_rank - start_of
    local_source = (neighbour_face * local_count + local_id).reshape(-1)
    source = jnp.where(recv_flat < 4, remote_source, local_source)
    span_whole = jnp.left_shift(jnp.ones_like(cluster), cluster)
    by_cluster = jnp.argsort(cluster, stable=True)
    levels = (FAST_DEV, FAST_DEV + MIDDLE_DEV, ELEM_DEV)
    sorted_rank = jnp.argsort(by_cluster, stable=True)

    def relabel(columns):
        face_part = columns // local_count
        return face_part * local_count + jnp.take(sorted_rank, columns - face_part * local_count)

    send_index = [relabel(entries) for entries in send_index]
    source_grid = jnp.take(source.reshape(4, local_count), by_cluster, axis=1)
    source = jnp.where(
        source_grid < face_count, relabel(jnp.minimum(source_grid, face_count - 1)), source_grid
    ).reshape(-1)
    fields = jnp.take(dofs, by_cluster, axis=2)
    star_work = jnp.take(star, by_cluster, axis=3)
    local_work = jnp.take(flux_local, by_cluster, axis=3)
    neigh_work = jnp.take(flux_neigh, by_cluster, axis=3)
    orient_work = jnp.take(orientation, by_cluster, axis=1)
    kind_work = jnp.take(face_kind, by_cluster, axis=1)
    span_work = jnp.take(span_whole, by_cluster, axis=0)
    span_float = span_work.astype(jnp.float32)
    taylor = jnp.zeros((ORDER,) + dofs.shape, jnp.float32)
    collected = jnp.zeros((QUANTITIES, FACE_BASIS, 4, local_count), jnp.float32)
    for slot_index in range(SLOTS):
        first_level = max((level for level in range(3) if slot_index % 2**level == 0))
        last_level = max((level for level in range(3) if (slot_index + 1) % 2**level == 0))
        begin_count = levels[first_level]
        renewed_terms = taylor_terms(
            fields[:, :, :begin_count], star_work[:, :, :, :begin_count], deriv_stiff
        )
        taylor = jnp.concatenate([renewed_terms, taylor[:, :, :, begin_count:]], axis=3)
        slot_offset = jnp.mod(slot_index, span_work).astype(jnp.float32)
        integral = weighted_sum(taylor, slot_weights(slot_offset))
        face_values = jnp.einsum("gmb,qbe->qmge", face_proj, integral, precision=HIGHEST)
        face_values = face_values.reshape(QUANTITIES * FACE_BASIS, face_count)
        buffers = [jnp.take(face_values, send_index[partner], axis=1) for partner in range(4)]
        near_in = [from_behind(buffers[partner], "dom", OFFSETS[partner]) for partner in (0, 1)]
        far_in = [from_behind(buffers[partner], "dom", OFFSETS[partner]) for partner in (2, 3)]
        sources_all = jnp.concatenate([face_values] + near_in + far_in, axis=1)
        collected = collected + jnp.take(sources_all, source, axis=1).reshape(
            QUANTITIES, FACE_BASIS, 4, local_count
        )
        end_count = levels[last_level]
        renewed = update_state(
            fields[:, :, :end_count],
            taylor[:, :, :, :end_count],
            collected[:, :, :, :end_count],
            star_work[:, :, :, :end_count],
            local_work[:, :, :, :end_count],
            neigh_work[:, :, :, :end_count],
            orient_work[:, :end_count],
            kind_work[:, :end_count],
            span_float[:end_count],
            update_stiff,
            face_proj,
            face_lift,
            orient_map,
        )
        fields = jnp.concatenate([renewed, fields[:, :, end_count:]], axis=2)
        collected = jnp.concatenate(
            [jnp.zeros_like(collected[:, :, :, :end_count]), collected[:, :, :, end_count:]], axis=3
        )
    fields = jnp.take(fields, sorted_rank, axis=2)
    return fields


def solution(mesh):
    in_specs = (
        P(None, None, "dom"),
        P(None, None, None, "dom"),
        P(None, None, None, "dom"),
        P(None, None, None, "dom"),
        P(None, "dom"),
        P(None, "dom"),
        P(None, "dom"),
        P(None, "dom"),
        P("dom"),
        P(),
        P(),
        P(),
        P(),
        P(),
    )
    out_specs = P(None, None, "dom")
    return jax.shard_map(body, mesh=mesh, in_specs=in_specs, out_specs=out_specs, check_vma=False)
```

profile of v0, /device:TPU:0, one launch (start us, length us, event | category | flops | bytes accessed | tf_op | source)
XLA Modules:
  0.0 578.2 jit_solution(10778932269495554035)
XLA Ops:
  15.9 4.0 gather_fusion
  19.9 13.4 %fusion.11 = f32[128,35,9]{1,2,0:T(8,128)S(1)} fusion(f32[3,9,35,128]{2,1,0,3:T(8,128)} %copy.713, f32[128,3,9,9]{3,1,2,0:T(4,128)S(1)} %gather_fusion, pred[128]{0:T(512)(128)(4,1)S(1)} %get-tuple-element.41), kind=kOutput, calls=%fused_computation.59 | convolution fusion | flops 13135104 | bytes 769664 | tf_op jit(solution)/shard_map/dqpe,dpxe->qxe/dot_general | solution.py:33
  38.1 13.4 %fusion.12 = f32[128,35,9]{1,2,0:T(8,128)S(1)} fusion(f32[3,9,35,128]{2,1,0,3:T(8,128)} %copy.715, f32[128,3,9,9]{3,1,2,0:T(4,128)S(1)} %gather_fusion, pred[128]{0:T(512)(128)(4,1)S(1)} %get-tuple-element.41), kind=kOutput, calls=%fused_computation.60 | convolution fusion | flops 13135104 | bytes 769664 | tf_op jit(solution)/shard_map/dqpe,dpxe->qxe/dot_general | solution.py:33
  63.9 14.3 %fusion.13 = f32[128,35,9]{1,2,0:T(8,128)} fusion(f32[3,9,35,128]{2,1,0,3:T(8,128)} %copy.717, f32[128,3,9,9]{3,1,2,0:T(4,128)S(1)} %gather_fusion, pred[128]{0:T(512)(128)(4,1)S(1)} %get-tuple-element.41), kind=kOutput, calls=%fused_computation.61 | convolution fusion | flops 13135104 | bytes 769664 | tf_op jit(solution)/shard_map/dqpe,dpxe->qxe/dot_general | solution.py:33
  83.3 11.7 %copy.719 = f32[3,9,35,128]{2,1,0,3:T(8,128)} copy(f32[3,9,35,128]{3,2,0,1:T(8,128)} %convolution_bitcast_fusion.11) | data formatting | bytes 967680 | tf_op jit(solution)/shard_map/dxy,pye->dpxe/transpose | solution.py:32
  95.0 14.3 %fusion.15 = f32[1,9,35,128]{2,1,3,0:T(8,128)} fusion(f32[3,9,35,128]{2,1,0,3:T(8,128)} %copy.719, f32[128,3,9,9]{3,1,2,0:T(4,128)S(1)} %gather_fusion, pred[128]{0:T(512)(128)(4,1)S(1)} %get-tuple-element.41), kind=kOutput, calls=%fused_computation.63 | convolution fusion | flops 13135104 | bytes 769664 | tf_op jit(solution)/shard_map/dqpe,dpxe->qxe/dot_general | solution.py:33
  144.9 3.8 sort.79
  165.3 5.9 %collective-permute-start.1 = (f32[135,64]{0,1:T(8,128)}, f32[135,64]{0,1:T(8,128)}, u32[]{:S(2)}, u32[]{:S(2)}) collective-permute-start(f32[135,64]{0,1:T(8,128)} %select_bitcast_fusion.14), channel_id=1, source_target_pairs={{0,31},{1,0},{2,1},{3,2},{4,3},{5,4},{6,5},{7,6},{8,7},{9,8},{10,9... | collective-permute-start | bytes 103688 | tf_op jit(solution)/shard_map/ppermute | solution.py:25
  176.7 5.6 collective-permute-start.3
  203.3 5.4 gather_fusion.4
  211.4 5.4 gather_fusion.21
  220.3 4.6 fusion
  249.3 4.6 fusion.10
  298.2 5.1 collective-permute-start.7
  323.0 5.8 %fusion.3 = f32[4,64,15,9]{3,2,1,0:T(8,128)S(1)} fusion(f32[9,15,4,64]{0,1,3,2:T(8,128)} %copy.784, f32[4,9,9,128]{2,1,3,0:T(8,128)} %get-tuple-element.114), kind=kOutput, calls=%fused_computation.45 | convolution fusion | flops 3732480 | bytes 4332544 | tf_op jit(solution)/shard_map/fqpe,pmfe->qmfe/dot_general | solution.py:88
  328.9 4.8 add_bitcast_fusion.1
  337.6 4.3 fusion.24
  346.6 3.8 fusion.18
  355.9 3.8 fusion.19
  365.1 3.8 fusion.20
  374.4 4.7 fusion.22
  414.0 5.4 collective-permute-start.9
  422.5 4.3 fusion.65
  441.2 4.6 fusion.9
  487.3 4.1 collective-permute-start.12
  492.1 3.8 collective-permute-start.13
  499.6 12.1 %fusion.222 = f32[4,128,15,9]{3,2,1,0:T(8,128)} fusion(f32[9,15,4,128]{0,1,3,2:T(8,128)} %copy.837, f32[128,4,9,9]{3,1,2,0:T(4,128)} %gather_fusion.4, pred[128]{0:T(512)(128)(4,1)S(1)} %get-tuple-element.41), kind=kOutput, calls=%fused_computation.586 | convolution fusion | flops 7506432 | bytes 718976 | tf_op jit(solution)/shard_map/fqpe,pmfe->qmfe/dot_general | solution.py:87
  512.4 5.6 collective-permute-start.15
  534.2 3.9 copy.849
  538.1 13.3 %add_bitcast_fusion = f32[9,15,4,128]{0,1,3,2:T(8,128)} fusion(f32[4,128,15,9]{3,2,1,0:T(8,128)} %fusion.222, f32[9,15,4,128]{0,1,3,2:T(8,128)} %copy.849, f32[128,4,9,9]{3,1,2,0:T(4,128)} %gather_fusion.21, pred[128]{0:T(512)(128)(4,1)S(1)} %get-tuple-element.41), kind=kOutput, calls=%fused_computation.42 | convolution fusion | flops 7575552 | bytes 995456 | tf_op jit(solution)/shard_map/fqpe,pmfe->qmfe/dot_general | solution.py:88
  551.4 4.1 copy.850
  560.0 14.8 %fusion.17 = f32[9,35,128]{1,0,2:T(8,128)} fusion(f32[3,9,35,128]{2,1,0,3:T(8,128)} %copy.834, f32[9,35,64]{1,0,2:T(8,128)S(1)} %copy-done.32, f32[9,35,64]{1,0,2:T(8,128)S(1)} %copy-done.14, f32[9,35,32]{1,0,2:T(8,128)} %copy-done.33, f32[9,128,35]{2,0,1:T(8,128)} %copy.852, f32[128,3,9,9]{3,1,2,0:T(4,128)S(1)} %gather_fusion, ...), kind=kOutput, calls=%fused_computation.65 | convolution fusion | flops 13336704 | bytes 1132544 | tf_op jit(solution)/shard_map/dqpe,dpxe->qxe/dot_general | solution.py:74
  (553 shorter events, 357.6 us)
Async XLA Ops:
  3.9 182.3 %copy-start.57 = (s32[1024]{0:T(1024)}, s32[1024]{0:T(1024)S(1)}, u32[]{:S(2)}) copy-start(s32[1024]{0:T(1024)S(1)} %pad_clamp_fusion.15) | copy-start | bytes 12292
  156.5 15.3 %copy-start.60 = (pred[64]{0:T(512)(128)(4,1)}, pred[64]{0:T(512)(128)(4,1)S(1)}, u32[]{:S(2)}) copy-start(pred[64]{0:T(512)(128)(4,1)S(1)} %get-tuple-element.69) | copy-start | bytes 196
  157.9 77.8 %collective-permute-start = (f32[135,64]{0,1:T(8,128)}, f32[135,64]{0,1:T(8,128)}, u32[]{:S(2)}, u32[]{:S(2)}) collective-permute-start(f32[135,64]{0,1:T(8,128)} %select_bitcast_fusion.15), channel_id=1, source_target_pairs={{0,1},{1,2},{2,3},{3,4},{4,5},{5,6},{6,7},{7,8},{8,9},{9,10},{10,1... | collective-permute-start | bytes 103688 | tf_op jit(solution)/shard_map/ppermute | solution.py:25
  163.9 19.4 %copy-start.62 = (pred[32]{0:T(512)(128)(4,1)}, pred[32]{0:T(512)(128)(4,1)S(1)}, u32[]{:S(2)}) copy-start(pred[32]{0:T(512)(128)(4,1)S(1)} %get-tuple-element.59) | copy-start | bytes 100
  165.3 71.3 %collective-permute-start.1 = (f32[135,64]{0,1:T(8,128)}, f32[135,64]{0,1:T(8,128)}, u32[]{:S(2)}, u32[]{:S(2)}) collective-permute-start(f32[135,64]{0,1:T(8,128)} %select_bitcast_fusion.14), channel_id=1, source_target_pairs={{0,31},{1,0},{2,1},{3,2},{4,3},{5,4},{6,5},{7,6},{8,7},{9,8},{10,9... | collective-permute-start | bytes 103688 | tf_op jit(solution)/shard_map/ppermute | solution.py:25
  171.9 65.5 %collective-permute-start.2 = (f32[135,32]{0,1:T(8,128)S(1)}, f32[135,32]{0,1:T(8,128)}, u32[]{:S(2)}, u32[]{:S(2)}) collective-permute-start(f32[135,32]{0,1:T(8,128)S(1)} %select_bitcast_fusion.23), channel_id=1, source_target_pairs={{0,2},{1,3},{2,4},{3,5},{4,6},{5,7},{6,8},{7,9},{8,10},{9,11},{10,... | collective-permute-start | bytes 51848 | tf_op jit(solution)/shard_map/ppermute | solution.py:25
  176.7 61.5 %collective-permute-start.3 = (f32[135,32]{0,1:T(8,128)}, f32[135,32]{0,1:T(8,128)}, u32[]{:S(2)}, u32[]{:S(2)}) collective-permute-start(f32[135,32]{0,1:T(8,128)} %select_bitcast_fusion.22), channel_id=1, source_target_pairs={{0,30},{1,31},{2,0},{3,1},{4,2},{5,3},{6,4},{7,5},{8,6},{9,7},{10,... | collective-permute-start | bytes 51848 | tf_op jit(solution)/shard_map/ppermute | solution.py:25
  231.8 13.0 %copy-start.41 = (f32[3,15,15]{2,1,0:T(8,128)S(1)}, f32[3,15,15]{2,1,0:T(8,128)}, u32[]{:S(2)}) copy-start(f32[3,15,15]{2,1,0:T(8,128)} %param.47) | copy-start | bytes 8104
  231.8 13.0 %copy-start.50 = (f32[4,32]{1,0:T(4,128)S(1)}, f32[4,32]{1,0:T(4,128)}, u32[]{:S(2)}) copy-start(f32[4,32]{1,0:T(4,128)} %get-tuple-element.92) | copy-start | bytes 1540
  289.4 20.6 %copy-start.9 = (f32[135,704]{0,1:T(8,128)S(1)}, f32[135,704]{0,1:T(8,128)}, u32[]{:S(2)}) copy-start(f32[135,704]{0,1:T(8,128)} %constant_dynamic-update-slice_fusion.14) | copy-start | bytes 1140484
  293.3 18.4 %collective-permute-start.6 = (f32[135,32]{0,1:T(8,128)}, f32[135,32]{0,1:T(8,128)}, u32[]{:S(2)}, u32[]{:S(2)}) collective-permute-start(f32[135,32]{0,1:T(8,128)} %select_bitcast_fusion.21), channel_id=1, source_target_pairs={{0,2},{1,3},{2,4},{3,5},{4,6},{5,7},{6,8},{7,9},{8,10},{9,11},{10,... | collective-permute-start | bytes 51848 | tf_op jit(solution)/shard_map/ppermute | solution.py:25
  294.3 16.6 %collective-permute-start.5 = (f32[135,64]{0,1:T(8,128)S(1)}, f32[135,64]{0,1:T(8,128)}, u32[]{:S(2)}, u32[]{:S(2)}) collective-permute-start(f32[135,64]{0,1:T(8,128)S(1)} %select_bitcast_fusion.12), channel_id=1, source_target_pairs={{0,31},{1,0},{2,1},{3,2},{4,3},{5,4},{6,5},{7,6},{8,7},{9,8},{10,9... | collective-permute-start | bytes 103688 | tf_op jit(solution)/shard_map/ppermute | solution.py:25
  296.9 13.1 %collective-permute-start.4 = (f32[135,64]{0,1:T(8,128)}, f32[135,64]{0,1:T(8,128)}, u32[]{:S(2)}, u32[]{:S(2)}) collective-permute-start(f32[135,64]{0,1:T(8,128)} %select_bitcast_fusion.13), channel_id=1, source_target_pairs={{0,1},{1,2},{2,3},{3,4},{4,5},{5,6},{6,7},{7,8},{8,9},{9,10},{10,1... | collective-permute-start | bytes 103688 | tf_op jit(solution)/shard_map/ppermute | solution.py:25
  298.2 14.3 %collective-permute-start.7 = (f32[135,32]{0,1:T(8,128)}, f32[135,32]{0,1:T(8,128)S(1)}, u32[]{:S(2)}, u32[]{:S(2)}) collective-permute-start(f32[135,32]{0,1:T(8,128)} %select_bitcast_fusion.20), channel_id=1, source_target_pairs={{0,30},{1,31},{2,0},{3,1},{4,2},{5,3},{6,4},{7,5},{8,6},{9,7},{10,... | collective-permute-start | bytes 51848 | tf_op jit(solution)/shard_map/ppermute | solution.py:25
  341.9 44.1 %copy-start.12 = (f32[9,35,64]{1,0,2:T(8,128)}, f32[9,35,64]{1,0,2:T(8,128)S(1)}, u32[]{:S(2)}) copy-start(f32[9,35,64]{1,0,2:T(8,128)S(1)} %fusion.24) | copy-start | bytes 241924
  379.1 12.5 %copy-start.54 = (f32[5,128]{1,0:T(8,128)S(1)}, f32[5,128]{1,0:T(8,128)}, u32[]{:S(2)}) copy-start(f32[5,128]{1,0:T(8,128)} %stack.226) | copy-start | bytes 7684
  409.4 17.4 %copy-start.44 = (f32[32,135]{1,0:T(8,128)S(1)}, f32[32,135]{1,0:T(8,128)}, u32[]{:S(2)}) copy-start(f32[32,135]{1,0:T(8,128)} %gather_fusion.30) | copy-start | bytes 51844
  409.4 19.2 %copy-start.10 = (f32[135,704]{0,1:T(8,128)S(1)}, f32[135,704]{0,1:T(8,128)}, u32[]{:S(2)}) copy-start(f32[135,704]{0,1:T(8,128)} %constant_dynamic-update-slice_fusion.24) | copy-start | bytes 1140484
  413.1 17.2 %collective-permute-start.10 = (f32[135,32]{0,1:T(8,128)}, f32[135,32]{0,1:T(8,128)}, u32[]{:S(2)}, u32[]{:S(2)}) collective-permute-start(f32[135,32]{0,1:T(8,128)} %select_bitcast_fusion.19), channel_id=1, source_target_pairs={{0,2},{1,3},{2,4},{3,5},{4,6},{5,7},{6,8},{7,9},{8,10},{9,11},{10,... | collective-permute-start | bytes 51848 | tf_op jit(solution)/shard_map/ppermute | solution.py:25
  414.0 15.4 %collective-permute-start.9 = (f32[135,64]{0,1:T(8,128)S(1)}, f32[135,64]{0,1:T(8,128)}, u32[]{:S(2)}, u32[]{:S(2)}) collective-permute-start(f32[135,64]{0,1:T(8,128)S(1)} %select_bitcast_fusion.10), channel_id=1, source_target_pairs={{0,31},{1,0},{2,1},{3,2},{4,3},{5,4},{6,5},{7,6},{8,7},{9,8},{10,9... | collective-permute-start | bytes 103688 | tf_op jit(solution)/shard_map/ppermute | solution.py:25
  421.0 7.6 %collective-permute-start.8 = (f32[135,64]{0,1:T(8,128)}, f32[135,64]{0,1:T(8,128)}, u32[]{:S(2)}, u32[]{:S(2)}) collective-permute-start(f32[135,64]{0,1:T(8,128)} %select_bitcast_fusion.11), channel_id=1, source_target_pairs={{0,1},{1,2},{2,3},{3,4},{4,5},{5,6},{6,7},{7,8},{8,9},{9,10},{10,1... | collective-permute-start | bytes 103688 | tf_op jit(solution)/shard_map/ppermute | solution.py:25
  427.5 3.9 collective-permute-start.11
  474.6 16.8 %copy-start.67 = (pred[64]{0:T(512)(128)(4,1)S(1)}, pred[64]{0:T(512)(128)(4,1)}, u32[]{:S(2)}) copy-start(pred[64]{0:T(512)(128)(4,1)} %copy-done.66) | copy-start | bytes 196
  474.6 21.3 %copy-start.65 = (pred[32]{0:T(512)(128)(4,1)S(1)}, pred[32]{0:T(512)(128)(4,1)}, u32[]{:S(2)}) copy-start(pred[32]{0:T(512)(128)(4,1)} %copy-done.62) | copy-start | bytes 100
  478.8 17.1 %copy-start.46 = (f32[32,135]{1,0:T(8,128)S(1)}, f32[32,135]{1,0:T(8,128)}, u32[]{:S(2)}) copy-start(f32[32,135]{1,0:T(8,128)} %gather_fusion.34) | copy-start | bytes 51844
  484.0 15.6 %copy-start.26 = (f32[9,15,4,128]{3,1,2,0:T(8,128)}, f32[9,15,4,128]{3,1,2,0:T(8,128)S(1)}, u32[]{:S(2)}) copy-start(f32[9,15,4,128]{3,1,2,0:T(8,128)S(1)} %convolution_bitcast_fusion.34) | copy-start | bytes 829444
  487.3 34.1 %collective-permute-start.12 = (f32[135,64]{0,1:T(8,128)S(1)}, f32[135,64]{0,1:T(8,128)}, u32[]{:S(2)}, u32[]{:S(2)}) collective-permute-start(f32[135,64]{0,1:T(8,128)S(1)} %select_bitcast_fusion.9), channel_id=1, source_target_pairs={{0,1},{1,2},{2,3},{3,4},{4,5},{5,6},{6,7},{7,8},{8,9},{9,10},{10,1... | collective-permute-start | bytes 103688 | tf_op jit(solution)/shard_map/ppermute | solution.py:25
  492.1 30.2 %collective-permute-start.13 = (f32[135,64]{0,1:T(8,128)}, f32[135,64]{0,1:T(8,128)}, u32[]{:S(2)}, u32[]{:S(2)}) collective-permute-start(f32[135,64]{0,1:T(8,128)} %select_bitcast_fusion.8), channel_id=1, source_target_pairs={{0,31},{1,0},{2,1},{3,2},{4,3},{5,4},{6,5},{7,6},{8,7},{9,8},{10,9... | collective-permute-start | bytes 103688 | tf_op jit(solution)/shard_map/ppermute | solution.py:25
  496.6 26.5 %collective-permute-start.14 = (f32[135,32]{0,1:T(8,128)}, f32[135,32]{0,1:T(8,128)}, u32[]{:S(2)}, u32[]{:S(2)}) collective-permute-start(f32[135,32]{0,1:T(8,128)} %select_bitcast_fusion.17), channel_id=1, source_target_pairs={{0,2},{1,3},{2,4},{3,5},{4,6},{5,7},{6,8},{7,9},{8,10},{9,11},{10,... | collective-permute-start | bytes 51848 | tf_op jit(solution)/shard_map/ppermute | solution.py:25
  512.4 14.5 %copy-start.59 = (pred[512]{0:T(512)(128)(4,1)S(1)}, pred[512]{0:T(512)(128)(4,1)}, u32[]{:S(2)}) copy-start(pred[512]{0:T(512)(128)(4,1)} %get-tuple-element.47) | copy-start | bytes 1540
  512.4 11.5 %collective-permute-start.15 = (f32[135,32]{0,1:T(8,128)}, f32[135,32]{0,1:T(8,128)}, u32[]{:S(2)}, u32[]{:S(2)}) collective-permute-start(f32[135,32]{0,1:T(8,128)} %select_bitcast_fusion.16), channel_id=1, source_target_pairs={{0,30},{1,31},{2,0},{3,1},{4,2},{5,3},{6,4},{7,5},{8,6},{9,7},{10,... | collective-permute-start | bytes 51848 | tf_op jit(solution)/shard_map/ppermute | solution.py:25
  560.0 16.8 %copy-start.107 = (pred[128]{0:T(512)(128)(4,1)S(1)}, pred[128]{0:T(512)(128)(4,1)}, u32[]{:S(2)}) copy-start(pred[128]{0:T(512)(128)(4,1)} %compare_and_fusion) | copy-start | bytes 388
  (92 other events, 626.9 us)
where the time goes:
time: 587 us; the launch traced here: 578 us
  local copies, waits for them, and re-layouts  224 us (38%)
  matrix products  223 us (38%)
  other arithmetic  90.9 us (15%)
  starting transfers between devices  37.8 us (6%)
    dot_general x16, matrix products, taylor_terms(): current = -jnp.einsum('dqpe,dpxe->qxe', star, contracted, precision=HIGHEST)  88.3 us
    unnamed x263, local copies, waits for them, and re-layouts  48.4 us
    ppermute x16, starting transfers between devices, from_behind(): lax.ppermute(shard, axis, [(i, (i + by) % devices) for i in range(devices)])  37.8 us
    transpose x8, local copies, waits for them, and re-layouts, taylor_terms(): jnp.einsum('dxy,pye->dpxe', deriv_stiff, current, precision=HIGHEST)  32 us
    dot_general x4, matrix products, update_state(): jnp.einsum('fqpe,pmfe->qmfe', flux_neigh, outside, precision=HIGHEST)  28.4 us
    dot_general x4, matrix products, update_state(): volume = jnp.einsum('dqpe,dpxe->qxe', star, contracted, precision=HIGHEST)  25.9 us
    dot_general x4, matrix products, update_state(): jnp.einsum('fqpe,pmfe->qmfe', flux_local, own_faces, precision=HIGHEST)  23.9 us
    another operation x14, local copies, waits for them, and re-layouts, taylor_terms(): return jnp.stack(terms)  23.7 us
  transfers between devices with their start and end apart: 16, of which 2 were waited for; matrix products, arithmetic and copies ran while one was open for 20% of the time, Pallas kernels for 0%

commit v1 on v0

v1 whole, which is shorter than its diff:
```python
import functools
import math
import types

import jax
import jax.numpy as jnp
from jax import lax
from jax.experimental import pallas as pl
from jax.experimental.pallas import tpu as pltpu
from jax.sharding import PartitionSpec as P

CAP_NEAR = 64
CAP_FAR = 32
QUANTITIES = 9
BASIS = 35
BASIS_PAD = 40
FACE_BASIS = 15
FACE_PAD = 16
FACES = 4
ORDER = 5
SLOTS = 4
LANES = 128
FACE_ROWS = QUANTITIES * FACE_PAD
SEND_ROWS = 80
PACK = 32
GROUPS = LANES // PACK
PACKS = 3

OFFSETS = (1, -1, 2, -2)
SEND_ORDER = (2, 1, 3, 0)
F32 = jnp.float32
BF16 = jnp.bfloat16
VMEM = pl.BlockSpec(memory_space=pltpu.VMEM)
NAMES = ("sent_a", "sent_x", "sent_y", "sent_z")


def exchange(sends):
    devices = lax.axis_size("dom")
    receives = {}
    for partner in SEND_ORDER:
        by = OFFSETS[partner]
        pairs = [(i, (i + (by if i % 2 == 0 else -by)) % devices) for i in range(devices)]
        receives[RECEIVED[partner]] = lax.ppermute(sends[NAMES[partner]], "dom", pairs)
    return receives


def split(x):
    high = x.astype(BF16).astype(F32)
    return high, x - high


def wide_basis(matrix):
    high, low = split(matrix)
    return high + pltpu.roll(high, 40, 1) + pltpu.roll(low, 80, 1)


def tall_basis(x):
    high, low = split(x)
    rest = jnp.zeros((LANES - 3 * BASIS_PAD, x.shape[1]), F32)
    return jnp.concatenate([high, low, high, rest], axis=0).astype(BF16)


def wide_faces(matrix):
    high, low = split(matrix)
    return jnp.concatenate([high + pltpu.roll(high, 64, 1), low], axis=1)


def tall_faces(x):
    high, low = split(x)
    return jnp.concatenate([high, low, high], axis=0).astype(BF16)


def matmul(left, right):
    return jnp.dot(left.astype(BF16), right, preferred_element_type=F32)


def side_by_side(pieces):
    return jnp.concatenate(pieces, axis=1)


def lanes_of(q):
    return slice(q * LANES, (q + 1) * LANES)


def star_tile(star, work, quantities, groups):
    total = [None] * len(quantities)
    for d in range(3):
        for p in range(groups):
            piece = work[d * BASIS_PAD : (d + 1) * BASIS_PAD, lanes_of(p)]
            for i, q in enumerate(quantities):
                term = star[q, p, d : d + 1, :] * piece
                total[i] = term if total[i] is None else total[i] + term
    return total


def apply_star(star, work, put):
    for first in range(0, QUANTITIES, 3):
        for i, value in enumerate(star_tile(star, work, range(first, first + 3), QUANTITIES)):
            put(first + i, value)


def apply_flux(flux, faces, lift_in):
    for f in range(FACES):
        total = [None] * QUANTITIES
        for p in range(QUANTITIES):
            piece = faces(f, p)
            for q in range(QUANTITIES):
                term = flux[q, p, f : f + 1, :] * piece
                total[q] = term if total[q] is None else total[q] + term
        for q in range(QUANTITIES):
            lift_in[f * FACE_PAD : (f + 1) * FACE_PAD, lanes_of(q)] = total[q]


def lift(lift_w, lift_in):
    right = side_by_side([tall_faces(lift_in[:, lanes_of(q)]) for q in range(QUANTITIES)])
    return matmul(lift_w[0:48, :192], right)


def predict(taylor, star, deriv_w, works):
    for k in range(ORDER):
        for first in range(0, QUANTITIES, 3):
            if k:
                values = star_tile(star, works[k % 2], range(first, first + 3), QUANTITIES)
                for i in range(3):
                    taylor[k, first + i] = values[i]
            else:
                values = [taylor[0, first + i] for i in range(3)]
            if k < ORDER - 1:
                right = side_by_side([tall_basis(value) for value in values])
                works[(k + 1) % 2][:, first * LANES : (first + 3) * LANES] = matmul(deriv_w[...], right)


def integral(taylor, q, j):
    total = None
    for k in range(ORDER):
        weight = ((j + 1) ** (k + 1) - j ** (k + 1)) / math.factorial(k + 1)
        term = taylor[k, q] * weight
        total = term if total is None else total + term
    return total


def step_integral(taylor, q, span):
    total = None
    power = span
    for k in range(ORDER):
        term = taylor[k, q] * (power * (1.0 / math.factorial(k + 1)))
        total = term if total is None else total + term
        power = power * span
    return total


def rotated_faces(turn_w, orientation, integrals, put):
    right = side_by_side([tall_basis(value) for value in integrals])
    result = matmul(turn_w[...], right)
    for g in range(FACES):
        turn = orientation[g : g + 1, :]
        for q in range(QUANTITIES):
            parts = []
            for o in range(3):
                first = (o * FACES + g) * FACE_PAD
                parts.append(result[first : first + FACE_PAD, lanes_of(q)])
            put(g, q, jnp.where(turn == 0, parts[0], jnp.where(turn == 1, parts[1], parts[2])))


def rows_of(q):
    return slice(q * FACE_PAD, (q + 1) * FACE_PAD)


def take_lanes(source, index):
    if source.shape[0] == 1:
        return take_lanes(jnp.broadcast_to(source, (8, LANES)), index)[0:1, :]
    return jnp.take_along_axis(source, jnp.broadcast_to(index, source.shape), axis=1)


def turn_lanes(x, shift):
    return pltpu.roll(x, shift % LANES, 1) if shift % LANES else x


def choose(pieces, lane, width):
    total = pieces[0]
    for j in range(1, len(pieces)):
        total = jnp.where(lane // width == j, pieces[j], total)
    return total


def pack_sends(faces, index, sends):
    tiles = []
    for row in (0, 2):
        lane = index[row : row + 1, :]
        face = index[row + 1 : row + 2, :]
        tile = take_lanes(faces[0], lane)
        for g in range(1, FACES):
            tile = jnp.where(face == g, take_lanes(faces[g], lane), tile)
        tiles.append(tile)
    lane = lax.broadcasted_iota(jnp.int32, (FACE_PAD, LANES), 1)
    nothing = jnp.zeros((FACE_PAD, LANES), F32)

    def piece(tile, q):
        return tiles[tile][rows_of(q), :] if q < QUANTITIES else nothing

    for k in range(5):
        low, high = piece(0, 2 * k), piece(0, 2 * k + 1)
        sends[0][rows_of(k), :] = choose([low, turn_lanes(high, 64)], lane, 64)
        sends[1][rows_of(k), :] = choose([turn_lanes(low, 64), high], lane, 64)
    for k in range(5):
        for side in range(2):
            value = nothing
            if k < PACKS:
                parts = [turn_lanes(piece(1, 4 * k + j), 32 * j - 64 * side) for j in range(4)]
                value = choose(parts, lane, 32)
            sends[2 + side][rows_of(k), :] = value


def unpack_receives(receives, near, far):
    lane = lax.broadcasted_iota(jnp.int32, (FACE_PAD, LANES), 1)
    for q in range(QUANTITIES):
        ahead, behind = receives[0][rows_of(q // 2), :], receives[1][rows_of(q // 2), :]
        shift = 64 * (q % 2)
        near[rows_of(q), :] = choose([turn_lanes(ahead, shift), turn_lanes(behind, 64 + shift)], lane, 64)
        ahead, behind = receives[2][rows_of(q // 4), :], receives[3][rows_of(q // 4), :]
        shift = -32 * (q % 4)
        far[rows_of(q), :] = choose([turn_lanes(ahead, shift), turn_lanes(behind, 64 + shift)], lane, 64)


def add_remote(index, near, far, collected, put):
    for f in range(FACES):
        place = index[f : f + 1, :]
        lane = jnp.bitwise_and(place, LANES - 1)
        from_near = take_lanes(near[...], lane)
        from_far = take_lanes(far[...], lane)
        remote = jnp.where(place >= LANES, from_far, jnp.where(place >= 0, from_near, 0.0))
        put(f, collected[f] + remote)


def transposed(rows, flip):
    flip[...] = jnp.zeros((LANES, LANES), F32)
    for f in range(FACES):
        flip[f : f + 1, :] = rows[f]
    return flip[...].T


def ranks(keys, flip):
    columns = transposed(keys, flip)
    result = []
    for f in range(FACES):
        total = None
        for other in range(FACES):
            less = jnp.where(columns[:, other : other + 1] < keys[f], 1.0, 0.0)
            total = less if total is None else total + less
        result.append(jnp.sum(total, axis=0, keepdims=True))
    return result


def group_places(groups, keys, flip):
    bases = (0.0, 64.0, 128.0, 192.0)
    order = ranks([groups[f] * 512.0 + keys[f] for f in range(FACES)], flip)
    sizes = []
    for partner in range(FACES):
        total = None
        for f in range(FACES):
            here = jnp.where(groups[f] == partner, 1.0, 0.0)
            total = here if total is None else total + here
        sizes.append(jnp.sum(total, axis=1, keepdims=True))
    places = []
    for f in range(FACES):
        place = jnp.full((1, LANES), -1.0, F32)
        start = jnp.zeros((1, 1), F32)
        for partner in range(FACES):
            place = jnp.where(groups[f] == partner, order[f] - start + bases[partner], place)
            start = start + sizes[partner]
        places.append(place)
    return places


def partner_groups(devices, neighbour, face_kind):
    here = lax.axis_index("dom")
    sign = 1 - 2 * jnp.bitwise_and(here, 1)
    targets = [jnp.where(sign * by < 0, sign * by + devices, sign * by) for by in OFFSETS]
    sources = targets[:2] + [devices - far for far in targets[2:]]
    send_groups, recv_groups, local = [], [], []
    for f in range(FACES):
        interior = face_kind[f : f + 1, :] == 0
        distance = lax.shift_right_logical(neighbour[f : f + 1, :], 7) - here
        distance = jnp.where(distance < 0, distance + devices, distance)
        send = jnp.full((1, LANES), 4, jnp.int32)
        recv = jnp.full((1, LANES), 4, jnp.int32)
        for partner in range(4):
            send = jnp.where(interior & (distance == targets[partner]), partner, send)
            recv = jnp.where(interior & (distance == sources[partner]), partner, recv)
        send_groups.append(send.astype(F32))
        recv_groups.append(recv.astype(F32))
        local.append(interior & (distance == 0))
    return send_groups, recv_groups, local


def make_send_index(devices, neighbour, face_kind, index, flip):
    groups, _, _ = partner_groups(devices, neighbour, face_kind)
    element = lax.broadcasted_iota(jnp.int32, (1, LANES), 1)
    keys = [(element + f * LANES).astype(F32) for f in range(FACES)]
    places = group_places(groups, keys, flip)
    for tile, (element, face) in enumerate(columns_of(places, flip)):
        index[2 * tile : 2 * tile + 1, :] = element
        index[2 * tile + 1 : 2 * tile + 2, :] = face


def columns_of(places, flip):
    columns = transposed(places, flip)
    row = lax.broadcasted_iota(jnp.int32, (LANES, LANES), 0).astype(F32)
    lane = lax.broadcasted_iota(jnp.int32, (LANES, LANES), 1).astype(F32)
    result = []
    for tile in range(2):
        total = None
        for f in range(FACES):
            hit = jnp.where(columns[:, f : f + 1] == lane + tile * 128.0, row + f * 128.0, 0.0)
            total = hit if total is None else total + hit
        code = jnp.sum(total, axis=0, keepdims=True).astype(jnp.int32)
        result.append((jnp.bitwise_and(code, LANES - 1), lax.shift_right_logical(code, 7)))
    return result


def make_recv_index(devices, neighbour, neighbour_face, face_kind, index, flip):
    _, groups, local = partner_groups(devices, neighbour, face_kind)
    index[...] = jnp.zeros((24, LANES), jnp.int32)
    keys = []
    for f in range(FACES):
        far_face = neighbour_face[f : f + 1, :]
        far_element = jnp.bitwise_and(neighbour[f : f + 1, :], LANES - 1)
        keys.append((far_face * LANES + far_element).astype(F32))
        index[8 + f : 9 + f, :] = far_element
        index[16 + f : 17 + f, :] = jnp.where(local[f], far_face, -1)
    places = group_places(groups, keys, flip)
    for f in range(FACES):
        index[f : f + 1, :] = places[f].astype(jnp.int32)


def make_deriv(deriv, frame, deriv_w):
    deriv_w[...] = frame[...]
    for d in range(3):
        deriv_w[d * BASIS_PAD : d * BASIS_PAD + BASIS, :BASIS] = -deriv[d]
    deriv_w[...] = wide_basis(deriv_w[...])


def make_faces(proj, orient, frame, proj_w, turn_w, flip):
    proj_w[...] = frame[0:64, :]
    for g in range(FACES):
        proj_w[g * FACE_PAD : g * FACE_PAD + FACE_BASIS, :BASIS] = proj[:, g, :]
    right = side_by_side([proj_w[rows_of(g), :] for g in range(FACES)])
    flip[...] = frame[...]
    for o in range(3):
        flip[o * FACE_PAD : o * FACE_PAD + FACE_BASIS, :FACE_BASIS] = orient[o]
    turned = jnp.dot(
        flip[0:48, :FACE_PAD], right, precision=lax.Precision.HIGHEST, preferred_element_type=F32
    )
    for o in range(3):
        for g in range(FACES):
            turn_w[rows_of(o * FACES + g), :] = wide_basis(turned[rows_of(o), lanes_of(g)])
    proj_w[...] = wide_basis(proj_w[...])


def make_update(update, update_w, flip):
    update_w[...] = jnp.zeros((LANES, LANES), F32)
    for d in range(3):
        flip[...] = jnp.zeros((LANES, LANES), F32)
        flip[:BASIS, :BASIS] = update[d]
        update_w[d * BASIS_PAD : (d + 1) * BASIS_PAD, :] = flip[...].T[:BASIS_PAD, :]
    update_w[...] = wide_basis(update_w[...])


def make_lift(lift_mat, deriv_w, lift_w, flip):
    total = None
    for f in range(FACES):
        flip[...] = jnp.zeros((LANES, LANES), F32)
        flip[:FACE_BASIS, :BASIS] = lift_mat[:, f, :]
        value = turn_lanes(flip[...].T[0:48, :], 16 * f)
        total = value if total is None else total + value
    lift_w[0:48, :] = wide_faces(total)
    lift_w[48:176, :] = wide_faces(matmul(deriv_w[...], tall_basis(total[0:BASIS_PAD, :])))


def pack(pieces, element, lane):
    return choose([take_lanes(piece, element) for piece in pieces], lane, PACK)


def pack_quantities(pieces, element):
    lane = lax.broadcasted_iota(jnp.int32, pieces[0].shape, 1)
    nothing = jnp.zeros(pieces[0].shape, F32)
    result = []
    for k in range(PACKS):
        group = [take_lanes(pieces[q], element) if q < QUANTITIES else nothing for q in range(4 * k, 4 * k + 4)]
        result.append(choose(group, lane, PACK))
    return result


def unpack_quantity(packed, q, rank):
    return take_lanes(packed(q // 4), rank + PACK * (q % 4))


def make_packs(r):
    row = lax.broadcasted_iota(jnp.int32, (LANES, LANES), 0).astype(F32)
    lane = lax.broadcasted_iota(jnp.int32, (LANES, LANES), 1)
    cluster = r.cluster[...].astype(F32)
    columns = transposed([cluster] * FACES, r.flip)
    before = jnp.where((columns[:, 0:1] == cluster) & (row < lane.astype(F32)), 1.0, 0.0)
    rank = jnp.sum(before, axis=0, keepdims=True)
    columns = transposed([cluster * 64.0 + rank] * FACES, r.flip)
    r.packs[...] = jnp.zeros((8, LANES), jnp.int32)
    for block in range(2):
        wanted = jnp.bitwise_and(lane, PACK - 1).astype(F32) + 64.0 * block
        hit = jnp.where(columns[:, 0:1] == wanted, row, 0.0)
        r.packs[block : block + 1, :] = jnp.sum(hit, axis=0, keepdims=True).astype(jnp.int32)
    rank = rank.astype(jnp.int32)
    r.packs[2:3, :] = jnp.bitwise_and(rank, PACK - 1)
    lane = lax.broadcasted_iota(jnp.int32, (1, LANES), 1)
    kinds = r.cluster[...]
    for f in range(FACES):
        r.source_cluster[f : f + 1, :] = take_lanes(kinds, r.index[8 + f : 9 + f, :])
    got = [r.index[f : f + 1, :].astype(F32) for f in range(FACES)]
    for tile, (element, _) in enumerate(columns_of(got, r.flip)):
        kind = take_lanes(kinds, element)
        for side in range(2):
            width = 32 if tile else 64
            parts = [turn_lanes(kind, width * j - 64 * side) for j in range(LANES // width)]
            first = 2 * tile + side
            r.column_cluster[first : first + 1, :] = choose(parts, lane, width)
    for tile in range(2):
        element = r.send_index[2 * tile : 2 * tile + 1, :]
        face = r.send_index[2 * tile + 1 : 2 * tile + 2, :]
        kind = take_lanes(kinds, element)
        order = take_lanes(jnp.bitwise_and(rank, PACK - 1), element)
        rows = [order] + [jnp.where(kind == block, face, -1) for block in range(2)]
        for side in range(2):
            width = 32 if tile else 64
            for i in range(3):
                parts = [turn_lanes(rows[i], width * j - 64 * side) for j in range(LANES // width)]
                value = choose(parts, lane, width)
                if i == 0:
                    value = value + PACK * (lane // width)
                first = 3 * (2 * tile + side) + i
                r.send_packs[first : first + 1, :] = value


def pack_flux(flux, element, packed):
    lane = lax.broadcasted_iota(jnp.int32, (FACES, LANES), 1)
    face = lax.broadcasted_iota(jnp.int32, (FACES, LANES), 0)
    for q in range(QUANTITIES):
        for p in range(QUANTITIES):
            value = jnp.where(face == lane // PACK, take_lanes(flux[q, p], element), 0.0)
            packed[q, p : p + 1, :] = jnp.sum(value, axis=0, keepdims=True)


def pack_block(r, block, where, star, flux):
    element = r.packs[block : block + 1, :]
    lane = lax.broadcasted_iota(jnp.int32, (1, LANES), 1)
    where[...] = jnp.zeros((8, LANES), jnp.int32)
    where[0:1, :] = pack([r.index[f : f + 1, :] for f in range(FACES)], element, lane)
    where[1:5, :] = take_lanes(r.orientation[...], element)
    where[5:6, :] = pack([r.index[8 + f : 9 + f, :] for f in range(FACES)], element, lane)
    where[6:7, :] = pack([r.index[16 + f : 17 + f, :] for f in range(FACES)], element, lane)
    for q in range(QUANTITIES):
        for k, value in enumerate(pack_quantities([r.star[q, p] for p in range(QUANTITIES)], element)):
            star[q, k] = value
    pack_flux(r.flux_neigh, element, flux)


def spread_faces(total, lift_in):
    lane = lax.broadcasted_iota(jnp.int32, (FACE_PAD, LANES), 1)
    nothing = jnp.zeros((FACE_PAD, LANES), F32)
    for k in range(PACKS):
        for f in range(FACES):
            parts = []
            for j in range(GROUPS):
                q = GROUPS * k + j
                parts.append(turn_lanes(total[q], PACK * (j - f)) if q < QUANTITIES else nothing)
            lift_in[f * FACE_PAD : (f + 1) * FACE_PAD, lanes_of(k)] = choose(parts, lane, PACK)
    return side_by_side([tall_faces(lift_in[:, lanes_of(k)]) for k in range(PACKS)])


def packed_fields(r, base, ahead, gathered, flux, where, lift_in, work):
    place = where[0:1, :]
    near = jnp.bitwise_and(place, 63)
    far = jnp.bitwise_and(place, PACK - 1)
    total = [None] * QUANTITIES
    for p in range(QUANTITIES):
        got = [take_lanes(ref[rows_of(p // 2), :], near + 64 * (p % 2)) for ref in (r.sum_a, r.sum_x)]
        got += [take_lanes(ref[rows_of(p // 4), :], far + PACK * (p % 4)) for ref in (r.sum_y, r.sum_z)]
        remote = jnp.where(place < 64, got[0], jnp.where(place < 128, got[1], jnp.where(place < 192, got[2], got[3])))
        piece = gathered[rows_of(p), :] + jnp.where(place >= 0, remote, 0.0)
        for q in range(QUANTITIES):
            term = flux[q, p : p + 1, :] * piece
            total[q] = term if total[q] is None else total[q] + term
    right = spread_faces(total, lift_in)
    lifted = matmul(r.lift_w[:, :192], right)
    work[...] = ahead[...] - lifted[48:176, :]
    return [base[k] - lifted[:BASIS_PAD, lanes_of(k)] for k in range(PACKS)]


def packed_derivatives(terms, deriv_w, work):
    for k in range(PACKS):
        work[:, lanes_of(k)] = matmul(deriv_w[...], tall_basis(terms[k]))


def gather_copies(values):
    lane = lax.broadcasted_iota(jnp.int32, (BASIS_PAD, LANES), 1)
    if len(values) == 1:
        total = values[0] + pltpu.roll(values[0], 64, 1)
        return jnp.where(lane < PACK, total + pltpu.roll(total, 96, 1), 0.0)
    low = lane < 64
    halves = []
    for i in range(2):
        a, b = values[i], values[i + 2]
        halves.append(jnp.where(low, a, b) + pltpu.roll(jnp.where(low, b, a), 64, 1))
    even = jnp.bitwise_and(lane, PACK) == 0
    swapped = take_lanes(jnp.where(even, halves[1], halves[0]), jnp.bitwise_xor(lane[0:1, :], PACK))
    return jnp.where(even, halves[0], halves[1]) + swapped


def packed_star(star, work, follow=None):
    result = []
    for k in range(PACKS):
        quantities = range(GROUPS * k, min(GROUPS * (k + 1), QUANTITIES))
        result.append(gather_copies(star_tile(star, work, quantities, PACKS)))
        if follow is not None:
            follow(k, result[k])
    return result


def packed_faces(integrals, turn_w, where, put):
    right = side_by_side([tall_basis(value) for value in integrals])
    result = matmul(turn_w[...], right)
    for g in range(FACES):
        turn = where[1 + g : 2 + g, :]
        for k in range(PACKS):
            parts = [result[rows_of(o * FACES + g), lanes_of(k)] for o in range(3)]
            put(g, k, jnp.where(turn == 0, parts[0], jnp.where(turn == 1, parts[1], parts[2])))


def add_terms(total, terms, weight):
    values = [term * weight for term in terms]
    return values if total is None else [a + b for a, b in zip(total, values)]


def add_received(r):
    for name in "axyz":
        getattr(r, "sum_" + name)[...] = getattr(r, "got_" + name)[...] + getattr(r, "old_" + name)[...]


def slot_kernel(slot, r):
    add_received(r)
    numbers = (0, 1) if slot == 2 else (0,)
    names = ("base", "ahead", "gathered", "flux", "where", "lift_in", "star", "fields", "step", "faces", "work", "spare")
    blocks = [types.SimpleNamespace(**{name: getattr(r, name + str(b)) for name in names}) for b in numbers]
    terms = []
    for block in blocks:
        terms.append(
            packed_fields(
                r, block.base, block.ahead, block.gathered, block.flux, block.where, block.lift_in, block.work
            )
        )
        for k in range(PACKS):
            block.fields[k] = terms[-1][k]
    first = [None] * len(blocks)
    second = None
    for k in range(ORDER):
        for b, block in enumerate(blocks):
            if k:
                work, other = (block.work, block.spare) if k % 2 else (block.spare, block.work)

                def follow(i, value, other=other):
                    other[:, lanes_of(i)] = matmul(r.deriv_w[...], tall_basis(value))

                terms[b] = packed_star(block.star, work, follow if k < ORDER - 1 else None)
            first[b] = add_terms(first[b], terms[b], 1.0 / math.factorial(k + 1))
        if slot == 2:
            second = add_terms(second, terms[1], (2.0 ** (k + 1) - 1.0) / math.factorial(k + 1))
    for b, block in enumerate(blocks):

        def put(g, k, value, faces=block.faces):
            faces[g, rows_of(k), :] = value

        packed_faces(first[b], r.turn_w, block.where, put)
        for k in range(PACKS):
            block.step[k] = first[b][k]
    if slot == 2:
        for k in range(PACKS):
            r.second1[k] = second[k]
    for partner in SEND_ORDER:
        later, sent = getattr(r, "later_" + NAMES[partner]), getattr(r, NAMES[partner])
        near = partner < 2
        lane = r.send_packs[3 * partner : 3 * partner + 1, :]
        for k in range(5 if near else PACKS):
            value = later[rows_of(k), :]
            source = k // 2 if near else k
            place = lane + 64 * (k % 2) if near else lane
            for b, block in enumerate(blocks):
                face = r.send_packs[3 * partner + 1 + b : 3 * partner + 2 + b, :]
                for g in range(FACES):
                    value = jnp.where(face == g, take_lanes(block.faces[g, rows_of(source), :], place), value)
            sent[rows_of(k), :] = value
        if not near:
            sent[48:80, :] = jnp.zeros((32, LANES), F32)


def frame_kernel(r):
    r.frame[...] = jnp.zeros((LANES, LANES), F32)


def prepare_kernel(devices, r):
    r.orientation_out[...] = r.orientation[...]
    r.cluster_out[...] = r.cluster[...].reshape(1, LANES)
    r.far_out[...] = r.neighbour_face[...]
    make_send_index(devices, r.neighbour, r.face_kind, r.send_index, r.flip)
    make_deriv(r.deriv, r.frame, r.deriv_w)
    make_faces(r.proj, r.orient, r.frame, r.proj_w, r.turn_w, r.flip)


def first_kernel(r):
    for q in range(QUANTITIES):
        r.taylor[0, q] = jnp.zeros((BASIS_PAD, LANES), F32)
        r.taylor[0, q, :BASIS, :] = r.dofs[q]
    predict(r.taylor, r.star, r.deriv_w, (r.spare, r.work))
    span = lax.shift_left(jnp.ones_like(r.cluster[...]), r.cluster[...]).astype(F32)
    for q in range(QUANTITIES):
        r.step[q] = step_integral(r.taylor, q, span)

    def put(g, q, value):
        r.faces[g, rows_of(q), :] = value

    rotated_faces(r.turn_w, r.orientation, [integral(r.taylor, q, 0) for q in range(QUANTITIES)], put)
    pack_sends(r.faces, r.send_index, [getattr(r, name) for name in NAMES])


def last_kernel(r):
    add_received(r)
    unpack_receives([r.sum_a, r.sum_x, r.sum_y, r.sum_z], r.near, r.far)

    def keep(f, value):
        r.collected[f] = value

    add_remote(r.index, r.near, r.far, r.gathered, keep)
    apply_flux(r.flux_neigh, lambda f, p: r.collected[f, rows_of(p), :], r.lift_in)
    lifted = lift(r.lift_w, r.lift_in)
    for q in range(QUANTITIES):
        r.out[q] = (r.base[q] - lifted[:BASIS_PAD, lanes_of(q)])[:BASIS, :]


def beside_kernel(slot, devices, r):
    if slot == 0:
        make_update(r.update, r.update_w, r.flip)
        make_lift(r.lift_mat, r.deriv_w, r.lift_w, r.flip)
        make_recv_index(devices, r.neighbour, r.neighbour_face, r.face_kind, r.index, r.flip)
        make_packs(r)
        pack_block(r, 0, r.where0, r.star0, r.flux0)
        mirror = jnp.where(r.face_kind[...] == 1, 1.0, 0.0)
        for p in range(QUANTITIES):
            sign = -mirror if p < 6 else mirror
            for q in range(QUANTITIES):
                r.flux_own[q, p] = r.flux_local[q, p] + sign * r.flux_neigh[q, p]
    cluster = r.cluster[...]
    started = cluster <= (0 if slot % 2 else 1)
    rank = r.packs[2:3, :]

    def unpacked(name, q, rows=None):
        def packed(ref):
            return (lambda k: ref[k]) if rows is None else (lambda k: ref[rows, rows_of(k), :])

        value = unpack_quantity(packed(getattr(r, name + "0")), q, rank)
        if slot == 2:
            value = jnp.where(cluster == 1, unpack_quantity(packed(getattr(r, name + "1")), q, rank), value)
        return value

    sums = r.sums
    for g in range(FACES):
        reset = r.source_cluster[g : g + 1, :] <= (0 if slot % 2 else 1)
        for q in range(QUANTITIES):
            if slot == 0:
                sums[g, rows_of(q), :] = r.faces[g, rows_of(q), :]
                continue
            value = jnp.where(started, unpacked("faces", q, g), r.later[g, rows_of(q), :])
            sums[g, rows_of(q), :] = value + jnp.where(reset, 0.0, r.old_sums[g, rows_of(q), :])
    for i, name in enumerate("axyz"):
        if slot:
            reset = r.column_cluster[i : i + 1, :] <= (0 if slot % 2 else 1)
            getattr(r, "old_" + name)[...] = jnp.where(reset, 0.0, getattr(r, "sum_" + name)[...])
        else:
            getattr(r, "old_" + name)[...] = jnp.zeros((SEND_ROWS, LANES), F32)
    if slot == 3:
        for f in range(FACES):
            lane = r.index[8 + f : 9 + f, :]
            face = r.index[16 + f : 17 + f, :]
            total = None
            for g in range(FACES):
                value = jnp.where(face == g, take_lanes(sums[g], lane), 0.0)
                total = value if total is None else total + value
            r.gathered[f] = total
    if slot == 0:
        fields = [r.taylor[0, q] for q in range(QUANTITIES)]
        steps = [r.step[q] for q in range(QUANTITIES)]
    else:
        fields = [unpacked("fields", q) for q in range(QUANTITIES)]
        steps = [unpacked("step", q) for q in range(QUANTITIES)]
        if slot == 2:
            for q in range(QUANTITIES):
                steps[q] = steps[q] + jnp.where(cluster == 1, unpack_quantity(lambda k: r.second1[k], q, rank), 0.0)
    right = side_by_side([tall_basis(value) for value in steps])
    own = matmul(r.proj_w[...], right)
    apply_flux(r.flux_own, lambda f, p: own[rows_of(f), lanes_of(p)], r.lift_in)
    lifted = lift(r.lift_w, r.lift_in)
    r.work[...] = matmul(r.update_w[...], right)

    def put(q, value):
        value = fields[q] + value - lifted[:BASIS_PAD, lanes_of(q)]
        r.base[q] = value if slot == 0 else jnp.where(started, value, r.old_base[q])

    apply_star(r.star, r.work, put)
    if slot == 1:
        pack_block(r, 1, r.where1, r.star1, r.flux1)
    if slot == 0:
        for j, later in ((1, r.later1), (2, r.later2), (3, r.later3)):

            def store(g, q, value, later=later):
                later[g, rows_of(q), :] = value

            rotated_faces(r.turn_w, r.orientation, [integral(r.taylor, q, j) for q in range(QUANTITIES)], store)
    if slot == 2:

        def merge(g, q, value):
            r.next_later[g, rows_of(q), :] = jnp.where(cluster == 1, value, r.after[g, rows_of(q), :])

        rotated_faces(
            r.turn_w,
            r.orientation,
            [unpack_quantity(lambda k: r.second1[k], q, rank) for q in range(QUANTITIES)],
            merge,
        )
    if slot == 3:
        return
    later = r.later1 if slot == 0 else r.after if slot == 1 else r.next_later
    pack_sends(later, r.send_index, [getattr(r, "later_" + name) for name in NAMES])
    targets = [(r.base0, r.ahead0, r.gathered0, r.where0)]
    if slot == 1:
        targets.append((r.base1, r.ahead1, r.gathered1, r.where1))
    for block, (base, ahead, gathered, where) in enumerate(targets):
        packed = pack_quantities([r.base[q] for q in range(QUANTITIES)], r.packs[block : block + 1, :])
        for k in range(PACKS):
            base[k] = packed[k]
        packed_derivatives(packed, r.deriv_w, ahead)
        lane, face = where[5:6, :], where[6:7, :]
        total = None
        for g in range(FACES):
            value = jnp.where(face == g, take_lanes(sums[g], lane), 0.0)
            total = value if total is None else total + value
        gathered[...] = total


def shape_of(array):
    return jax.ShapeDtypeStruct(array.shape, array.dtype)


def shape(*dims):
    return jax.ShapeDtypeStruct(dims, F32)


def ints(rows):
    return jax.ShapeDtypeStruct((rows, LANES), jnp.int32)


RECEIVED = ("got_a", "got_x", "got_y", "got_z")
TAYLOR = shape(ORDER, QUANTITIES, BASIS_PAD, LANES)
STATE = shape(QUANTITIES, BASIS_PAD, LANES)
PACKED = shape(PACKS, BASIS_PAD, LANES)
AHEAD = shape(LANES, PACKS * LANES)
PACKED_STAR = shape(QUANTITIES, PACKS, 3, LANES)
PACKED_FLUX = shape(QUANTITIES, QUANTITIES, LANES)
PACKED_LIFT = shape(FACES * FACE_PAD, PACKS * LANES)
TURNED = shape(FACES, FACE_ROWS, LANES)
TILE = shape(FACE_ROWS, LANES)
SQUARE = shape(LANES, LANES)
WORK = shape(LANES, QUANTITIES * LANES)
LIFT_IN = shape(FACES * FACE_PAD, QUANTITIES * LANES)
SENDS = {NAMES[i]: shape(SEND_ROWS, LANES) for i in SEND_ORDER}
OLD = {"old_" + name: shape(SEND_ROWS, LANES) for name in "axyz"}
SUMS = {"sum_" + name: shape(SEND_ROWS, LANES) for name in "axyz"}
LATER_SENDS = {"later_" + name: value for name, value in SENDS.items()}
EARLY_FLOPS = 5_000_000_000


def call(kernel, name, ins, outs, scratch, flops):
    names = [*ins, *outs, *scratch]
    size = sum(math.prod(a.shape) * 4 for a in [*ins.values(), *outs.values()])

    def run(*refs):
        kernel(types.SimpleNamespace(**dict(zip(names, refs))))

    result = pl.pallas_call(
        run,
        out_shape=list(outs.values()),
        in_specs=[VMEM] * len(ins),
        out_specs=[VMEM] * len(outs),
        scratch_shapes=[pltpu.VMEM(a.shape, a.dtype) for a in scratch.values()],
        compiler_params=pltpu.CompilerParams(vmem_limit_bytes=32 * 1024 * 1024),
        cost_estimate=pl.CostEstimate(flops=flops, bytes_accessed=size, transcendentals=0),
        name=name,
    )(*ins.values())
    return dict(zip(outs, result))


def some(values, *names):
    return {name: values[name] for name in names}


def body(
    dofs, star, flux_local, flux_neigh, neighbour, neighbour_face, orientation, face_kind, cluster,
    deriv_stiff, update_stiff, face_proj, face_lift, orient_map,
):
    devices = lax.axis_size("dom")
    star, flux_local, flux_neigh = [jnp.transpose(a, (1, 2, 0, 3)) for a in (star, flux_local, flux_neigh)]
    face_proj, face_lift = jnp.transpose(face_proj, (1, 0, 2)), jnp.transpose(face_lift, (2, 0, 1))
    v = dict(
        star=star, flux_local=flux_local, flux_neigh=flux_neigh, neighbour=neighbour,
        face_kind=face_kind, update=update_stiff, lift_mat=face_lift,
    )
    frame = call(frame_kernel, "frame", {}, dict(frame=SQUARE), {}, EARLY_FLOPS)["frame"]
    ready = call(
        functools.partial(prepare_kernel, devices),
        "prepare",
        dict(frame=frame, neighbour=neighbour, neighbour_face=neighbour_face, face_kind=face_kind,
             orientation=orientation, cluster=cluster, deriv=deriv_stiff, proj=face_proj, orient=orient_map),
        dict(deriv_w=SQUARE, far_out=ints(FACES), proj_w=shape(64, LANES), turn_w=shape(192, LANES), send_index=ints(8),
             orientation_out=ints(FACES), cluster_out=ints(1)),
        dict(flip=SQUARE),
        EARLY_FLOPS,
    )
    v.update(ready, orientation=ready["orientation_out"], cluster=ready["cluster_out"], neighbour_face=ready["far_out"])
    sends = call(
        first_kernel,
        "start",
        dict(dofs=dofs, **some(v, "star", "orientation", "cluster", "deriv_w", "turn_w", "send_index")),
        dict(taylor=TAYLOR, step=STATE, faces=TURNED, **SENDS),
        dict(work=WORK, spare=WORK),
        100_000_000,
    )
    receives = exchange(sends)
    kept = call(
        functools.partial(beside_kernel, 0, devices),
        "beside0",
        {**some(sends, "taylor", "step", "faces"),
         **some(v, "star", "orientation", "cluster", "flux_local", "flux_neigh", "face_kind", "neighbour",
                "neighbour_face", "update", "lift_mat", "deriv_w", "proj_w", "turn_w", "send_index")},
        dict(base=STATE, sums=TURNED, source_cluster=ints(FACES), column_cluster=ints(4), **OLD,
             flux_own=shape_of(flux_local), later1=TURNED, later2=TURNED,
             later3=TURNED, update_w=SQUARE, lift_w=shape(176, 256), index=ints(24), packs=ints(8),
             send_packs=ints(12), where0=ints(8), star0=PACKED_STAR, flux0=PACKED_FLUX,
             base0=PACKED, ahead0=AHEAD, gathered0=TILE, **LATER_SENDS),
        dict(work=WORK, lift_in=LIFT_IN, flip=SQUARE),
        50_000_000,
    )
    v.update(kept)
    later = {1: v["later1"], 2: v["later2"], 3: v["later3"]}
    for slot in range(1, SLOTS):
        numbers = (0, 1) if slot == 2 else (0,)
        per_block = [name + str(b) for b in numbers for name in ("base", "ahead", "gathered", "flux", "star", "where")]
        outs, scratch = {}, {}
        for b in numbers:
            outs.update({"fields%d" % b: PACKED, "step%d" % b: PACKED, "faces%d" % b: shape(FACES, 48, LANES)})
            scratch.update(
                {"work%d" % b: AHEAD, "spare%d" % b: AHEAD, "lift_in%d" % b: PACKED_LIFT}
            )
        if slot == 2:
            outs["second1"] = PACKED
        sends = call(
            functools.partial(slot_kernel, slot),
            "slot%d" % slot,
            {**receives, **some(v, *OLD, *per_block, *LATER_SENDS, "deriv_w", "turn_w", "lift_w", "send_packs")},
            {**outs, **SUMS, **SENDS},
            scratch,
            100_000_000,
        )
        receives = exchange(sends)
        ins = some(sends, *outs, *SUMS)
        ins.update(old_base=v["base"], old_sums=v["sums"], later=later[slot])
        ins.update(
            some(v, "star", "cluster", "flux_own", "proj_w", "update_w", "lift_w", "packs", "source_cluster",
                 "column_cluster")
        )
        results = dict(base=STATE, **OLD)
        scratch = dict(work=WORK, lift_in=LIFT_IN)
        if slot < 3:
            ins.update(after=later[slot + 1], **some(v, "send_index", "deriv_w", "where0"))
            results.update(sums=TURNED, base0=PACKED, ahead0=AHEAD, gathered0=TILE, **LATER_SENDS)
        else:
            ins.update(some(v, "index"))
            results.update(gathered=TURNED)
            scratch.update(sums=TURNED)
        if slot == 1:
            ins.update(some(v, "flux_neigh", "orientation", "index"))
            results.update(base1=PACKED, ahead1=AHEAD, gathered1=TILE, where1=ints(8), star1=PACKED_STAR,
                           flux1=PACKED_FLUX)
        if slot == 2:
            ins.update(some(v, "orientation", "turn_w"))
            results.update(next_later=TURNED)
        v.update(
            call(
                functools.partial(beside_kernel, slot, devices), "beside%d" % slot, ins, results,
                scratch, 50_000_000,
            )
        )
        if slot == 2:
            later[3] = v["next_later"]
    return call(
        last_kernel,
        "finish",
        {**receives, **some(v, *OLD, "base", "gathered", "flux_neigh", "lift_w", "index")},
        dict(out=shape(*dofs.shape)),
        dict(**SUMS, near=TILE, far=TILE, collected=TURNED, lift_in=LIFT_IN),
        10_000_000,
    )["out"]


def solution(mesh):
    in_specs = (
        P(None, None, "dom"),
        P(None, None, None, "dom"),
        P(None, None, None, "dom"),
        P(None, None, None, "dom"),
        P(None, "dom"),
        P(None, "dom"),
        P(None, "dom"),
        P(None, "dom"),
        P("dom"),
        P(),
        P(),
        P(),
        P(),
        P(),
    )
    out_specs = P(None, None, "dom")
    return jax.shard_map(body, mesh=mesh, in_specs=in_specs, out_specs=out_specs, check_vma=False)
```

time: 587 us -> 50.4 us (0.09); the launches traced: 578 us -> 50.2 us
  matrix products: 223 us -> 0 us
  local copies, waits for them, and re-layouts: 224 us -> 1.17 us
  other arithmetic: 90.9 us -> 0 us
  Pallas kernels: 0 us -> 20.6 us
  starting transfers between devices: 37.8 us -> 25.1 us
    dot_general x72 -> x0, matrix products: 223 us -> none  [the longest x16 88.3 us: taylor_terms(): current = -jnp.einsum('dqpe,dpxe->qxe', star, contracted, precision=HIGHEST)]
    gather x41 -> x0, local copies, waits for them, and re-layouts: 59.2 us -> none  [the longest x16 19 us: body(): jnp.take(face_values, send_index[partner], axis=1)]
    unnamed x263 -> x28, local copies, waits for them, and re-layouts: 48.4 us -> 1.17 us
    transpose x18 -> x0, local copies, waits for them, and re-layouts: 46.9 us -> none  [the longest x8 32 us: taylor_terms(): jnp.einsum('dxy,pye->dpxe', deriv_stiff, current, precision=HIGHEST)]
    select_n x35 -> x0, other arithmetic: 33.7 us -> none  [the longest x16 14.2 us: body(): jnp.take(face_values, send_index[partner], axis=1)]
    another operation x21 -> x0, local copies, waits for them, and re-layouts: 26.8 us -> none  [the longest x14 23.7 us: taylor_terms(): return jnp.stack(terms)]
    pallas_call x0 -> x11, Pallas kernels: none -> 20.6 us  [call(): pl.pallas_call(run, out_shape=list(outs.values()), in_specs=[VMEM] * len(...]
    sort x5 -> x0, other arithmetic: 17 us -> none  [the longest x1 3.77 us: body(): recv_order = jnp.argsort(recv_flat * (4 * everyone) + far_key, stable=True)]
  transfers between devices with their start and end apart: 16 -> 16, of which waited for: 2 -> 5; matrix products, arithmetic and copies ran while one was open for 20% -> 0% of each run, Pallas kernels for 0% -> 16%
where the time goes in v1:
time: 50.4 us; the launch traced here: 50.2 us
  starting transfers between devices  25.1 us (50%)
  Pallas kernels  20.6 us (41%)
  waiting for transfers between devices  3.1 us (6%)
  local copies, waits for them, and re-layouts  1.17 us (2%)
    ppermute x16, starting transfers between devices, exchange(): lax.ppermute(sends[NAMES[partner]], 'dom', pairs)  25.1 us
    pallas_call x11, Pallas kernels, call(): pl.pallas_call(run, out_shape=list(outs.values()), in_specs=[VMEM] * len(...  20.6 us
    ppermute x16, waiting for transfers between devices, exchange(): lax.ppermute(sends[NAMES[partner]], 'dom', pairs)  3.1 us
    unnamed x28, local copies, waits for them, and re-layouts  1.17 us
  transfers between devices with their start and end apart: 16, of which 5 were waited for; matrix products, arithmetic and copies ran while one was open for 0% of the time, Pallas kernels for 16%

profile of v1, /device:TPU:0, one launch (start us, length us, event | category | flops | bytes accessed | tf_op | source)
XLA Modules:
  0.0 50.2 jit_solution(7889875026406903413)
XLA Ops:
  0.1 0.6 %copy-done.7 = s32[4,128]{1,0:T(4,128)S(1)} copy-done((s32[4,128]{1,0:T(4,128)S(1)}, s32[4,128]{1,0:T(4,128)}, u32[]{:S(2)}) %copy-start.7) | copy-done | bytes 2072
  0.7 0.1 copy-done.10
  0.8 0.1 copy-done.8
  0.9 0.7 %prepare.1 = (f32[128,128]{1,0:T(8,128)S(1)}, s32[4,128]{1,0:T(4,128)S(1)}, f32[64,128]{1,0:T(8,128)S(1)}, f32[192,128]{1,0:T(8,128)S(1)}, s32[8,128]{1,0:T(8,12...) custom-call(f32[128,128]{1,0:T(8,128)S(1)} %frame.1.refs_0_, s32[4,128]{1,0:T(4,128)S(1)} %copy-done.6, ...), custom_call_target="tpu_custom_call" | custom-call | flops 5000000000 | bytes 305352 | tf_op jit(solution)/shard_map/prepare/pallas_call | solution.py:794
  1.6 0.2 copy-done
  1.8 0.1 copy-done.2
  1.9 2.6 %start.1 = (f32[5,9,40,128]{3,2,1,0:T(8,128)S(1)}, f32[9,40,128]{2,1,0:T(8,128)S(1)}, f32[4,144,128]{2,1,0:T(8,128)S(1)}, f32[80,128]{1,0:T(8,128)S(1)}, f32[80,...) custom-call(f32[9,35,128]{2,1,0:T(8,128)S(1)} %copy-done.2, f32[9,9,3,128]{3,2,1,0:T(4,128)S(1)} %bitcast.5, ...), custom_call_target="tpu_custom_call" | custom-call | flops 100000000 | bytes 2020864 | tf_op jit(solution)/shard_map/start/pallas_call | solution.py:794
  4.6 3.0 %collective-permute-start = (f32[80,128]{1,0:T(8,128)S(1)}, f32[80,128]{1,0:T(8,128)S(1)}, u32[]{:S(2)}, u32[]{:S(2)}) collective-permute-start(f32[80,128]{1,0:T(8,128)S(1)} %get-tuple-element.127), channel_id=1, source_target_pairs={{0,2},{1,31},{2,4},{3,1},{4,6},{5,3},{6,8},{7,5},{8,10},{9,7},{10,... | collective-permute-start | bytes 122888 | tf_op jit(solution)/shard_map/ppermute | solution.py:43
  7.5 3.7 %collective-permute-start.1 = (f32[80,128]{1,0:T(8,128)S(1)}, f32[80,128]{1,0:T(8,128)S(1)}, u32[]{:S(2)}, u32[]{:S(2)}) collective-permute-start(f32[80,128]{1,0:T(8,128)S(1)} %get-tuple-element.128), channel_id=1, source_target_pairs={{0,31},{1,2},{2,1},{3,4},{4,3},{5,6},{6,5},{7,8},{8,7},{9,10},{10,... | collective-permute-start | bytes 122888 | tf_op jit(solution)/shard_map/ppermute | solution.py:43
  11.2 1.4 %collective-permute-start.2 = (f32[80,128]{1,0:T(8,128)S(1)}, f32[80,128]{1,0:T(8,128)S(1)}, u32[]{:S(2)}, u32[]{:S(2)}) collective-permute-start(f32[80,128]{1,0:T(8,128)S(1)} %get-tuple-element.129), channel_id=1, source_target_pairs={{0,30},{1,3},{2,0},{3,5},{4,2},{5,7},{6,4},{7,9},{8,6},{9,11},{10,... | collective-permute-start | bytes 122888 | tf_op jit(solution)/shard_map/ppermute | solution.py:43
  12.7 2.5 %beside0.1 = (f32[9,40,128]{2,1,0:T(8,128)S(1)}, f32[4,144,128]{2,1,0:T(8,128)S(1)}, s32[4,128]{1,0:T(4,128)S(1)}, s32[4,128]{1,0:T(4,128)S(1)}, f32[80,128]{1,0...) custom-call(f32[5,9,40,128]{3,2,1,0:T(8,128)S(1)} %get-tuple-element, ...), custom_call_target="tpu_custom_call" | custom-call | flops 50000000 | bytes 4638268 | tf_op jit(solution)/shard_map/beside0/pallas_call | solution.py:794
  15.3 2.4 %slot1.1 = (f32[3,40,128]{2,1,0:T(8,128)S(1)}, f32[3,40,128]{2,1,0:T(8,128)S(1)}, f32[4,48,128]{2,1,0:T(8,128)S(1)}, f32[80,128]{1,0:T(8,128)S(1)}, f32[80,128]{...) custom-call(f32[80,128]{1,0:T(8,128)S(1)} %collective-permute-done.r, ...), custom_call_target="tpu_custom_call" | custom-call | flops 100000000 | bytes 1809408 | tf_op jit(solution)/shard_map/slot1/pallas_call | solution.py:794
  17.7 2.4 %collective-permute-start.4 = (f32[80,128]{1,0:T(8,128)S(1)}, f32[80,128]{1,0:T(8,128)S(1)}, u32[]{:S(2)}, u32[]{:S(2)}) collective-permute-start(f32[80,128]{1,0:T(8,128)S(1)} %get-tuple-element.152), channel_id=1, source_target_pairs={{0,2},{1,31},{2,4},{3,1},{4,6},{5,3},{6,8},{7,5},{8,10},{9,7},{10,... | collective-permute-start | bytes 122888 | tf_op jit(solution)/shard_map/ppermute | solution.py:43
  20.1 1.1 %collective-permute-start.5 = (f32[80,128]{1,0:T(8,128)S(1)}, f32[80,128]{1,0:T(8,128)S(1)}, u32[]{:S(2)}, u32[]{:S(2)}) collective-permute-start(f32[80,128]{1,0:T(8,128)S(1)} %get-tuple-element.153), channel_id=1, source_target_pairs={{0,31},{1,2},{2,1},{3,4},{4,3},{5,6},{6,5},{7,8},{8,7},{9,10},{10,... | collective-permute-start | bytes 122888 | tf_op jit(solution)/shard_map/ppermute | solution.py:43
  21.2 2.2 %collective-permute-start.6 = (f32[80,128]{1,0:T(8,128)S(1)}, f32[80,128]{1,0:T(8,128)S(1)}, u32[]{:S(2)}, u32[]{:S(2)}) collective-permute-start(f32[80,128]{1,0:T(8,128)S(1)} %get-tuple-element.154), channel_id=1, source_target_pairs={{0,30},{1,3},{2,0},{3,5},{4,2},{5,7},{6,4},{7,9},{8,6},{9,11},{10,... | collective-permute-start | bytes 122888 | tf_op jit(solution)/shard_map/ppermute | solution.py:43
  23.4 1.7 %beside1.1 = (f32[9,40,128]{2,1,0:T(8,128)S(1)}, f32[80,128]{1,0:T(8,128)S(1)}, f32[80,128]{1,0:T(8,128)S(1)}, f32[80,128]{1,0:T(8,128)S(1)}, f32[80,128]{1,0:T(...) custom-call(f32[3,40,128]{2,1,0:T(8,128)S(1)} %get-tuple-element.156, ...), custom_call_target="tpu_custom_call" | custom-call | flops 50000000 | bytes 3843072 | tf_op jit(solution)/shard_map/beside1/pallas_call | solution.py:794
  25.2 0.2 collective-permute-done.4.refs_0_
  25.4 1.8 %collective-permute-done.5.refs_1_ = f32[80,128]{1,0:T(8,128)S(1)} collective-permute-done((f32[80,128]{1,0:T(8,128)S(1)}, f32[80,128]{1,0:T(8,128)S(1)}, u32[]{:S(2)}, u32[]{:S(2)}) %collective-permute-start.5) | collective-permute-done | bytes 40992 | tf_op jit(solution)/shard_map/ppermute | solution.py:43
  27.1 3.2 %slot2.1 = (f32[3,40,128]{2,1,0:T(8,128)S(1)}, f32[3,40,128]{2,1,0:T(8,128)S(1)}, f32[4,48,128]{2,1,0:T(8,128)S(1)}, f32[3,40,128]{2,1,0:T(8,128)S(1)}, f32[3,40...) custom-call(f32[80,128]{1,0:T(8,128)S(1)} %collective-permute-done.4, ...), custom_call_target="tpu_custom_call" | custom-call | flops 100000000 | bytes 2510848 | tf_op jit(solution)/shard_map/slot2/pallas_call | solution.py:794
  30.4 0.7 %collective-permute-start.8 = (f32[80,128]{1,0:T(8,128)S(1)}, f32[80,128]{1,0:T(8,128)S(1)}, u32[]{:S(2)}, u32[]{:S(2)}) collective-permute-start(f32[80,128]{1,0:T(8,128)S(1)} %get-tuple-element.190), channel_id=1, source_target_pairs={{0,2},{1,31},{2,4},{3,1},{4,6},{5,3},{6,8},{7,5},{8,10},{9,7},{10,... | collective-permute-start | bytes 122888 | tf_op jit(solution)/shard_map/ppermute | solution.py:43
  31.1 0.9 %collective-permute-start.9 = (f32[80,128]{1,0:T(8,128)S(1)}, f32[80,128]{1,0:T(8,128)S(1)}, u32[]{:S(2)}, u32[]{:S(2)}) collective-permute-start(f32[80,128]{1,0:T(8,128)S(1)} %get-tuple-element.191), channel_id=1, source_target_pairs={{0,31},{1,2},{2,1},{3,4},{4,3},{5,6},{6,5},{7,8},{8,7},{9,10},{10,... | collective-permute-start | bytes 122888 | tf_op jit(solution)/shard_map/ppermute | solution.py:43
  32.0 4.0 %collective-permute-start.10 = (f32[80,128]{1,0:T(8,128)S(1)}, f32[80,128]{1,0:T(8,128)S(1)}, u32[]{:S(2)}, u32[]{:S(2)}) collective-permute-start(f32[80,128]{1,0:T(8,128)S(1)} %get-tuple-element.192), channel_id=1, source_target_pairs={{0,30},{1,3},{2,0},{3,5},{4,2},{5,7},{6,4},{7,9},{8,6},{9,11},{10,... | collective-permute-start | bytes 122888 | tf_op jit(solution)/shard_map/ppermute | solution.py:43
  36.0 2.2 %beside2.1 = (f32[9,40,128]{2,1,0:T(8,128)S(1)}, f32[80,128]{1,0:T(8,128)S(1)}, f32[80,128]{1,0:T(8,128)S(1)}, f32[80,128]{1,0:T(8,128)S(1)}, f32[80,128]{1,0:T(...) custom-call(f32[3,40,128]{2,1,0:T(8,128)S(1)} %get-tuple-element.194, ...), custom_call_target="tpu_custom_call" | custom-call | flops 50000000 | bytes 3921920 | tf_op jit(solution)/shard_map/beside2/pallas_call | solution.py:794
  38.2 0.1 collective-permute-done.8.refs_0_
  38.4 0.1 collective-permute-done.9.refs_1_
  38.5 2.4 %slot3.1 = (f32[3,40,128]{2,1,0:T(8,128)S(1)}, f32[3,40,128]{2,1,0:T(8,128)S(1)}, f32[4,48,128]{2,1,0:T(8,128)S(1)}, f32[80,128]{1,0:T(8,128)S(1)}, f32[80,128]{...) custom-call(f32[80,128]{1,0:T(8,128)S(1)} %collective-permute-done.8, ...), custom_call_target="tpu_custom_call" | custom-call | flops 100000000 | bytes 1809408 | tf_op jit(solution)/shard_map/slot3/pallas_call | solution.py:794
  40.9 0.1 collective-permute-start.12
  40.9 2.8 %collective-permute-start.13 = (f32[80,128]{1,0:T(8,128)S(1)}, f32[80,128]{1,0:T(8,128)S(1)}, u32[]{:S(2)}, u32[]{:S(2)}) collective-permute-start(f32[80,128]{1,0:T(8,128)S(1)} %get-tuple-element.220), channel_id=1, source_target_pairs={{0,31},{1,2},{2,1},{3,4},{4,3},{5,6},{6,5},{7,8},{8,7},{9,10},{10,... | collective-permute-start | bytes 122888 | tf_op jit(solution)/shard_map/ppermute | solution.py:43
  43.7 2.8 %collective-permute-start.14 = (f32[80,128]{1,0:T(8,128)S(1)}, f32[80,128]{1,0:T(8,128)S(1)}, u32[]{:S(2)}, u32[]{:S(2)}) collective-permute-start(f32[80,128]{1,0:T(8,128)S(1)} %get-tuple-element.221), channel_id=1, source_target_pairs={{0,30},{1,3},{2,0},{3,5},{4,2},{5,7},{6,4},{7,9},{8,6},{9,11},{10,... | collective-permute-start | bytes 122888 | tf_op jit(solution)/shard_map/ppermute | solution.py:43
  46.6 1.4 %beside3.1 = (f32[9,40,128]{2,1,0:T(8,128)S(1)}, f32[80,128]{1,0:T(8,128)S(1)}, f32[80,128]{1,0:T(8,128)S(1)}, f32[80,128]{1,0:T(8,128)S(1)}, f32[80,128]{1,0:T(8,128)S(1)}, /*index=5*/f32[4,144,128]{2,1,0:T(8,128)S(1)}) custom-call(f32[3,40,128]{2,1,0:T(8,128)S(1)} %get-tuple-element.223.refs_0_, f32[3,40,128]{2,1,0:T(8,128)S(1)} %get-tuple-element.224.refs_1_, ...), custom_call_target="tpu_custom_call" | custom-call | flops 50000000 | bytes 2392064 | tf_op jit(solution)/shard_map/beside3/pallas_call | solution.py:794
  48.0 0.9 %collective-permute-done.12.refs_0_ = f32[80,128]{1,0:T(8,128)S(1)} collective-permute-done((f32[80,128]{1,0:T(8,128)S(1)}, f32[80,128]{1,0:T(8,128)S(1)}, u32[]{:S(2)}, u32[]{:S(2)}) %collective-permute-start.12) | collective-permute-done | bytes 40992 | tf_op jit(solution)/shard_map/ppermute | solution.py:43
  48.8 1.4 %finish.1 = f32[9,35,128]{2,1,0:T(8,128)} custom-call(f32[80,128]{1,0:T(8,128)S(1)} %collective-permute-done.12.refs_0_, f32[80,128]{1,0:T(8,128)S(1)} %collective-permute-done.13.refs_1_, f32[80,128]{1,0:T(8,128)S(1)} %collective-permute-done.14.refs_2_, f32[80,128]{1,0:T(8,128)S(1)} %collective-permute-done.15.refs_3_, ...), custom_call_target="tpu_custom_call" | custom-call | flops 10000000 | bytes 1326592 | tf_op jit(solution)/shard_map/finish/pallas_call | solution.py:794
  (39 shorter events, 0.1 us)
Async XLA Ops:
  0.0 0.7 %copy-start.7 = (s32[4,128]{1,0:T(4,128)S(1)}, s32[4,128]{1,0:T(4,128)}, u32[]{:S(2)}) copy-start(s32[4,128]{1,0:T(4,128)} %refs_8_.3) | copy-start | bytes 6148
  0.0 0.7 %copy-start.6 = (s32[4,128]{1,0:T(4,128)S(1)}, s32[4,128]{1,0:T(4,128)}, u32[]{:S(2)}) copy-start(s32[4,128]{1,0:T(4,128)} %refs_9_.1) | copy-start | bytes 6148
  0.0 0.8 %copy-start.10 = (f32[3,15,15]{2,1,0:T(8,128)S(1)}, f32[3,15,15]{2,1,0:T(8,128)}, u32[]{:S(2)}) copy-start(f32[3,15,15]{2,1,0:T(8,128)} %refs_8_.2) | copy-start | bytes 8104
  0.0 0.8 %copy-start.9 = (f32[4,15,35]{2,0,1:T(4,128)S(1)}, f32[4,15,35]{2,0,1:T(4,128)}, u32[]{:S(2)}) copy-start(f32[4,15,35]{2,0,1:T(4,128)} %param.25) | copy-start | bytes 25204
  0.0 0.9 %copy-start.8 = (f32[3,35,35]{2,1,0:T(8,128)S(1)}, f32[3,35,35]{2,1,0:T(8,128)}, u32[]{:S(2)}) copy-start(f32[3,35,35]{2,1,0:T(8,128)} %refs_6_.1) | copy-start | bytes 44104
  0.0 0.9 %copy-start.12 = (s32[4,128]{1,0:T(4,128)S(1)}, s32[4,128]{1,0:T(4,128)}, u32[]{:S(2)}) copy-start(s32[4,128]{1,0:T(4,128)} %refs_4_.1) | copy-start | bytes 6148
  0.0 0.9 %copy-start.11 = (s32[4,128]{1,0:T(4,128)S(1)}, s32[4,128]{1,0:T(4,128)}, u32[]{:S(2)}) copy-start(s32[4,128]{1,0:T(4,128)} %refs_2_.1) | copy-start | bytes 6148
  0.0 0.9 %copy-start.13 = (s32[128]{0:T(128)S(1)}, s32[128]{0:T(128)}, u32[]{:S(2)}) copy-start(s32[128]{0:T(128)} %refs_5_.1) | copy-start | bytes 1540
  0.9 0.9 %copy-start = (f32[3,9,9,128]{3,0,2,1:T(4,128)S(1)}, f32[3,9,9,128]{3,0,2,1:T(4,128)}, u32[]{:S(2)}) copy-start(f32[3,9,9,128]{3,0,2,1:T(4,128)} %param.15) | copy-start | bytes 373252
  0.9 1.0 %copy-start.2 = (f32[9,35,128]{2,1,0:T(8,128)S(1)}, f32[9,35,128]{2,1,0:T(8,128)}, u32[]{:S(2)}) copy-start(f32[9,35,128]{2,1,0:T(8,128)} %refs_0_.1) | copy-start | bytes 483844
  1.9 10.8 %copy-start.1 = (f32[4,9,9,128]{3,0,2,1:T(4,128)S(1)}, f32[4,9,9,128]{3,0,2,1:T(4,128)}, u32[]{:S(2)}) copy-start(f32[4,9,9,128]{3,0,2,1:T(4,128)} %param.17) | copy-start | bytes 497668
  1.9 10.8 %copy-start.3 = (f32[4,9,9,128]{3,0,2,1:T(4,128)S(1)}, f32[4,9,9,128]{3,0,2,1:T(4,128)}, u32[]{:S(2)}) copy-start(f32[4,9,9,128]{3,0,2,1:T(4,128)} %param.16) | copy-start | bytes 497668
  1.9 10.8 %copy-start.4 = (f32[3,35,35]{2,1,0:T(8,128)S(1)}, f32[3,35,35]{2,1,0:T(8,128)}, u32[]{:S(2)}) copy-start(f32[3,35,35]{2,1,0:T(8,128)} %refs_11_.1) | copy-start | bytes 44104
  1.9 10.8 %copy-start.5 = (f32[4,35,15]{1,0,2:T(4,128)S(1)}, f32[4,35,15]{1,0,2:T(4,128)}, u32[]{:S(2)}) copy-start(f32[4,35,15]{1,0,2:T(4,128)} %param.26) | copy-start | bytes 25204
  4.6 10.7 %collective-permute-start = (f32[80,128]{1,0:T(8,128)S(1)}, f32[80,128]{1,0:T(8,128)S(1)}, u32[]{:S(2)}, u32[]{:S(2)}) collective-permute-start(f32[80,128]{1,0:T(8,128)S(1)} %get-tuple-element.127), channel_id=1, source_target_pairs={{0,2},{1,31},{2,4},{3,1},{4,6},{5,3},{6,8},{7,5},{8,10},{9,7},{10,... | collective-permute-start | bytes 122888 | tf_op jit(solution)/shard_map/ppermute | solution.py:43
  7.5 7.7 %collective-permute-start.1 = (f32[80,128]{1,0:T(8,128)S(1)}, f32[80,128]{1,0:T(8,128)S(1)}, u32[]{:S(2)}, u32[]{:S(2)}) collective-permute-start(f32[80,128]{1,0:T(8,128)S(1)} %get-tuple-element.128), channel_id=1, source_target_pairs={{0,31},{1,2},{2,1},{3,4},{4,3},{5,6},{6,5},{7,8},{8,7},{9,10},{10,... | collective-permute-start | bytes 122888 | tf_op jit(solution)/shard_map/ppermute | solution.py:43
  11.2 4.0 %collective-permute-start.2 = (f32[80,128]{1,0:T(8,128)S(1)}, f32[80,128]{1,0:T(8,128)S(1)}, u32[]{:S(2)}, u32[]{:S(2)}) collective-permute-start(f32[80,128]{1,0:T(8,128)S(1)} %get-tuple-element.129), channel_id=1, source_target_pairs={{0,30},{1,3},{2,0},{3,5},{4,2},{5,7},{6,4},{7,9},{8,6},{9,11},{10,... | collective-permute-start | bytes 122888 | tf_op jit(solution)/shard_map/ppermute | solution.py:43
  12.7 2.6 %collective-permute-start.3 = (f32[80,128]{1,0:T(8,128)S(1)}, f32[80,128]{1,0:T(8,128)S(1)}, u32[]{:S(2)}, u32[]{:S(2)}) collective-permute-start(f32[80,128]{1,0:T(8,128)S(1)} %get-tuple-element.130), channel_id=1, source_target_pairs={{0,1},{1,0},{2,3},{3,2},{4,5},{5,4},{6,7},{7,6},{8,9},{9,8},{10,11... | collective-permute-start | bytes 122888 | tf_op jit(solution)/shard_map/ppermute | solution.py:43
  17.7 7.7 %collective-permute-start.4 = (f32[80,128]{1,0:T(8,128)S(1)}, f32[80,128]{1,0:T(8,128)S(1)}, u32[]{:S(2)}, u32[]{:S(2)}) collective-permute-start(f32[80,128]{1,0:T(8,128)S(1)} %get-tuple-element.152), channel_id=1, source_target_pairs={{0,2},{1,31},{2,4},{3,1},{4,6},{5,3},{6,8},{7,5},{8,10},{9,7},{10,... | collective-permute-start | bytes 122888 | tf_op jit(solution)/shard_map/ppermute | solution.py:43
  20.1 7.0 %collective-permute-start.5 = (f32[80,128]{1,0:T(8,128)S(1)}, f32[80,128]{1,0:T(8,128)S(1)}, u32[]{:S(2)}, u32[]{:S(2)}) collective-permute-start(f32[80,128]{1,0:T(8,128)S(1)} %get-tuple-element.153), channel_id=1, source_target_pairs={{0,31},{1,2},{2,1},{3,4},{4,3},{5,6},{6,5},{7,8},{8,7},{9,10},{10,... | collective-permute-start | bytes 122888 | tf_op jit(solution)/shard_map/ppermute | solution.py:43
  21.2 5.9 %collective-permute-start.6 = (f32[80,128]{1,0:T(8,128)S(1)}, f32[80,128]{1,0:T(8,128)S(1)}, u32[]{:S(2)}, u32[]{:S(2)}) collective-permute-start(f32[80,128]{1,0:T(8,128)S(1)} %get-tuple-element.154), channel_id=1, source_target_pairs={{0,30},{1,3},{2,0},{3,5},{4,2},{5,7},{6,4},{7,9},{8,6},{9,11},{10,... | collective-permute-start | bytes 122888 | tf_op jit(solution)/shard_map/ppermute | solution.py:43
  23.4 3.7 %collective-permute-start.7 = (f32[80,128]{1,0:T(8,128)S(1)}, f32[80,128]{1,0:T(8,128)S(1)}, u32[]{:S(2)}, u32[]{:S(2)}) collective-permute-start(f32[80,128]{1,0:T(8,128)S(1)} %get-tuple-element.155), channel_id=1, source_target_pairs={{0,1},{1,0},{2,3},{3,2},{4,5},{5,4},{6,7},{7,6},{8,9},{9,8},{10,11... | collective-permute-start | bytes 122888 | tf_op jit(solution)/shard_map/ppermute | solution.py:43
  30.4 8.0 %collective-permute-start.8 = (f32[80,128]{1,0:T(8,128)S(1)}, f32[80,128]{1,0:T(8,128)S(1)}, u32[]{:S(2)}, u32[]{:S(2)}) collective-permute-start(f32[80,128]{1,0:T(8,128)S(1)} %get-tuple-element.190), channel_id=1, source_target_pairs={{0,2},{1,31},{2,4},{3,1},{4,6},{5,3},{6,8},{7,5},{8,10},{9,7},{10,... | collective-permute-start | bytes 122888 | tf_op jit(solution)/shard_map/ppermute | solution.py:43
  31.1 7.4 %collective-permute-start.9 = (f32[80,128]{1,0:T(8,128)S(1)}, f32[80,128]{1,0:T(8,128)S(1)}, u32[]{:S(2)}, u32[]{:S(2)}) collective-permute-start(f32[80,128]{1,0:T(8,128)S(1)} %get-tuple-element.191), channel_id=1, source_target_pairs={{0,31},{1,2},{2,1},{3,4},{4,3},{5,6},{6,5},{7,8},{8,7},{9,10},{10,... | collective-permute-start | bytes 122888 | tf_op jit(solution)/shard_map/ppermute | solution.py:43
  32.0 6.4 %collective-permute-start.10 = (f32[80,128]{1,0:T(8,128)S(1)}, f32[80,128]{1,0:T(8,128)S(1)}, u32[]{:S(2)}, u32[]{:S(2)}) collective-permute-start(f32[80,128]{1,0:T(8,128)S(1)} %get-tuple-element.192), channel_id=1, source_target_pairs={{0,30},{1,3},{2,0},{3,5},{4,2},{5,7},{6,4},{7,9},{8,6},{9,11},{10,... | collective-permute-start | bytes 122888 | tf_op jit(solution)/shard_map/ppermute | solution.py:43
  36.0 2.4 %collective-permute-start.11 = (f32[80,128]{1,0:T(8,128)S(1)}, f32[80,128]{1,0:T(8,128)S(1)}, u32[]{:S(2)}, u32[]{:S(2)}) collective-permute-start(f32[80,128]{1,0:T(8,128)S(1)} %get-tuple-element.193), channel_id=1, source_target_pairs={{0,1},{1,0},{2,3},{3,2},{4,5},{5,4},{6,7},{7,6},{8,9},{9,8},{10,11... | collective-permute-start | bytes 122888 | tf_op jit(solution)/shard_map/ppermute | solution.py:43
  40.9 7.9 %collective-permute-start.12 = (f32[80,128]{1,0:T(8,128)S(1)}, f32[80,128]{1,0:T(8,128)S(1)}, u32[]{:S(2)}, u32[]{:S(2)}) collective-permute-start(f32[80,128]{1,0:T(8,128)S(1)} %get-tuple-element.219), channel_id=1, source_target_pairs={{0,2},{1,31},{2,4},{3,1},{4,6},{5,3},{6,8},{7,5},{8,10},{9,7},{10,... | collective-permute-start | bytes 122888 | tf_op jit(solution)/shard_map/ppermute | solution.py:43
  40.9 7.9 %collective-permute-start.13 = (f32[80,128]{1,0:T(8,128)S(1)}, f32[80,128]{1,0:T(8,128)S(1)}, u32[]{:S(2)}, u32[]{:S(2)}) collective-permute-start(f32[80,128]{1,0:T(8,128)S(1)} %get-tuple-element.220), channel_id=1, source_target_pairs={{0,31},{1,2},{2,1},{3,4},{4,3},{5,6},{6,5},{7,8},{8,7},{9,10},{10,... | collective-permute-start | bytes 122888 | tf_op jit(solution)/shard_map/ppermute | solution.py:43
  43.7 5.1 %collective-permute-start.14 = (f32[80,128]{1,0:T(8,128)S(1)}, f32[80,128]{1,0:T(8,128)S(1)}, u32[]{:S(2)}, u32[]{:S(2)}) collective-permute-start(f32[80,128]{1,0:T(8,128)S(1)} %get-tuple-element.221), channel_id=1, source_target_pairs={{0,30},{1,3},{2,0},{3,5},{4,2},{5,7},{6,4},{7,9},{8,6},{9,11},{10,... | collective-permute-start | bytes 122888 | tf_op jit(solution)/shard_map/ppermute | solution.py:43
  46.6 2.3 %collective-permute-start.15 = (f32[80,128]{1,0:T(8,128)S(1)}, f32[80,128]{1,0:T(8,128)S(1)}, u32[]{:S(2)}, u32[]{:S(2)}) collective-permute-start(f32[80,128]{1,0:T(8,128)S(1)} %get-tuple-element.222), channel_id=1, source_target_pairs={{0,1},{1,0},{2,3},{3,2},{4,5},{5,4},{6,7},{7,6},{8,9},{9,8},{10,11... | collective-permute-start | bytes 122888 | tf_op jit(solution)/shard_map/ppermute | solution.py:43

commit v2 on v1

--- a/solution.py
+++ b/solution.py
@@ -475,14 +475,16 @@
     return side_by_side([tall_faces(lift_in[:, lanes_of(k)]) for k in range(PACKS)])
 
 
-def packed_fields(r, base, ahead, gathered, flux, where, lift_in, work):
+def packed_fields(r, block, base, ahead, gathered, flux, where, lift_in, work):
+    near_refs = (r.got_a, r.got_x) if block == 0 else (r.sum_a, r.sum_x)
+    far_refs = (r.got_y, r.got_z) if block == 0 else (r.sum_y, r.sum_z)
     place = where[0:1, :]
     near = jnp.bitwise_and(place, 63)
     far = jnp.bitwise_and(place, PACK - 1)
     total = [None] * QUANTITIES
     for p in range(QUANTITIES):
-        got = [take_lanes(ref[rows_of(p // 2), :], near + 64 * (p % 2)) for ref in (r.sum_a, r.sum_x)]
-        got += [take_lanes(ref[rows_of(p // 4), :], far + PACK * (p % 4)) for ref in (r.sum_y, r.sum_z)]
+        got = [take_lanes(ref[rows_of(p // 2), :], near + 64 * (p % 2)) for ref in near_refs]
+        got += [take_lanes(ref[rows_of(p // 4), :], far + PACK * (p % 4)) for ref in far_refs]
         remote = jnp.where(place < 64, got[0], jnp.where(place < 128, got[1], jnp.where(place < 192, got[2], got[3])))
         piece = gathered[rows_of(p), :] + jnp.where(place >= 0, remote, 0.0)
         for q in range(QUANTITIES):
@@ -545,15 +547,16 @@
 
 
 def slot_kernel(slot, r):
-    add_received(r)
+    if slot == 2:
+        add_received(r)
     numbers = (0, 1) if slot == 2 else (0,)
     names = ("base", "ahead", "gathered", "flux", "where", "lift_in", "star", "fields", "step", "faces", "work", "spare")
     blocks = [types.SimpleNamespace(**{name: getattr(r, name + str(b)) for name in names}) for b in numbers]
     terms = []
-    for block in blocks:
+    for b, block in enumerate(blocks):
         terms.append(
             packed_fields(
-                r, block.base, block.ahead, block.gathered, block.flux, block.where, block.lift_in, block.work
+                r, b, block.base, block.ahead, block.gathered, block.flux, block.where, block.lift_in, block.work
             )
         )
         for k in range(PACKS):
@@ -604,21 +607,18 @@
     r.frame[...] = jnp.zeros((LANES, LANES), F32)
 
 
-def prepare_kernel(devices, r):
+def first_kernel(devices, r):
+    make_deriv(r.deriv, r.frame, r.deriv_w)
+    for q in range(QUANTITIES):
+        r.taylor[0, q] = jnp.zeros((BASIS_PAD, LANES), F32)
+        r.taylor[0, q, :BASIS, :] = r.dofs[q]
     r.orientation_out[...] = r.orientation[...]
     r.cluster_out[...] = r.cluster[...].reshape(1, LANES)
     r.far_out[...] = r.neighbour_face[...]
     make_send_index(devices, r.neighbour, r.face_kind, r.send_index, r.flip)
-    make_deriv(r.deriv, r.frame, r.deriv_w)
-    make_faces(r.proj, r.orient, r.frame, r.proj_w, r.turn_w, r.flip)
-
-
-def first_kernel(r):
-    for q in range(QUANTITIES):
-        r.taylor[0, q] = jnp.zeros((BASIS_PAD, LANES), F32)
-        r.taylor[0, q, :BASIS, :] = r.dofs[q]
+    make_faces(r.proj, r.orient, r.frame, r.proj_w, r.turn_w, r.flop)
     predict(r.taylor, r.star, r.deriv_w, (r.spare, r.work))
-    span = lax.shift_left(jnp.ones_like(r.cluster[...]), r.cluster[...]).astype(F32)
+    span = lax.shift_left(jnp.ones_like(r.cluster_out[...]), r.cluster_out[...]).astype(F32)
     for q in range(QUANTITIES):
         r.step[q] = step_integral(r.taylor, q, span)
 
@@ -641,6 +641,13 @@
     lifted = lift(r.lift_w, r.lift_in)
     for q in range(QUANTITIES):
         r.out[q] = (r.base[q] - lifted[:BASIS_PAD, lanes_of(q)])[:BASIS, :]
+
+
+def later_faces(r, j, later):
+    def store(g, q, value):
+        later[g, rows_of(q), :] = value
+
+    rotated_faces(r.turn_w, r.orientation, [integral(r.taylor, q, j) for q in range(QUANTITIES)], store)
 
 
 def beside_kernel(slot, devices, r):
@@ -677,12 +684,13 @@
                 continue
             value = jnp.where(started, unpacked("faces", q, g), r.later[g, rows_of(q), :])
             sums[g, rows_of(q), :] = value + jnp.where(reset, 0.0, r.old_sums[g, rows_of(q), :])
-    for i, name in enumerate("axyz"):
-        if slot:
+    if slot:
+        for i, name in enumerate("axyz"):
             reset = r.column_cluster[i : i + 1, :] <= (0 if slot % 2 else 1)
-            getattr(r, "old_" + name)[...] = jnp.where(reset, 0.0, getattr(r, "sum_" + name)[...])
-        else:
-            getattr(r, "old_" + name)[...] = jnp.zeros((SEND_ROWS, LANES), F32)
+            total = getattr(r, "sum_" + name)[...] if slot == 2 else getattr(r, "got_" + name)[...]
+            if slot == 3:
+                total = total + getattr(r, "older_" + name)[...]
+            getattr(r, "old_" + name)[...] = jnp.where(reset, 0.0, total)
     if slot == 3:
         for f in range(FACES):
             lane = r.index[8 + f : 9 + f, :]
@@ -715,12 +723,10 @@
     if slot == 1:
         pack_block(r, 1, r.where1, r.star1, r.flux1)
     if slot == 0:
-        for j, later in ((1, r.later1), (2, r.later2), (3, r.later3)):
-
-            def store(g, q, value, later=later):
-                later[g, rows_of(q), :] = value
-
-            rotated_faces(r.turn_w, r.orientation, [integral(r.taylor, q, j) for q in range(QUANTITIES)], store)
+        later_faces(r, 1, r.later1)
+    if slot == 1:
+        later_faces(r, 2, r.later2)
+        later_faces(r, 3, r.later3)
     if slot == 2:
 
         def merge(g, q, value):
@@ -734,7 +740,7 @@
         )
     if slot == 3:
         return
-    later = r.later1 if slot == 0 else r.after if slot == 1 else r.next_later
+    later = r.later1 if slot == 0 else r.later2 if slot == 1 else r.next_later
     pack_sends(later, r.send_index, [getattr(r, "later_" + name) for name in NAMES])
     targets = [(r.base0, r.ahead0, r.gathered0, r.where0)]
     if slot == 1:
@@ -820,25 +826,20 @@
         face_kind=face_kind, update=update_stiff, lift_mat=face_lift,
     )
     frame = call(frame_kernel, "frame", {}, dict(frame=SQUARE), {}, EARLY_FLOPS)["frame"]
-    ready = call(
-        functools.partial(prepare_kernel, devices),
-        "prepare",
+    sends = call(
+        functools.partial(first_kernel, devices),
+        "start",
         dict(frame=frame, neighbour=neighbour, neighbour_face=neighbour_face, face_kind=face_kind,
-             orientation=orientation, cluster=cluster, deriv=deriv_stiff, proj=face_proj, orient=orient_map),
-        dict(deriv_w=SQUARE, far_out=ints(FACES), proj_w=shape(64, LANES), turn_w=shape(192, LANES), send_index=ints(8),
-             orientation_out=ints(FACES), cluster_out=ints(1)),
-        dict(flip=SQUARE),
-        EARLY_FLOPS,
-    )
-    v.update(ready, orientation=ready["orientation_out"], cluster=ready["cluster_out"], neighbour_face=ready["far_out"])
-    sends = call(
-        first_kernel,
-        "start",
-        dict(dofs=dofs, **some(v, "star", "orientation", "cluster", "deriv_w", "turn_w", "send_index")),
-        dict(taylor=TAYLOR, step=STATE, faces=TURNED, **SENDS),
-        dict(work=WORK, spare=WORK),
+             orientation=orientation, cluster=cluster, deriv=deriv_stiff, proj=face_proj, orient=orient_map,
+             dofs=dofs, star=star),
+        dict(deriv_w=SQUARE, far_out=ints(FACES), proj_w=shape(64, LANES), turn_w=shape(192, LANES),
+             send_index=ints(8), orientation_out=ints(FACES), cluster_out=ints(1),
+             taylor=TAYLOR, step=STATE, faces=TURNED, **SENDS),
+        dict(work=WORK, spare=WORK, flip=SQUARE, flop=SQUARE),
         100_000_000,
     )
+    v.update(some(sends, "deriv_w", "proj_w", "turn_w", "send_index"), orientation=sends["orientation_out"],
+             cluster=sends["cluster_out"], neighbour_face=sends["far_out"])
     receives = exchange(sends)
     kept = call(
         functools.partial(beside_kernel, 0, devices),
@@ -846,16 +847,15 @@
         {**some(sends, "taylor", "step", "faces"),
          **some(v, "star", "orientation", "cluster", "flux_local", "flux_neigh", "face_kind", "neighbour",
                 "neighbour_face", "update", "lift_mat", "deriv_w", "proj_w", "turn_w", "send_index")},
-        dict(base=STATE, sums=TURNED, source_cluster=ints(FACES), column_cluster=ints(4), **OLD,
-             flux_own=shape_of(flux_local), later1=TURNED, later2=TURNED,
-             later3=TURNED, update_w=SQUARE, lift_w=shape(176, 256), index=ints(24), packs=ints(8),
+        dict(base=STATE, sums=TURNED, source_cluster=ints(FACES), column_cluster=ints(4),
+             flux_own=shape_of(flux_local), later1=TURNED, update_w=SQUARE, lift_w=shape(176, 256), index=ints(24), packs=ints(8),
              send_packs=ints(12), where0=ints(8), star0=PACKED_STAR, flux0=PACKED_FLUX,
              base0=PACKED, ahead0=AHEAD, gathered0=TILE, **LATER_SENDS),
         dict(work=WORK, lift_in=LIFT_IN, flip=SQUARE),
         50_000_000,
     )
     v.update(kept)
-    later = {1: v["later1"], 2: v["later2"], 3: v["later3"]}
+    v.update(taylor=sends["taylor"])
     for slot in range(1, SLOTS):
         numbers = (0, 1) if slot == 2 else (0,)
         per_block = [name + str(b) for b in numbers for name in ("base", "ahead", "gathered", "flux", "star", "where")]
@@ -870,14 +870,19 @@
         sends = call(
             functools.partial(slot_kernel, slot),
             "slot%d" % slot,
-            {**receives, **some(v, *OLD, *per_block, *LATER_SENDS, "deriv_w", "turn_w", "lift_w", "send_packs")},
-            {**outs, **SUMS, **SENDS},
+            {**receives, **(some(v, *OLD) if slot == 2 else {}),
+             **some(v, *per_block, *LATER_SENDS, "deriv_w", "turn_w", "lift_w", "send_packs")},
+            {**outs, **(SUMS if slot == 2 else {}), **SENDS},
             scratch,
             100_000_000,
         )
-        receives = exchange(sends)
-        ins = some(sends, *outs, *SUMS)
-        ins.update(old_base=v["base"], old_sums=v["sums"], later=later[slot])
+        previous, receives = receives, exchange(sends)
+        ins = some(sends, *outs, *(SUMS if slot == 2 else ()))
+        if slot != 2:
+            ins.update(previous)
+        if slot == 3:
+            ins.update({"older_" + name: v["old_" + name] for name in "axyz"})
+        ins.update(old_base=v["base"], old_sums=v["sums"], later=v["later%d" % slot])
         ins.update(
             some(v, "star", "cluster", "flux_own", "proj_w", "update_w", "lift_w", "packs", "source_cluster",
                  "column_cluster")
@@ -885,18 +890,18 @@
         results = dict(base=STATE, **OLD)
         scratch = dict(work=WORK, lift_in=LIFT_IN)
         if slot < 3:
-            ins.update(after=later[slot + 1], **some(v, "send_index", "deriv_w", "where0"))
+            ins.update(some(v, "send_index", "deriv_w", "where0"))
             results.update(sums=TURNED, base0=PACKED, ahead0=AHEAD, gathered0=TILE, **LATER_SENDS)
         else:
             ins.update(some(v, "index"))
             results.update(gathered=TURNED)
             scratch.update(sums=TURNED)
         if slot == 1:
-            ins.update(some(v, "flux_neigh", "orientation", "index"))
-            results.update(base1=PACKED, ahead1=AHEAD, gathered1=TILE, where1=ints(8), star1=PACKED_STAR,
+            ins.update(some(v, "flux_neigh", "orientation", "index", "turn_w", "taylor"))
+            results.update(later2=TURNED, later3=TURNED, base1=PACKED, ahead1=AHEAD, gathered1=TILE, where1=ints(8), star1=PACKED_STAR,
                            flux1=PACKED_FLUX)
         if slot == 2:
-            ins.update(some(v, "orientation", "turn_w"))
+            ins.update(after=v["later3"], **some(v, "orientation", "turn_w"))
             results.update(next_later=TURNED)
         v.update(
             call(
@@ -905,7 +910,7 @@
             )
         )
         if slot == 2:
-            later[3] = v["next_later"]
+            v["later3"] = v["next_later"]
     return call(
         last_kernel,
         "finish",

time: 50.4 us -> 49.9 us (0.990)
    pallas_call x11 -> x10, Pallas kernels: 20.6 us -> 20.5 us  [call(): pl.pallas_call(run, out_shape=list(outs.values()), in_specs=[VMEM] * len(...]
  transfers between devices with their start and end apart: 16 -> 16, of which waited for: 5 -> 3; matrix products, arithmetic and copies ran while one was open for 0% -> 0% of each run, Pallas kernels for 16% -> 16%
where the time goes in v2:
time: 49.9 us; the launch traced here: 49.8 us
  starting transfers between devices  25.1 us (50%)
  Pallas kernels  20.5 us (41%)
  waiting for transfers between devices  2.89 us (6%)
  local copies, waits for them, and re-layouts  1.04 us (2%)
    ppermute x16, starting transfers between devices, exchange(): lax.ppermute(sends[NAMES[partner]], 'dom', pairs)  25.1 us
    pallas_call x10, Pallas kernels, call(): pl.pallas_call(run, out_shape=list(outs.values()), in_specs=[VMEM] * len(...  20.5 us
    ppermute x16, waiting for transfers between devices, exchange(): lax.ppermute(sends[NAMES[partner]], 'dom', pairs)  2.89 us
    unnamed x28, local copies, waits for them, and re-layouts  1.04 us
  transfers between devices with their start and end apart: 16, of which 3 were waited for; matrix products, arithmetic and copies ran while one was open for 0% of the time, Pallas kernels for 16%

profile of v2, /device:TPU:0, one launch (start us, length us, event | category | flops | bytes accessed | tf_op | source)
XLA Modules:
  0.0 49.8 jit_solution(15946735855792435850)
XLA Ops:
  0.1 0.0 copy-start.13
  0.1 0.7 %copy-done.8 = f32[3,15,15]{2,1,0:T(8,128)S(1)} copy-done((f32[3,15,15]{2,1,0:T(8,128)S(1)}, f32[3,15,15]{2,1,0:T(8,128)}, u32[]{:S(2)}) %copy-start.8) | copy-done | bytes 2724
  0.7 0.0 copy-done.7
  0.8 0.1 copy-done.4
  0.9 0.1 copy-done
  1.0 0.1 copy-done.2
  1.1 3.0 %start.1 = (f32[128,128]{1,0:T(8,128)S(1)}, s32[4,128]{1,0:T(4,128)S(1)}, f32[64,128]{1,0:T(8,128)S(1)}, f32[192,128]{1,0:T(8,128)S(1)}, s32[8,128]{1,0:T(8,128)...) custom-call(f32[128,128]{1,0:T(8,128)S(1)} %frame.1.refs_0_, ...), custom_call_target="tpu_custom_call" | custom-call | flops 100000000 | bytes 2155720 | tf_op jit(solution)/shard_map/start/pallas_call | solution.py:800
  4.1 3.0 %collective-permute-start = (f32[80,128]{1,0:T(8,128)S(1)}, f32[80,128]{1,0:T(8,128)S(1)}, u32[]{:S(2)}, u32[]{:S(2)}) collective-permute-start(f32[80,128]{1,0:T(8,128)S(1)} %get-tuple-element.110), channel_id=1, source_target_pairs={{0,2},{1,31},{2,4},{3,1},{4,6},{5,3},{6,8},{7,5},{8,10},{9,7},{10,... | collective-permute-start | bytes 122888 | tf_op jit(solution)/shard_map/ppermute | solution.py:43
  7.1 3.7 %collective-permute-start.1 = (f32[80,128]{1,0:T(8,128)S(1)}, f32[80,128]{1,0:T(8,128)S(1)}, u32[]{:S(2)}, u32[]{:S(2)}) collective-permute-start(f32[80,128]{1,0:T(8,128)S(1)} %get-tuple-element.111), channel_id=1, source_target_pairs={{0,31},{1,2},{2,1},{3,4},{4,3},{5,6},{6,5},{7,8},{8,7},{9,10},{10,... | collective-permute-start | bytes 122888 | tf_op jit(solution)/shard_map/ppermute | solution.py:43
  10.8 1.4 %collective-permute-start.2 = (f32[80,128]{1,0:T(8,128)S(1)}, f32[80,128]{1,0:T(8,128)S(1)}, u32[]{:S(2)}, u32[]{:S(2)}) collective-permute-start(f32[80,128]{1,0:T(8,128)S(1)} %get-tuple-element.112), channel_id=1, source_target_pairs={{0,30},{1,3},{2,0},{3,5},{4,2},{5,7},{6,4},{7,9},{8,6},{9,11},{10,... | collective-permute-start | bytes 122888 | tf_op jit(solution)/shard_map/ppermute | solution.py:43
  12.3 2.5 %beside0.1 = (f32[9,40,128]{2,1,0:T(8,128)S(1)}, f32[4,144,128]{2,1,0:T(8,128)S(1)}, s32[4,128]{1,0:T(4,128)S(1)}, s32[4,128]{1,0:T(4,128)S(1)}, f32[9,9,4,128]{...) custom-call(f32[5,9,40,128]{3,2,1,0:T(8,128)S(1)} %get-tuple-element, ...), custom_call_target="tpu_custom_call" | custom-call | flops 50000000 | bytes 3884604 | tf_op jit(solution)/shard_map/beside0/pallas_call | solution.py:800
  14.8 0.0 collective-permute-done.2.refs_2_.refs_5_
  14.8 2.4 %slot1.1 = (f32[3,40,128]{2,1,0:T(8,128)S(1)}, f32[3,40,128]{2,1,0:T(8,128)S(1)}, f32[4,48,128]{2,1,0:T(8,128)S(1)}, f32[80,128]{1,0:T(8,128)S(1)}, f32[80,128]{...) custom-call(f32[80,128]{1,0:T(8,128)S(1)} %collective-permute-done.refs_0_.refs_3_, ...), custom_call_target="tpu_custom_call" | custom-call | flops 100000000 | bytes 1481728 | tf_op jit(solution)/shard_map/slot1/pallas_call | solution.py:800
  17.2 2.4 %collective-permute-start.4 = (f32[80,128]{1,0:T(8,128)S(1)}, f32[80,128]{1,0:T(8,128)S(1)}, u32[]{:S(2)}, u32[]{:S(2)}) collective-permute-start(f32[80,128]{1,0:T(8,128)S(1)} %get-tuple-element.136), channel_id=1, source_target_pairs={{0,2},{1,31},{2,4},{3,1},{4,6},{5,3},{6,8},{7,5},{8,10},{9,7},{10,... | collective-permute-start | bytes 122888 | tf_op jit(solution)/shard_map/ppermute | solution.py:43
  19.7 1.1 %collective-permute-start.5 = (f32[80,128]{1,0:T(8,128)S(1)}, f32[80,128]{1,0:T(8,128)S(1)}, u32[]{:S(2)}, u32[]{:S(2)}) collective-permute-start(f32[80,128]{1,0:T(8,128)S(1)} %get-tuple-element.137), channel_id=1, source_target_pairs={{0,31},{1,2},{2,1},{3,4},{4,3},{5,6},{6,5},{7,8},{8,7},{9,10},{10,... | collective-permute-start | bytes 122888 | tf_op jit(solution)/shard_map/ppermute | solution.py:43
  20.7 2.2 %collective-permute-start.6 = (f32[80,128]{1,0:T(8,128)S(1)}, f32[80,128]{1,0:T(8,128)S(1)}, u32[]{:S(2)}, u32[]{:S(2)}) collective-permute-start(f32[80,128]{1,0:T(8,128)S(1)} %get-tuple-element.138), channel_id=1, source_target_pairs={{0,30},{1,3},{2,0},{3,5},{4,2},{5,7},{6,4},{7,9},{8,6},{9,11},{10,... | collective-permute-start | bytes 122888 | tf_op jit(solution)/shard_map/ppermute | solution.py:43
  22.9 2.1 %beside1.1 = (f32[9,40,128]{2,1,0:T(8,128)S(1)}, f32[80,128]{1,0:T(8,128)S(1)}, f32[80,128]{1,0:T(8,128)S(1)}, f32[80,128]{1,0:T(8,128)S(1)}, f32[80,128]{1,0:T(...) custom-call(f32[3,40,128]{2,1,0:T(8,128)S(1)} %get-tuple-element.140, ...), custom_call_target="tpu_custom_call" | custom-call | flops 50000000 | bytes 5157888 | tf_op jit(solution)/shard_map/beside1/pallas_call | solution.py:800
  25.0 1.7 %collective-permute-done.5.refs_1_ = f32[80,128]{1,0:T(8,128)S(1)} collective-permute-done((f32[80,128]{1,0:T(8,128)S(1)}, f32[80,128]{1,0:T(8,128)S(1)}, u32[]{:S(2)}, u32[]{:S(2)}) %collective-permute-start.5) | collective-permute-done | bytes 40992 | tf_op jit(solution)/shard_map/ppermute | solution.py:43
  26.7 3.2 %slot2.1 = (f32[3,40,128]{2,1,0:T(8,128)S(1)}, f32[3,40,128]{2,1,0:T(8,128)S(1)}, f32[4,48,128]{2,1,0:T(8,128)S(1)}, f32[3,40,128]{2,1,0:T(8,128)S(1)}, f32[3,40...) custom-call(f32[80,128]{1,0:T(8,128)S(1)} %collective-permute-done.4, ...), custom_call_target="tpu_custom_call" | custom-call | flops 100000000 | bytes 2510848 | tf_op jit(solution)/shard_map/slot2/pallas_call | solution.py:800
  29.9 0.7 %collective-permute-start.8 = (f32[80,128]{1,0:T(8,128)S(1)}, f32[80,128]{1,0:T(8,128)S(1)}, u32[]{:S(2)}, u32[]{:S(2)}) collective-permute-start(f32[80,128]{1,0:T(8,128)S(1)} %get-tuple-element.169), channel_id=1, source_target_pairs={{0,2},{1,31},{2,4},{3,1},{4,6},{5,3},{6,8},{7,5},{8,10},{9,7},{10,... | collective-permute-start | bytes 122888 | tf_op jit(solution)/shard_map/ppermute | solution.py:43
  30.6 1.3 %collective-permute-start.9 = (f32[80,128]{1,0:T(8,128)S(1)}, f32[80,128]{1,0:T(8,128)S(1)}, u32[]{:S(2)}, u32[]{:S(2)}) collective-permute-start(f32[80,128]{1,0:T(8,128)S(1)} %get-tuple-element.170), channel_id=1, source_target_pairs={{0,31},{1,2},{2,1},{3,4},{4,3},{5,6},{6,5},{7,8},{8,7},{9,10},{10,... | collective-permute-start | bytes 122888 | tf_op jit(solution)/shard_map/ppermute | solution.py:43
  31.9 3.7 %collective-permute-start.10 = (f32[80,128]{1,0:T(8,128)S(1)}, f32[80,128]{1,0:T(8,128)S(1)}, u32[]{:S(2)}, u32[]{:S(2)}) collective-permute-start(f32[80,128]{1,0:T(8,128)S(1)} %get-tuple-element.171), channel_id=1, source_target_pairs={{0,30},{1,3},{2,0},{3,5},{4,2},{5,7},{6,4},{7,9},{8,6},{9,11},{10,... | collective-permute-start | bytes 122888 | tf_op jit(solution)/shard_map/ppermute | solution.py:43
  35.6 2.2 %beside2.1 = (f32[9,40,128]{2,1,0:T(8,128)S(1)}, f32[80,128]{1,0:T(8,128)S(1)}, f32[80,128]{1,0:T(8,128)S(1)}, f32[80,128]{1,0:T(8,128)S(1)}, f32[80,128]{1,0:T(...) custom-call(f32[3,40,128]{2,1,0:T(8,128)S(1)} %get-tuple-element.173, ...), custom_call_target="tpu_custom_call" | custom-call | flops 50000000 | bytes 3921920 | tf_op jit(solution)/shard_map/beside2/pallas_call | solution.py:800
  37.7 0.2 collective-permute-done.8.refs_0_.refs_3_
  38.0 0.0 collective-permute-done.9.refs_1_.refs_4_
  38.0 2.4 %slot3.1 = (f32[3,40,128]{2,1,0:T(8,128)S(1)}, f32[3,40,128]{2,1,0:T(8,128)S(1)}, f32[4,48,128]{2,1,0:T(8,128)S(1)}, f32[80,128]{1,0:T(8,128)S(1)}, f32[80,128]{...) custom-call(f32[80,128]{1,0:T(8,128)S(1)} %collective-permute-done.8.refs_0_.refs_3_, ...), custom_call_target="tpu_custom_call" | custom-call | flops 100000000 | bytes 1481728 | tf_op jit(solution)/shard_map/slot3/pallas_call | solution.py:800
  40.4 0.1 collective-permute-start.12
  40.5 2.8 %collective-permute-start.13 = (f32[80,128]{1,0:T(8,128)S(1)}, f32[80,128]{1,0:T(8,128)S(1)}, u32[]{:S(2)}, u32[]{:S(2)}) collective-permute-start(f32[80,128]{1,0:T(8,128)S(1)} %get-tuple-element.196), channel_id=1, source_target_pairs={{0,31},{1,2},{2,1},{3,4},{4,3},{5,6},{6,5},{7,8},{8,7},{9,10},{10,... | collective-permute-start | bytes 122888 | tf_op jit(solution)/shard_map/ppermute | solution.py:43
  43.3 2.8 %collective-permute-start.14 = (f32[80,128]{1,0:T(8,128)S(1)}, f32[80,128]{1,0:T(8,128)S(1)}, u32[]{:S(2)}, u32[]{:S(2)}) collective-permute-start(f32[80,128]{1,0:T(8,128)S(1)} %get-tuple-element.197), channel_id=1, source_target_pairs={{0,30},{1,3},{2,0},{3,5},{4,2},{5,7},{6,4},{7,9},{8,6},{9,11},{10,... | collective-permute-start | bytes 122888 | tf_op jit(solution)/shard_map/ppermute | solution.py:43
  46.1 1.4 %beside3.1 = (f32[9,40,128]{2,1,0:T(8,128)S(1)}, f32[80,128]{1,0:T(8,128)S(1)}, f32[80,128]{1,0:T(8,128)S(1)}, f32[80,128]{1,0:T(8,128)S(1)}, f32[80,128]{1,0:T(8,128)S(1)}, /*index=5*/f32[4,144,128]{2,1,0:T(8,128)S(1)}) custom-call(f32[3,40,128]{2,1,0:T(8,128)S(1)} %get-tuple-element.199.refs_0_, f32[3,40,128]{2,1,0:T(8,128)S(1)} %get-tuple-element.200.refs_1_, ...), custom_call_target="tpu_custom_call" | custom-call | flops 50000000 | bytes 2555904 | tf_op jit(solution)/shard_map/beside3/pallas_call | solution.py:800
  47.5 0.9 %collective-permute-done.12.refs_0_ = f32[80,128]{1,0:T(8,128)S(1)} collective-permute-done((f32[80,128]{1,0:T(8,128)S(1)}, f32[80,128]{1,0:T(8,128)S(1)}, u32[]{:S(2)}, u32[]{:S(2)}) %collective-permute-start.12) | collective-permute-done | bytes 40992 | tf_op jit(solution)/shard_map/ppermute | solution.py:43
  48.4 1.4 %finish.1 = f32[9,35,128]{2,1,0:T(8,128)} custom-call(f32[80,128]{1,0:T(8,128)S(1)} %collective-permute-done.12.refs_0_, f32[80,128]{1,0:T(8,128)S(1)} %collective-permute-done.13.refs_1_, f32[80,128]{1,0:T(8,128)S(1)} %collective-permute-done.14.refs_2_, f32[80,128]{1,0:T(8,128)S(1)} %collective-permute-done.15.refs_3_, ...), custom_call_target="tpu_custom_call" | custom-call | flops 10000000 | bytes 1326592 | tf_op jit(solution)/shard_map/finish/pallas_call | solution.py:800
  (38 shorter events, 0.1 us)
Async XLA Ops:
  0.0 0.7 %copy-start.8 = (f32[3,15,15]{2,1,0:T(8,128)S(1)}, f32[3,15,15]{2,1,0:T(8,128)}, u32[]{:S(2)}) copy-start(f32[3,15,15]{2,1,0:T(8,128)} %refs_8_.2) | copy-start | bytes 8104
  0.0 0.8 %copy-start.7 = (f32[4,15,35]{2,0,1:T(4,128)S(1)}, f32[4,15,35]{2,0,1:T(4,128)}, u32[]{:S(2)}) copy-start(f32[4,15,35]{2,0,1:T(4,128)} %param.25) | copy-start | bytes 25204
  0.0 0.9 %copy-start.4 = (f32[3,35,35]{2,1,0:T(8,128)S(1)}, f32[3,35,35]{2,1,0:T(8,128)}, u32[]{:S(2)}) copy-start(f32[3,35,35]{2,1,0:T(8,128)} %refs_6_.1) | copy-start | bytes 44104
  0.0 1.0 %copy-start = (f32[3,9,9,128]{3,0,2,1:T(4,128)S(1)}, f32[3,9,9,128]{3,0,2,1:T(4,128)}, u32[]{:S(2)}) copy-start(f32[3,9,9,128]{3,0,2,1:T(4,128)} %param.15) | copy-start | bytes 373252
  0.0 1.1 %copy-start.2 = (f32[9,35,128]{2,1,0:T(8,128)S(1)}, f32[9,35,128]{2,1,0:T(8,128)}, u32[]{:S(2)}) copy-start(f32[9,35,128]{2,1,0:T(8,128)} %refs_9_.2) | copy-start | bytes 483844
  0.0 1.1 %copy-start.10 = (s32[4,128]{1,0:T(4,128)S(1)}, s32[4,128]{1,0:T(4,128)}, u32[]{:S(2)}) copy-start(s32[4,128]{1,0:T(4,128)} %refs_8_.3) | copy-start | bytes 6148
  0.0 1.1 %copy-start.11 = (s32[4,128]{1,0:T(4,128)S(1)}, s32[4,128]{1,0:T(4,128)}, u32[]{:S(2)}) copy-start(s32[4,128]{1,0:T(4,128)} %refs_2_.1) | copy-start | bytes 6148
  0.0 1.0 %copy-start.12 = (s32[4,128]{1,0:T(4,128)S(1)}, s32[4,128]{1,0:T(4,128)}, u32[]{:S(2)}) copy-start(s32[4,128]{1,0:T(4,128)} %refs_4_.1) | copy-start | bytes 6148
  0.1 1.0 %copy-start.9 = (s32[4,128]{1,0:T(4,128)S(1)}, s32[4,128]{1,0:T(4,128)}, u32[]{:S(2)}) copy-start(s32[4,128]{1,0:T(4,128)} %refs_9_.3) | copy-start | bytes 6148
  0.1 1.0 %copy-start.13 = (s32[128]{0:T(128)S(1)}, s32[128]{0:T(128)}, u32[]{:S(2)}) copy-start(s32[128]{0:T(128)} %refs_5_.1) | copy-start | bytes 1540
  1.1 11.2 %copy-start.1 = (f32[4,9,9,128]{3,0,2,1:T(4,128)S(1)}, f32[4,9,9,128]{3,0,2,1:T(4,128)}, u32[]{:S(2)}) copy-start(f32[4,9,9,128]{3,0,2,1:T(4,128)} %param.17) | copy-start | bytes 497668
  1.1 11.1 %copy-start.3 = (f32[4,9,9,128]{3,0,2,1:T(4,128)S(1)}, f32[4,9,9,128]{3,0,2,1:T(4,128)}, u32[]{:S(2)}) copy-start(f32[4,9,9,128]{3,0,2,1:T(4,128)} %param.16) | copy-start | bytes 497668
  1.1 11.1 %copy-start.5 = (f32[3,35,35]{2,1,0:T(8,128)S(1)}, f32[3,35,35]{2,1,0:T(8,128)}, u32[]{:S(2)}) copy-start(f32[3,35,35]{2,1,0:T(8,128)} %refs_11_.1) | copy-start | bytes 44104
  4.1 8.2 %copy-start.6 = (f32[4,35,15]{1,0,2:T(4,128)S(1)}, f32[4,35,15]{1,0,2:T(4,128)}, u32[]{:S(2)}) copy-start(f32[4,35,15]{1,0,2:T(4,128)} %param.26) | copy-start | bytes 25204
  4.1 10.6 %collective-permute-start = (f32[80,128]{1,0:T(8,128)S(1)}, f32[80,128]{1,0:T(8,128)S(1)}, u32[]{:S(2)}, u32[]{:S(2)}) collective-permute-start(f32[80,128]{1,0:T(8,128)S(1)} %get-tuple-element.110), channel_id=1, source_target_pairs={{0,2},{1,31},{2,4},{3,1},{4,6},{5,3},{6,8},{7,5},{8,10},{9,7},{10,... | collective-permute-start | bytes 122888 | tf_op jit(solution)/shard_map/ppermute | solution.py:43
  7.1 7.7 %collective-permute-start.1 = (f32[80,128]{1,0:T(8,128)S(1)}, f32[80,128]{1,0:T(8,128)S(1)}, u32[]{:S(2)}, u32[]{:S(2)}) collective-permute-start(f32[80,128]{1,0:T(8,128)S(1)} %get-tuple-element.111), channel_id=1, source_target_pairs={{0,31},{1,2},{2,1},{3,4},{4,3},{5,6},{6,5},{7,8},{8,7},{9,10},{10,... | collective-permute-start | bytes 122888 | tf_op jit(solution)/shard_map/ppermute | solution.py:43
  10.8 4.0 %collective-permute-start.2 = (f32[80,128]{1,0:T(8,128)S(1)}, f32[80,128]{1,0:T(8,128)S(1)}, u32[]{:S(2)}, u32[]{:S(2)}) collective-permute-start(f32[80,128]{1,0:T(8,128)S(1)} %get-tuple-element.112), channel_id=1, source_target_pairs={{0,30},{1,3},{2,0},{3,5},{4,2},{5,7},{6,4},{7,9},{8,6},{9,11},{10,... | collective-permute-start | bytes 122888 | tf_op jit(solution)/shard_map/ppermute | solution.py:43
  12.2 2.6 %collective-permute-start.3 = (f32[80,128]{1,0:T(8,128)S(1)}, f32[80,128]{1,0:T(8,128)S(1)}, u32[]{:S(2)}, u32[]{:S(2)}) collective-permute-start(f32[80,128]{1,0:T(8,128)S(1)} %get-tuple-element.113), channel_id=1, source_target_pairs={{0,1},{1,0},{2,3},{3,2},{4,5},{5,4},{6,7},{7,6},{8,9},{9,8},{10,11... | collective-permute-start | bytes 122888 | tf_op jit(solution)/shard_map/ppermute | solution.py:43
  17.2 7.8 %collective-permute-start.4 = (f32[80,128]{1,0:T(8,128)S(1)}, f32[80,128]{1,0:T(8,128)S(1)}, u32[]{:S(2)}, u32[]{:S(2)}) collective-permute-start(f32[80,128]{1,0:T(8,128)S(1)} %get-tuple-element.136), channel_id=1, source_target_pairs={{0,2},{1,31},{2,4},{3,1},{4,6},{5,3},{6,8},{7,5},{8,10},{9,7},{10,... | collective-permute-start | bytes 122888 | tf_op jit(solution)/shard_map/ppermute | solution.py:43
  19.7 7.0 %collective-permute-start.5 = (f32[80,128]{1,0:T(8,128)S(1)}, f32[80,128]{1,0:T(8,128)S(1)}, u32[]{:S(2)}, u32[]{:S(2)}) collective-permute-start(f32[80,128]{1,0:T(8,128)S(1)} %get-tuple-element.137), channel_id=1, source_target_pairs={{0,31},{1,2},{2,1},{3,4},{4,3},{5,6},{6,5},{7,8},{8,7},{9,10},{10,... | collective-permute-start | bytes 122888 | tf_op jit(solution)/shard_map/ppermute | solution.py:43
  20.7 6.0 %collective-permute-start.6 = (f32[80,128]{1,0:T(8,128)S(1)}, f32[80,128]{1,0:T(8,128)S(1)}, u32[]{:S(2)}, u32[]{:S(2)}) collective-permute-start(f32[80,128]{1,0:T(8,128)S(1)} %get-tuple-element.138), channel_id=1, source_target_pairs={{0,30},{1,3},{2,0},{3,5},{4,2},{5,7},{6,4},{7,9},{8,6},{9,11},{10,... | collective-permute-start | bytes 122888 | tf_op jit(solution)/shard_map/ppermute | solution.py:43
  22.9 3.8 %collective-permute-start.7 = (f32[80,128]{1,0:T(8,128)S(1)}, f32[80,128]{1,0:T(8,128)S(1)}, u32[]{:S(2)}, u32[]{:S(2)}) collective-permute-start(f32[80,128]{1,0:T(8,128)S(1)} %get-tuple-element.139), channel_id=1, source_target_pairs={{0,1},{1,0},{2,3},{3,2},{4,5},{5,4},{6,7},{7,6},{8,9},{9,8},{10,11... | collective-permute-start | bytes 122888 | tf_op jit(solution)/shard_map/ppermute | solution.py:43
  29.9 8.1 %collective-permute-start.8 = (f32[80,128]{1,0:T(8,128)S(1)}, f32[80,128]{1,0:T(8,128)S(1)}, u32[]{:S(2)}, u32[]{:S(2)}) collective-permute-start(f32[80,128]{1,0:T(8,128)S(1)} %get-tuple-element.169), channel_id=1, source_target_pairs={{0,2},{1,31},{2,4},{3,1},{4,6},{5,3},{6,8},{7,5},{8,10},{9,7},{10,... | collective-permute-start | bytes 122888 | tf_op jit(solution)/shard_map/ppermute | solution.py:43
  30.6 7.4 %collective-permute-start.9 = (f32[80,128]{1,0:T(8,128)S(1)}, f32[80,128]{1,0:T(8,128)S(1)}, u32[]{:S(2)}, u32[]{:S(2)}) collective-permute-start(f32[80,128]{1,0:T(8,128)S(1)} %get-tuple-element.170), channel_id=1, source_target_pairs={{0,31},{1,2},{2,1},{3,4},{4,3},{5,6},{6,5},{7,8},{8,7},{9,10},{10,... | collective-permute-start | bytes 122888 | tf_op jit(solution)/shard_map/ppermute | solution.py:43
  31.9 6.1 %collective-permute-start.10 = (f32[80,128]{1,0:T(8,128)S(1)}, f32[80,128]{1,0:T(8,128)S(1)}, u32[]{:S(2)}, u32[]{:S(2)}) collective-permute-start(f32[80,128]{1,0:T(8,128)S(1)} %get-tuple-element.171), channel_id=1, source_target_pairs={{0,30},{1,3},{2,0},{3,5},{4,2},{5,7},{6,4},{7,9},{8,6},{9,11},{10,... | collective-permute-start | bytes 122888 | tf_op jit(solution)/shard_map/ppermute | solution.py:43
  35.6 2.4 %collective-permute-start.11 = (f32[80,128]{1,0:T(8,128)S(1)}, f32[80,128]{1,0:T(8,128)S(1)}, u32[]{:S(2)}, u32[]{:S(2)}) collective-permute-start(f32[80,128]{1,0:T(8,128)S(1)} %get-tuple-element.172), channel_id=1, source_target_pairs={{0,1},{1,0},{2,3},{3,2},{4,5},{5,4},{6,7},{7,6},{8,9},{9,8},{10,11... | collective-permute-start | bytes 122888 | tf_op jit(solution)/shard_map/ppermute | solution.py:43
  40.4 8.0 %collective-permute-start.12 = (f32[80,128]{1,0:T(8,128)S(1)}, f32[80,128]{1,0:T(8,128)S(1)}, u32[]{:S(2)}, u32[]{:S(2)}) collective-permute-start(f32[80,128]{1,0:T(8,128)S(1)} %get-tuple-element.195), channel_id=1, source_target_pairs={{0,2},{1,31},{2,4},{3,1},{4,6},{5,3},{6,8},{7,5},{8,10},{9,7},{10,... | collective-permute-start | bytes 122888 | tf_op jit(solution)/shard_map/ppermute | solution.py:43
  40.5 7.9 %collective-permute-start.13 = (f32[80,128]{1,0:T(8,128)S(1)}, f32[80,128]{1,0:T(8,128)S(1)}, u32[]{:S(2)}, u32[]{:S(2)}) collective-permute-start(f32[80,128]{1,0:T(8,128)S(1)} %get-tuple-element.196), channel_id=1, source_target_pairs={{0,31},{1,2},{2,1},{3,4},{4,3},{5,6},{6,5},{7,8},{8,7},{9,10},{10,... | collective-permute-start | bytes 122888 | tf_op jit(solution)/shard_map/ppermute | solution.py:43
  43.3 5.1 %collective-permute-start.14 = (f32[80,128]{1,0:T(8,128)S(1)}, f32[80,128]{1,0:T(8,128)S(1)}, u32[]{:S(2)}, u32[]{:S(2)}) collective-permute-start(f32[80,128]{1,0:T(8,128)S(1)} %get-tuple-element.197), channel_id=1, source_target_pairs={{0,30},{1,3},{2,0},{3,5},{4,2},{5,7},{6,4},{7,9},{8,6},{9,11},{10,... | collective-permute-start | bytes 122888 | tf_op jit(solution)/shard_map/ppermute | solution.py:43
  46.1 2.3 %collective-permute-start.15 = (f32[80,128]{1,0:T(8,128)S(1)}, f32[80,128]{1,0:T(8,128)S(1)}, u32[]{:S(2)}, u32[]{:S(2)}) collective-permute-start(f32[80,128]{1,0:T(8,128)S(1)} %get-tuple-element.198), channel_id=1, source_target_pairs={{0,1},{1,0},{2,3},{3,2},{4,5},{5,4},{6,7},{7,6},{8,9},{9,8},{10,11... | collective-permute-start | bytes 122888 | tf_op jit(solution)/shard_map/ppermute | solution.py:43

commit v3 on v2

--- a/solution.py
+++ b/solution.py
@@ -74,6 +74,16 @@
     return jnp.dot(left.astype(BF16), right, preferred_element_type=F32)
 
 
+def matmul_each(left, pieces, group=3):
+    left = left.astype(BF16)
+    results = []
+    for first in range(0, len(pieces), group):
+        part = pieces[first : first + group]
+        product = matmul(left, side_by_side(part) if len(part) > 1 else part[0])
+        results += [product[:, lanes_of(i)] for i in range(len(part))]
+    return results
+
+
 def side_by_side(pieces):
     return jnp.concatenate(pieces, axis=1)
 
@@ -84,8 +94,8 @@
 
 def star_tile(star, work, quantities, groups):
     total = [None] * len(quantities)
-    for d in range(3):
-        for p in range(groups):
+    for p in range(groups):
+        for d in range(3):
             piece = work[d * BASIS_PAD : (d + 1) * BASIS_PAD, lanes_of(p)]
             for i, q in enumerate(quantities):
                 term = star[q, p, d : d + 1, :] * piece
@@ -112,8 +122,7 @@
 
 
 def lift(lift_w, lift_in):
-    right = side_by_side([tall_faces(lift_in[:, lanes_of(q)]) for q in range(QUANTITIES)])
-    return matmul(lift_w[0:48, :192], right)
+    return matmul_each(lift_w[0:48, :192], [tall_faces(lift_in[:, lanes_of(q)]) for q in range(QUANTITIES)])
 
 
 def predict(taylor, star, deriv_w, works):
@@ -150,15 +159,14 @@
 
 
 def rotated_faces(turn_w, orientation, integrals, put):
-    right = side_by_side([tall_basis(value) for value in integrals])
-    result = matmul(turn_w[...], right)
-    for g in range(FACES):
-        turn = orientation[g : g + 1, :]
-        for q in range(QUANTITIES):
+    result = matmul_each(turn_w[...], [tall_basis(value) for value in integrals])
+    for q in range(QUANTITIES):
+        for g in range(FACES):
+            turn = orientation[g : g + 1, :]
             parts = []
             for o in range(3):
                 first = (o * FACES + g) * FACE_PAD
-                parts.append(result[first : first + FACE_PAD, lanes_of(q)])
+                parts.append(result[q][first : first + FACE_PAD, :])
             put(g, q, jnp.where(turn == 0, parts[0], jnp.where(turn == 1, parts[1], parts[2])))
 
 
@@ -293,12 +301,12 @@
     return send_groups, recv_groups, local
 
 
-def make_send_index(devices, neighbour, face_kind, index, flip):
+def make_send_index(devices, neighbour, face_kind, index, flip, spare):
     groups, _, _ = partner_groups(devices, neighbour, face_kind)
     element = lax.broadcasted_iota(jnp.int32, (1, LANES), 1)
     keys = [(element + f * LANES).astype(F32) for f in range(FACES)]
     places = group_places(groups, keys, flip)
-    for tile, (element, face) in enumerate(columns_of(places, flip)):
+    for tile, (element, face) in enumerate(columns_of(places, spare)):
         index[2 * tile : 2 * tile + 1, :] = element
         index[2 * tile + 1 : 2 * tile + 2, :] = face
 
@@ -357,18 +365,20 @@
     proj_w[...] = wide_basis(proj_w[...])
 
 
-def make_update(update, update_w, flip):
+def make_update(update, update_w, flips):
     update_w[...] = jnp.zeros((LANES, LANES), F32)
     for d in range(3):
+        flip = flips.at[d]
         flip[...] = jnp.zeros((LANES, LANES), F32)
         flip[:BASIS, :BASIS] = update[d]
         update_w[d * BASIS_PAD : (d + 1) * BASIS_PAD, :] = flip[...].T[:BASIS_PAD, :]
     update_w[...] = wide_basis(update_w[...])
 
 
-def make_lift(lift_mat, deriv_w, lift_w, flip):
+def make_lift(lift_mat, deriv_w, lift_w, flips):
     total = None
     for f in range(FACES):
+        flip = flips.at[f]
         flip[...] = jnp.zeros((LANES, LANES), F32)
         flip[:FACE_BASIS, :BASIS] = lift_mat[:, f, :]
         value = turn_lanes(flip[...].T[0:48, :], 16 * f)
@@ -399,10 +409,10 @@
     row = lax.broadcasted_iota(jnp.int32, (LANES, LANES), 0).astype(F32)
     lane = lax.broadcasted_iota(jnp.int32, (LANES, LANES), 1)
     cluster = r.cluster[...].astype(F32)
-    columns = transposed([cluster] * FACES, r.flip)
+    columns = transposed([cluster] * FACES, r.flips.at[8])
     before = jnp.where((columns[:, 0:1] == cluster) & (row < lane.astype(F32)), 1.0, 0.0)
     rank = jnp.sum(before, axis=0, keepdims=True)
-    columns = transposed([cluster * 64.0 + rank] * FACES, r.flip)
+    columns = transposed([cluster * 64.0 + rank] * FACES, r.flips.at[9])
     r.packs[...] = jnp.zeros((8, LANES), jnp.int32)
     for block in range(2):
         wanted = jnp.bitwise_and(lane, PACK - 1).astype(F32) + 64.0 * block
@@ -415,7 +425,7 @@
     for f in range(FACES):
         r.source_cluster[f : f + 1, :] = take_lanes(kinds, r.index[8 + f : 9 + f, :])
     got = [r.index[f : f + 1, :].astype(F32) for f in range(FACES)]
-    for tile, (element, _) in enumerate(columns_of(got, r.flip)):
+    for tile, (element, _) in enumerate(columns_of(got, r.flips.at[10])):
         kind = take_lanes(kinds, element)
         for side in range(2):
             width = 32 if tile else 64
@@ -472,7 +482,7 @@
                 q = GROUPS * k + j
                 parts.append(turn_lanes(total[q], PACK * (j - f)) if q < QUANTITIES else nothing)
             lift_in[f * FACE_PAD : (f + 1) * FACE_PAD, lanes_of(k)] = choose(parts, lane, PACK)
-    return side_by_side([tall_faces(lift_in[:, lanes_of(k)]) for k in range(PACKS)])
+    return [tall_faces(lift_in[:, lanes_of(k)]) for k in range(PACKS)]
 
 
 def packed_fields(r, block, base, ahead, gathered, flux, where, lift_in, work):
@@ -490,10 +500,10 @@
         for q in range(QUANTITIES):
             term = flux[q, p : p + 1, :] * piece
             total[q] = term if total[q] is None else total[q] + term
-    right = spread_faces(total, lift_in)
-    lifted = matmul(r.lift_w[:, :192], right)
-    work[...] = ahead[...] - lifted[48:176, :]
-    return [base[k] - lifted[:BASIS_PAD, lanes_of(k)] for k in range(PACKS)]
+    lifted = matmul_each(r.lift_w[:, :192], spread_faces(total, lift_in), 1)
+    for k in range(PACKS):
+        work[:, lanes_of(k)] = ahead[:, lanes_of(k)] - lifted[k][48:176, :]
+    return [base[k] - lifted[k][:BASIS_PAD, :] for k in range(PACKS)]
 
 
 def packed_derivatives(terms, deriv_w, work):
@@ -504,16 +514,14 @@
 def gather_copies(values):
     lane = lax.broadcasted_iota(jnp.int32, (BASIS_PAD, LANES), 1)
     if len(values) == 1:
-        total = values[0] + pltpu.roll(values[0], 64, 1)
-        return jnp.where(lane < PACK, total + pltpu.roll(total, 96, 1), 0.0)
-    low = lane < 64
-    halves = []
-    for i in range(2):
-        a, b = values[i], values[i + 2]
-        halves.append(jnp.where(low, a, b) + pltpu.roll(jnp.where(low, b, a), 64, 1))
-    even = jnp.bitwise_and(lane, PACK) == 0
-    swapped = take_lanes(jnp.where(even, halves[1], halves[0]), jnp.bitwise_xor(lane[0:1, :], PACK))
-    return jnp.where(even, halves[0], halves[1]) + swapped
+        value = values[0]
+        rolled = [pltpu.roll(value, PACK * shift, 1) for shift in (1, 2, 3)]
+        return jnp.where(lane < PACK, (value + rolled[0]) + (rolled[1] + rolled[2]), 0.0)
+    parts = []
+    for shift in range(GROUPS):
+        mixed = choose([values[(copy + shift) % GROUPS] for copy in range(GROUPS)], lane, PACK)
+        parts.append(turn_lanes(mixed, PACK * shift))
+    return (parts[0] + parts[1]) + (parts[2] + parts[3])
 
 
 def packed_star(star, work, follow=None):
@@ -527,12 +535,11 @@
 
 
 def packed_faces(integrals, turn_w, where, put):
-    right = side_by_side([tall_basis(value) for value in integrals])
-    result = matmul(turn_w[...], right)
-    for g in range(FACES):
-        turn = where[1 + g : 2 + g, :]
-        for k in range(PACKS):
-            parts = [result[rows_of(o * FACES + g), lanes_of(k)] for o in range(3)]
+    result = matmul_each(turn_w[...], [tall_basis(value) for value in integrals], 1)
+    for k in range(PACKS):
+        for g in range(FACES):
+            turn = where[1 + g : 2 + g, :]
+            parts = [result[k][rows_of(o * FACES + g), :] for o in range(3)]
             put(g, k, jnp.where(turn == 0, parts[0], jnp.where(turn == 1, parts[1], parts[2])))
 
 
@@ -615,7 +622,7 @@
     r.orientation_out[...] = r.orientation[...]
     r.cluster_out[...] = r.cluster[...].reshape(1, LANES)
     r.far_out[...] = r.neighbour_face[...]
-    make_send_index(devices, r.neighbour, r.face_kind, r.send_index, r.flip)
+    make_send_index(devices, r.neighbour, r.face_kind, r.send_index, r.flip, r.flap)
     make_faces(r.proj, r.orient, r.frame, r.proj_w, r.turn_w, r.flop)
     predict(r.taylor, r.star, r.deriv_w, (r.spare, r.work))
     span = lax.shift_left(jnp.ones_like(r.cluster_out[...]), r.cluster_out[...]).astype(F32)
@@ -640,7 +647,7 @@
     apply_flux(r.flux_neigh, lambda f, p: r.collected[f, rows_of(p), :], r.lift_in)
     lifted = lift(r.lift_w, r.lift_in)
     for q in range(QUANTITIES):
-        r.out[q] = (r.base[q] - lifted[:BASIS_PAD, lanes_of(q)])[:BASIS, :]
+        r.out[q] = (r.base[q] - lifted[q][:BASIS_PAD, :])[:BASIS, :]
 
 
 def later_faces(r, j, later):
@@ -652,9 +659,9 @@
 
 def beside_kernel(slot, devices, r):
     if slot == 0:
-        make_update(r.update, r.update_w, r.flip)
-        make_lift(r.lift_mat, r.deriv_w, r.lift_w, r.flip)
-        make_recv_index(devices, r.neighbour, r.neighbour_face, r.face_kind, r.index, r.flip)
+        make_update(r.update, r.update_w, r.flips.at[0:3])
+        make_lift(r.lift_mat, r.deriv_w, r.lift_w, r.flips.at[3:7])
+        make_recv_index(devices, r.neighbour, r.neighbour_face, r.face_kind, r.index, r.flips.at[7])
         make_packs(r)
         pack_block(r, 0, r.where0, r.star0, r.flux0)
         mirror = jnp.where(r.face_kind[...] == 1, 1.0, 0.0)
@@ -709,14 +716,15 @@
         if slot == 2:
             for q in range(QUANTITIES):
                 steps[q] = steps[q] + jnp.where(cluster == 1, unpack_quantity(lambda k: r.second1[k], q, rank), 0.0)
-    right = side_by_side([tall_basis(value) for value in steps])
-    own = matmul(r.proj_w[...], right)
-    apply_flux(r.flux_own, lambda f, p: own[rows_of(f), lanes_of(p)], r.lift_in)
+    right = [tall_basis(value) for value in steps]
+    own = matmul_each(r.proj_w[...], right)
+    apply_flux(r.flux_own, lambda f, p: own[p][rows_of(f), :], r.lift_in)
     lifted = lift(r.lift_w, r.lift_in)
-    r.work[...] = matmul(r.update_w[...], right)
+    for q, value in enumerate(matmul_each(r.update_w[...], right)):
+        r.work[:, lanes_of(q)] = value
 
     def put(q, value):
-        value = fields[q] + value - lifted[:BASIS_PAD, lanes_of(q)]
+        value = fields[q] + value - lifted[q][:BASIS_PAD, :]
         r.base[q] = value if slot == 0 else jnp.where(started, value, r.old_base[q])
 
     apply_star(r.star, r.work, put)
@@ -835,7 +843,7 @@
         dict(deriv_w=SQUARE, far_out=ints(FACES), proj_w=shape(64, LANES), turn_w=shape(192, LANES),
              send_index=ints(8), orientation_out=ints(FACES), cluster_out=ints(1),
              taylor=TAYLOR, step=STATE, faces=TURNED, **SENDS),
-        dict(work=WORK, spare=WORK, flip=SQUARE, flop=SQUARE),
+        dict(work=WORK, spare=WORK, flip=SQUARE, flap=SQUARE, flop=SQUARE),
         100_000_000,
     )
     v.update(some(sends, "deriv_w", "proj_w", "turn_w", "send_index"), orientation=sends["orientation_out"],
@@ -851,7 +859,7 @@
              flux_own=shape_of(flux_local), later1=TURNED, update_w=SQUARE, lift_w=shape(176, 256), index=ints(24), packs=ints(8),
              send_packs=ints(12), where0=ints(8), star0=PACKED_STAR, flux0=PACKED_FLUX,
              base0=PACKED, ahead0=AHEAD, gathered0=TILE, **LATER_SENDS),
-        dict(work=WORK, lift_in=LIFT_IN, flip=SQUARE),
+        dict(work=WORK, lift_in=LIFT_IN, flips=shape(11, LANES, LANES)),
         50_000_000,
     )
     v.update(kept)

time: 49.9 us -> 48.9 us (0.980)
  Pallas kernels: 20.5 us -> 19.8 us
    pallas_call x10, Pallas kernels: 20.5 us -> 19.8 us  [call(): pl.pallas_call(run, out_shape=list(outs.values()), in_specs=[VMEM] * len(...]
  transfers between devices with their start and end apart: 16 -> 16, of which waited for: 3 -> 4; matrix products, arithmetic and copies ran while one was open for 0% -> 0% of each run, Pallas kernels for 16% -> 17%
where the time goes in v3:
time: 48.9 us; the launch traced here: 48.7 us
  starting transfers between devices  25.2 us (52%)
  Pallas kernels  19.8 us (40%)
  waiting for transfers between devices  2.56 us (5%)
  local copies, waits for them, and re-layouts  1.04 us (2%)
    ppermute x16, starting transfers between devices, exchange(): lax.ppermute(sends[NAMES[partner]], 'dom', pairs)  25.2 us
    pallas_call x10, Pallas kernels, call(): pl.pallas_call(run, out_shape=list(outs.values()), in_specs=[VMEM] * len(...  19.8 us
    ppermute x16, waiting for transfers between devices, exchange(): lax.ppermute(sends[NAMES[partner]], 'dom', pairs)  2.56 us
    unnamed x28, local copies, waits for them, and re-layouts  1.04 us
  transfers between devices with their start and end apart: 16, of which 4 were waited for; matrix products, arithmetic and copies ran while one was open for 0% of the time, Pallas kernels for 17%

profile of v3, /device:TPU:0, one launch (start us, length us, event | category | flops | bytes accessed | tf_op | source)
XLA Modules:
  0.0 48.7 jit_solution(7765615790802935447)
XLA Ops:
  0.1 0.0 copy-start.13
  0.1 0.7 %copy-done.8 = f32[3,15,15]{2,1,0:T(8,128)S(1)} copy-done((f32[3,15,15]{2,1,0:T(8,128)S(1)}, f32[3,15,15]{2,1,0:T(8,128)}, u32[]{:S(2)}) %copy-start.8) | copy-done | bytes 2724
  0.7 0.0 copy-done.7
  0.8 0.1 copy-done.4
  0.9 0.1 copy-done
  1.0 0.1 copy-done.2
  1.1 0.0 copy-start.1
  1.1 3.0 %start.1 = (f32[128,128]{1,0:T(8,128)S(1)}, s32[4,128]{1,0:T(4,128)S(1)}, f32[64,128]{1,0:T(8,128)S(1)}, f32[192,128]{1,0:T(8,128)S(1)}, s32[8,128]{1,0:T(8,128)...) custom-call(f32[128,128]{1,0:T(8,128)S(1)} %frame.1.refs_0_, ...), custom_call_target="tpu_custom_call" | custom-call | flops 100000000 | bytes 2155720 | tf_op jit(solution)/shard_map/start/pallas_call | solution.py:808
  4.1 3.0 %collective-permute-start = (f32[80,128]{1,0:T(8,128)S(1)}, f32[80,128]{1,0:T(8,128)S(1)}, u32[]{:S(2)}, u32[]{:S(2)}) collective-permute-start(f32[80,128]{1,0:T(8,128)S(1)} %get-tuple-element.110), channel_id=1, source_target_pairs={{0,2},{1,31},{2,4},{3,1},{4,6},{5,3},{6,8},{7,5},{8,10},{9,7},{10,... | collective-permute-start | bytes 122888 | tf_op jit(solution)/shard_map/ppermute | solution.py:43
  7.1 3.7 %collective-permute-start.1 = (f32[80,128]{1,0:T(8,128)S(1)}, f32[80,128]{1,0:T(8,128)S(1)}, u32[]{:S(2)}, u32[]{:S(2)}) collective-permute-start(f32[80,128]{1,0:T(8,128)S(1)} %get-tuple-element.111), channel_id=1, source_target_pairs={{0,31},{1,2},{2,1},{3,4},{4,3},{5,6},{6,5},{7,8},{8,7},{9,10},{10,... | collective-permute-start | bytes 122888 | tf_op jit(solution)/shard_map/ppermute | solution.py:43
  10.8 1.4 %collective-permute-start.2 = (f32[80,128]{1,0:T(8,128)S(1)}, f32[80,128]{1,0:T(8,128)S(1)}, u32[]{:S(2)}, u32[]{:S(2)}) collective-permute-start(f32[80,128]{1,0:T(8,128)S(1)} %get-tuple-element.112), channel_id=1, source_target_pairs={{0,30},{1,3},{2,0},{3,5},{4,2},{5,7},{6,4},{7,9},{8,6},{9,11},{10,... | collective-permute-start | bytes 122888 | tf_op jit(solution)/shard_map/ppermute | solution.py:43
  12.3 2.6 %beside0.1 = (f32[9,40,128]{2,1,0:T(8,128)S(1)}, f32[4,144,128]{2,1,0:T(8,128)S(1)}, s32[4,128]{1,0:T(4,128)S(1)}, s32[4,128]{1,0:T(4,128)S(1)}, f32[9,9,4,128]{...) custom-call(f32[5,9,40,128]{3,2,1,0:T(8,128)S(1)} %get-tuple-element, ...), custom_call_target="tpu_custom_call" | custom-call | flops 50000000 | bytes 3884604 | tf_op jit(solution)/shard_map/beside0/pallas_call | solution.py:808
  14.9 2.0 %slot1.1 = (f32[3,40,128]{2,1,0:T(8,128)S(1)}, f32[3,40,128]{2,1,0:T(8,128)S(1)}, f32[4,48,128]{2,1,0:T(8,128)S(1)}, f32[80,128]{1,0:T(8,128)S(1)}, f32[80,128]{...) custom-call(f32[80,128]{1,0:T(8,128)S(1)} %collective-permute-done.refs_0_.refs_3_, ...), custom_call_target="tpu_custom_call" | custom-call | flops 100000000 | bytes 1481728 | tf_op jit(solution)/shard_map/slot1/pallas_call | solution.py:808
  17.0 2.3 %collective-permute-start.4 = (f32[80,128]{1,0:T(8,128)S(1)}, f32[80,128]{1,0:T(8,128)S(1)}, u32[]{:S(2)}, u32[]{:S(2)}) collective-permute-start(f32[80,128]{1,0:T(8,128)S(1)} %get-tuple-element.136), channel_id=1, source_target_pairs={{0,2},{1,31},{2,4},{3,1},{4,6},{5,3},{6,8},{7,5},{8,10},{9,7},{10,... | collective-permute-start | bytes 122888 | tf_op jit(solution)/shard_map/ppermute | solution.py:43
  19.3 1.2 %collective-permute-start.5 = (f32[80,128]{1,0:T(8,128)S(1)}, f32[80,128]{1,0:T(8,128)S(1)}, u32[]{:S(2)}, u32[]{:S(2)}) collective-permute-start(f32[80,128]{1,0:T(8,128)S(1)} %get-tuple-element.137), channel_id=1, source_target_pairs={{0,31},{1,2},{2,1},{3,4},{4,3},{5,6},{6,5},{7,8},{8,7},{9,10},{10,... | collective-permute-start | bytes 122888 | tf_op jit(solution)/shard_map/ppermute | solution.py:43
  20.5 2.2 %collective-permute-start.6 = (f32[80,128]{1,0:T(8,128)S(1)}, f32[80,128]{1,0:T(8,128)S(1)}, u32[]{:S(2)}, u32[]{:S(2)}) collective-permute-start(f32[80,128]{1,0:T(8,128)S(1)} %get-tuple-element.138), channel_id=1, source_target_pairs={{0,30},{1,3},{2,0},{3,5},{4,2},{5,7},{6,4},{7,9},{8,6},{9,11},{10,... | collective-permute-start | bytes 122888 | tf_op jit(solution)/shard_map/ppermute | solution.py:43
  22.6 2.1 %beside1.1 = (f32[9,40,128]{2,1,0:T(8,128)S(1)}, f32[80,128]{1,0:T(8,128)S(1)}, f32[80,128]{1,0:T(8,128)S(1)}, f32[80,128]{1,0:T(8,128)S(1)}, f32[80,128]{1,0:T(...) custom-call(f32[3,40,128]{2,1,0:T(8,128)S(1)} %get-tuple-element.140, ...), custom_call_target="tpu_custom_call" | custom-call | flops 50000000 | bytes 5157888 | tf_op jit(solution)/shard_map/beside1/pallas_call | solution.py:808
  24.8 1.5 %collective-permute-done.5.refs_1_ = f32[80,128]{1,0:T(8,128)S(1)} collective-permute-done((f32[80,128]{1,0:T(8,128)S(1)}, f32[80,128]{1,0:T(8,128)S(1)}, u32[]{:S(2)}, u32[]{:S(2)}) %collective-permute-start.5) | collective-permute-done | bytes 40992 | tf_op jit(solution)/shard_map/ppermute | solution.py:43
  26.3 2.9 %slot2.1 = (f32[3,40,128]{2,1,0:T(8,128)S(1)}, f32[3,40,128]{2,1,0:T(8,128)S(1)}, f32[4,48,128]{2,1,0:T(8,128)S(1)}, f32[3,40,128]{2,1,0:T(8,128)S(1)}, f32[3,40...) custom-call(f32[80,128]{1,0:T(8,128)S(1)} %collective-permute-done.4, ...), custom_call_target="tpu_custom_call" | custom-call | flops 100000000 | bytes 2510848 | tf_op jit(solution)/shard_map/slot2/pallas_call | solution.py:808
  29.3 0.8 %collective-permute-start.8 = (f32[80,128]{1,0:T(8,128)S(1)}, f32[80,128]{1,0:T(8,128)S(1)}, u32[]{:S(2)}, u32[]{:S(2)}) collective-permute-start(f32[80,128]{1,0:T(8,128)S(1)} %get-tuple-element.169), channel_id=1, source_target_pairs={{0,2},{1,31},{2,4},{3,1},{4,6},{5,3},{6,8},{7,5},{8,10},{9,7},{10,... | collective-permute-start | bytes 122888 | tf_op jit(solution)/shard_map/ppermute | solution.py:43
  30.0 1.3 %collective-permute-start.9 = (f32[80,128]{1,0:T(8,128)S(1)}, f32[80,128]{1,0:T(8,128)S(1)}, u32[]{:S(2)}, u32[]{:S(2)}) collective-permute-start(f32[80,128]{1,0:T(8,128)S(1)} %get-tuple-element.170), channel_id=1, source_target_pairs={{0,31},{1,2},{2,1},{3,4},{4,3},{5,6},{6,5},{7,8},{8,7},{9,10},{10,... | collective-permute-start | bytes 122888 | tf_op jit(solution)/shard_map/ppermute | solution.py:43
  31.3 3.6 %collective-permute-start.10 = (f32[80,128]{1,0:T(8,128)S(1)}, f32[80,128]{1,0:T(8,128)S(1)}, u32[]{:S(2)}, u32[]{:S(2)}) collective-permute-start(f32[80,128]{1,0:T(8,128)S(1)} %get-tuple-element.171), channel_id=1, source_target_pairs={{0,30},{1,3},{2,0},{3,5},{4,2},{5,7},{6,4},{7,9},{8,6},{9,11},{10,... | collective-permute-start | bytes 122888 | tf_op jit(solution)/shard_map/ppermute | solution.py:43
  35.0 2.2 %beside2.1 = (f32[9,40,128]{2,1,0:T(8,128)S(1)}, f32[80,128]{1,0:T(8,128)S(1)}, f32[80,128]{1,0:T(8,128)S(1)}, f32[80,128]{1,0:T(8,128)S(1)}, f32[80,128]{1,0:T(...) custom-call(f32[3,40,128]{2,1,0:T(8,128)S(1)} %get-tuple-element.173, ...), custom_call_target="tpu_custom_call" | custom-call | flops 50000000 | bytes 3921920 | tf_op jit(solution)/shard_map/beside2/pallas_call | solution.py:808
  37.2 0.1 collective-permute-done.8.refs_0_.refs_3_
  37.2 0.1 collective-permute-done.9.refs_1_.refs_4_
  37.4 2.0 %slot3.1 = (f32[3,40,128]{2,1,0:T(8,128)S(1)}, f32[3,40,128]{2,1,0:T(8,128)S(1)}, f32[4,48,128]{2,1,0:T(8,128)S(1)}, f32[80,128]{1,0:T(8,128)S(1)}, f32[80,128]{...) custom-call(f32[80,128]{1,0:T(8,128)S(1)} %collective-permute-done.8.refs_0_.refs_3_, ...), custom_call_target="tpu_custom_call" | custom-call | flops 100000000 | bytes 1481728 | tf_op jit(solution)/shard_map/slot3/pallas_call | solution.py:808
  39.4 0.1 collective-permute-start.12
  39.5 2.8 %collective-permute-start.13 = (f32[80,128]{1,0:T(8,128)S(1)}, f32[80,128]{1,0:T(8,128)S(1)}, u32[]{:S(2)}, u32[]{:S(2)}) collective-permute-start(f32[80,128]{1,0:T(8,128)S(1)} %get-tuple-element.196), channel_id=1, source_target_pairs={{0,31},{1,2},{2,1},{3,4},{4,3},{5,6},{6,5},{7,8},{8,7},{9,10},{10,... | collective-permute-start | bytes 122888 | tf_op jit(solution)/shard_map/ppermute | solution.py:43
  42.3 2.8 %collective-permute-start.14 = (f32[80,128]{1,0:T(8,128)S(1)}, f32[80,128]{1,0:T(8,128)S(1)}, u32[]{:S(2)}, u32[]{:S(2)}) collective-permute-start(f32[80,128]{1,0:T(8,128)S(1)} %get-tuple-element.197), channel_id=1, source_target_pairs={{0,30},{1,3},{2,0},{3,5},{4,2},{5,7},{6,4},{7,9},{8,6},{9,11},{10,... | collective-permute-start | bytes 122888 | tf_op jit(solution)/shard_map/ppermute | solution.py:43
  45.1 1.4 %beside3.1 = (f32[9,40,128]{2,1,0:T(8,128)S(1)}, f32[80,128]{1,0:T(8,128)S(1)}, f32[80,128]{1,0:T(8,128)S(1)}, f32[80,128]{1,0:T(8,128)S(1)}, f32[80,128]{1,0:T(8,128)S(1)}, /*index=5*/f32[4,144,128]{2,1,0:T(8,128)S(1)}) custom-call(f32[3,40,128]{2,1,0:T(8,128)S(1)} %get-tuple-element.199.refs_0_, f32[3,40,128]{2,1,0:T(8,128)S(1)} %get-tuple-element.200.refs_1_, ...), custom_call_target="tpu_custom_call" | custom-call | flops 50000000 | bytes 2555904 | tf_op jit(solution)/shard_map/beside3/pallas_call | solution.py:808
  46.5 0.8 %collective-permute-done.12.refs_0_ = f32[80,128]{1,0:T(8,128)S(1)} collective-permute-done((f32[80,128]{1,0:T(8,128)S(1)}, f32[80,128]{1,0:T(8,128)S(1)}, u32[]{:S(2)}, u32[]{:S(2)}) %collective-permute-start.12) | collective-permute-done | bytes 40992 | tf_op jit(solution)/shard_map/ppermute | solution.py:43
  47.3 1.4 %finish.1 = f32[9,35,128]{2,1,0:T(8,128)} custom-call(f32[80,128]{1,0:T(8,128)S(1)} %collective-permute-done.12.refs_0_, f32[80,128]{1,0:T(8,128)S(1)} %collective-permute-done.13.refs_1_, f32[80,128]{1,0:T(8,128)S(1)} %collective-permute-done.14.refs_2_, f32[80,128]{1,0:T(8,128)S(1)} %collective-permute-done.15.refs_3_, ...), custom_call_target="tpu_custom_call" | custom-call | flops 10000000 | bytes 1326592 | tf_op jit(solution)/shard_map/finish/pallas_call | solution.py:808
  (38 shorter events, 0.1 us)
Async XLA Ops:
  0.0 0.7 %copy-start.8 = (f32[3,15,15]{2,1,0:T(8,128)S(1)}, f32[3,15,15]{2,1,0:T(8,128)}, u32[]{:S(2)}) copy-start(f32[3,15,15]{2,1,0:T(8,128)} %refs_8_.2) | copy-start | bytes 8104
  0.0 0.8 %copy-start.7 = (f32[4,15,35]{2,0,1:T(4,128)S(1)}, f32[4,15,35]{2,0,1:T(4,128)}, u32[]{:S(2)}) copy-start(f32[4,15,35]{2,0,1:T(4,128)} %param.25) | copy-start | bytes 25204
  0.0 0.9 %copy-start.4 = (f32[3,35,35]{2,1,0:T(8,128)S(1)}, f32[3,35,35]{2,1,0:T(8,128)}, u32[]{:S(2)}) copy-start(f32[3,35,35]{2,1,0:T(8,128)} %refs_6_.1) | copy-start | bytes 44104
  0.0 1.0 %copy-start = (f32[3,9,9,128]{3,0,2,1:T(4,128)S(1)}, f32[3,9,9,128]{3,0,2,1:T(4,128)}, u32[]{:S(2)}) copy-start(f32[3,9,9,128]{3,0,2,1:T(4,128)} %param.15) | copy-start | bytes 373252
  0.0 1.1 %copy-start.2 = (f32[9,35,128]{2,1,0:T(8,128)S(1)}, f32[9,35,128]{2,1,0:T(8,128)}, u32[]{:S(2)}) copy-start(f32[9,35,128]{2,1,0:T(8,128)} %refs_9_.2) | copy-start | bytes 483844
  0.0 1.1 %copy-start.10 = (s32[4,128]{1,0:T(4,128)S(1)}, s32[4,128]{1,0:T(4,128)}, u32[]{:S(2)}) copy-start(s32[4,128]{1,0:T(4,128)} %refs_8_.3) | copy-start | bytes 6148
  0.0 1.1 %copy-start.11 = (s32[4,128]{1,0:T(4,128)S(1)}, s32[4,128]{1,0:T(4,128)}, u32[]{:S(2)}) copy-start(s32[4,128]{1,0:T(4,128)} %refs_2_.1) | copy-start | bytes 6148
  0.0 1.0 %copy-start.12 = (s32[4,128]{1,0:T(4,128)S(1)}, s32[4,128]{1,0:T(4,128)}, u32[]{:S(2)}) copy-start(s32[4,128]{1,0:T(4,128)} %refs_4_.1) | copy-start | bytes 6148
  0.1 1.0 %copy-start.9 = (s32[4,128]{1,0:T(4,128)S(1)}, s32[4,128]{1,0:T(4,128)}, u32[]{:S(2)}) copy-start(s32[4,128]{1,0:T(4,128)} %refs_9_.3) | copy-start | bytes 6148
  0.1 1.0 %copy-start.13 = (s32[128]{0:T(128)S(1)}, s32[128]{0:T(128)}, u32[]{:S(2)}) copy-start(s32[128]{0:T(128)} %refs_5_.1) | copy-start | bytes 1540
  1.1 11.2 %copy-start.1 = (f32[4,9,9,128]{3,0,2,1:T(4,128)S(1)}, f32[4,9,9,128]{3,0,2,1:T(4,128)}, u32[]{:S(2)}) copy-start(f32[4,9,9,128]{3,0,2,1:T(4,128)} %param.17) | copy-start | bytes 497668
  1.1 11.2 %copy-start.3 = (f32[4,9,9,128]{3,0,2,1:T(4,128)S(1)}, f32[4,9,9,128]{3,0,2,1:T(4,128)}, u32[]{:S(2)}) copy-start(f32[4,9,9,128]{3,0,2,1:T(4,128)} %param.16) | copy-start | bytes 497668
  1.1 11.1 %copy-start.5 = (f32[3,35,35]{2,1,0:T(8,128)S(1)}, f32[3,35,35]{2,1,0:T(8,128)}, u32[]{:S(2)}) copy-start(f32[3,35,35]{2,1,0:T(8,128)} %refs_11_.1) | copy-start | bytes 44104
  4.1 8.1 %copy-start.6 = (f32[4,35,15]{1,0,2:T(4,128)S(1)}, f32[4,35,15]{1,0,2:T(4,128)}, u32[]{:S(2)}) copy-start(f32[4,35,15]{1,0,2:T(4,128)} %param.26) | copy-start | bytes 25204
  4.1 10.7 %collective-permute-start = (f32[80,128]{1,0:T(8,128)S(1)}, f32[80,128]{1,0:T(8,128)S(1)}, u32[]{:S(2)}, u32[]{:S(2)}) collective-permute-start(f32[80,128]{1,0:T(8,128)S(1)} %get-tuple-element.110), channel_id=1, source_target_pairs={{0,2},{1,31},{2,4},{3,1},{4,6},{5,3},{6,8},{7,5},{8,10},{9,7},{10,... | collective-permute-start | bytes 122888 | tf_op jit(solution)/shard_map/ppermute | solution.py:43
  7.1 7.8 %collective-permute-start.1 = (f32[80,128]{1,0:T(8,128)S(1)}, f32[80,128]{1,0:T(8,128)S(1)}, u32[]{:S(2)}, u32[]{:S(2)}) collective-permute-start(f32[80,128]{1,0:T(8,128)S(1)} %get-tuple-element.111), channel_id=1, source_target_pairs={{0,31},{1,2},{2,1},{3,4},{4,3},{5,6},{6,5},{7,8},{8,7},{9,10},{10,... | collective-permute-start | bytes 122888 | tf_op jit(solution)/shard_map/ppermute | solution.py:43
  10.8 4.1 %collective-permute-start.2 = (f32[80,128]{1,0:T(8,128)S(1)}, f32[80,128]{1,0:T(8,128)S(1)}, u32[]{:S(2)}, u32[]{:S(2)}) collective-permute-start(f32[80,128]{1,0:T(8,128)S(1)} %get-tuple-element.112), channel_id=1, source_target_pairs={{0,30},{1,3},{2,0},{3,5},{4,2},{5,7},{6,4},{7,9},{8,6},{9,11},{10,... | collective-permute-start | bytes 122888 | tf_op jit(solution)/shard_map/ppermute | solution.py:43
  12.3 2.6 %collective-permute-start.3 = (f32[80,128]{1,0:T(8,128)S(1)}, f32[80,128]{1,0:T(8,128)S(1)}, u32[]{:S(2)}, u32[]{:S(2)}) collective-permute-start(f32[80,128]{1,0:T(8,128)S(1)} %get-tuple-element.113), channel_id=1, source_target_pairs={{0,1},{1,0},{2,3},{3,2},{4,5},{5,4},{6,7},{7,6},{8,9},{9,8},{10,11... | collective-permute-start | bytes 122888 | tf_op jit(solution)/shard_map/ppermute | solution.py:43
  17.0 7.8 %collective-permute-start.4 = (f32[80,128]{1,0:T(8,128)S(1)}, f32[80,128]{1,0:T(8,128)S(1)}, u32[]{:S(2)}, u32[]{:S(2)}) collective-permute-start(f32[80,128]{1,0:T(8,128)S(1)} %get-tuple-element.136), channel_id=1, source_target_pairs={{0,2},{1,31},{2,4},{3,1},{4,6},{5,3},{6,8},{7,5},{8,10},{9,7},{10,... | collective-permute-start | bytes 122888 | tf_op jit(solution)/shard_map/ppermute | solution.py:43
  19.3 7.0 %collective-permute-start.5 = (f32[80,128]{1,0:T(8,128)S(1)}, f32[80,128]{1,0:T(8,128)S(1)}, u32[]{:S(2)}, u32[]{:S(2)}) collective-permute-start(f32[80,128]{1,0:T(8,128)S(1)} %get-tuple-element.137), channel_id=1, source_target_pairs={{0,31},{1,2},{2,1},{3,4},{4,3},{5,6},{6,5},{7,8},{8,7},{9,10},{10,... | collective-permute-start | bytes 122888 | tf_op jit(solution)/shard_map/ppermute | solution.py:43
  20.5 5.9 %collective-permute-start.6 = (f32[80,128]{1,0:T(8,128)S(1)}, f32[80,128]{1,0:T(8,128)S(1)}, u32[]{:S(2)}, u32[]{:S(2)}) collective-permute-start(f32[80,128]{1,0:T(8,128)S(1)} %get-tuple-element.138), channel_id=1, source_target_pairs={{0,30},{1,3},{2,0},{3,5},{4,2},{5,7},{6,4},{7,9},{8,6},{9,11},{10,... | collective-permute-start | bytes 122888 | tf_op jit(solution)/shard_map/ppermute | solution.py:43
  22.6 3.7 %collective-permute-start.7 = (f32[80,128]{1,0:T(8,128)S(1)}, f32[80,128]{1,0:T(8,128)S(1)}, u32[]{:S(2)}, u32[]{:S(2)}) collective-permute-start(f32[80,128]{1,0:T(8,128)S(1)} %get-tuple-element.139), channel_id=1, source_target_pairs={{0,1},{1,0},{2,3},{3,2},{4,5},{5,4},{6,7},{7,6},{8,9},{9,8},{10,11... | collective-permute-start | bytes 122888 | tf_op jit(solution)/shard_map/ppermute | solution.py:43
  29.3 8.0 %collective-permute-start.8 = (f32[80,128]{1,0:T(8,128)S(1)}, f32[80,128]{1,0:T(8,128)S(1)}, u32[]{:S(2)}, u32[]{:S(2)}) collective-permute-start(f32[80,128]{1,0:T(8,128)S(1)} %get-tuple-element.169), channel_id=1, source_target_pairs={{0,2},{1,31},{2,4},{3,1},{4,6},{5,3},{6,8},{7,5},{8,10},{9,7},{10,... | collective-permute-start | bytes 122888 | tf_op jit(solution)/shard_map/ppermute | solution.py:43
  30.0 7.3 %collective-permute-start.9 = (f32[80,128]{1,0:T(8,128)S(1)}, f32[80,128]{1,0:T(8,128)S(1)}, u32[]{:S(2)}, u32[]{:S(2)}) collective-permute-start(f32[80,128]{1,0:T(8,128)S(1)} %get-tuple-element.170), channel_id=1, source_target_pairs={{0,31},{1,2},{2,1},{3,4},{4,3},{5,6},{6,5},{7,8},{8,7},{9,10},{10,... | collective-permute-start | bytes 122888 | tf_op jit(solution)/shard_map/ppermute | solution.py:43
  31.3 6.1 %collective-permute-start.10 = (f32[80,128]{1,0:T(8,128)S(1)}, f32[80,128]{1,0:T(8,128)S(1)}, u32[]{:S(2)}, u32[]{:S(2)}) collective-permute-start(f32[80,128]{1,0:T(8,128)S(1)} %get-tuple-element.171), channel_id=1, source_target_pairs={{0,30},{1,3},{2,0},{3,5},{4,2},{5,7},{6,4},{7,9},{8,6},{9,11},{10,... | collective-permute-start | bytes 122888 | tf_op jit(solution)/shard_map/ppermute | solution.py:43
  35.0 2.4 %collective-permute-start.11 = (f32[80,128]{1,0:T(8,128)S(1)}, f32[80,128]{1,0:T(8,128)S(1)}, u32[]{:S(2)}, u32[]{:S(2)}) collective-permute-start(f32[80,128]{1,0:T(8,128)S(1)} %get-tuple-element.172), channel_id=1, source_target_pairs={{0,1},{1,0},{2,3},{3,2},{4,5},{5,4},{6,7},{7,6},{8,9},{9,8},{10,11... | collective-permute-start | bytes 122888 | tf_op jit(solution)/shard_map/ppermute | solution.py:43
  39.4 7.9 %collective-permute-start.12 = (f32[80,128]{1,0:T(8,128)S(1)}, f32[80,128]{1,0:T(8,128)S(1)}, u32[]{:S(2)}, u32[]{:S(2)}) collective-permute-start(f32[80,128]{1,0:T(8,128)S(1)} %get-tuple-element.195), channel_id=1, source_target_pairs={{0,2},{1,31},{2,4},{3,1},{4,6},{5,3},{6,8},{7,5},{8,10},{9,7},{10,... | collective-permute-start | bytes 122888 | tf_op jit(solution)/shard_map/ppermute | solution.py:43
  39.5 7.8 %collective-permute-start.13 = (f32[80,128]{1,0:T(8,128)S(1)}, f32[80,128]{1,0:T(8,128)S(1)}, u32[]{:S(2)}, u32[]{:S(2)}) collective-permute-start(f32[80,128]{1,0:T(8,128)S(1)} %get-tuple-element.196), channel_id=1, source_target_pairs={{0,31},{1,2},{2,1},{3,4},{4,3},{5,6},{6,5},{7,8},{8,7},{9,10},{10,... | collective-permute-start | bytes 122888 | tf_op jit(solution)/shard_map/ppermute | solution.py:43
  42.3 5.0 %collective-permute-start.14 = (f32[80,128]{1,0:T(8,128)S(1)}, f32[80,128]{1,0:T(8,128)S(1)}, u32[]{:S(2)}, u32[]{:S(2)}) collective-permute-start(f32[80,128]{1,0:T(8,128)S(1)} %get-tuple-element.197), channel_id=1, source_target_pairs={{0,30},{1,3},{2,0},{3,5},{4,2},{5,7},{6,4},{7,9},{8,6},{9,11},{10,... | collective-permute-start | bytes 122888 | tf_op jit(solution)/shard_map/ppermute | solution.py:43
  45.1 2.2 %collective-permute-start.15 = (f32[80,128]{1,0:T(8,128)S(1)}, f32[80,128]{1,0:T(8,128)S(1)}, u32[]{:S(2)}, u32[]{:S(2)}) collective-permute-start(f32[80,128]{1,0:T(8,128)S(1)} %get-tuple-element.198), channel_id=1, source_target_pairs={{0,1},{1,0},{2,3},{3,2},{4,5},{5,4},{6,7},{7,6},{8,9},{9,8},{10,11... | collective-permute-start | bytes 122888 | tf_op jit(solution)/shard_map/ppermute | solution.py:43

commit v4 on v3

--- a/solution.py
+++ b/solution.py
@@ -125,8 +125,10 @@
     return matmul_each(lift_w[0:48, :192], [tall_faces(lift_in[:, lanes_of(q)]) for q in range(QUANTITIES)])
 
 
-def predict(taylor, star, deriv_w, works):
+def predict(taylor, star, deriv_w, works, between):
     for k in range(ORDER):
+        if k in between:
+            between[k]()
         for first in range(0, QUANTITIES, 3):
             if k:
                 values = star_tile(star, works[k % 2], range(first, first + 3), QUANTITIES)
@@ -276,6 +278,28 @@
         for partner in range(FACES):
             place = jnp.where(groups[f] == partner, order[f] - start + bases[partner], place)
             start = start + sizes[partner]
+        places.append(place)
+    return places
+
+
+def send_places(groups, scratch):
+    row = lax.broadcasted_iota(jnp.int32, (LANES, LANES), 0)
+    lane = lax.broadcasted_iota(jnp.int32, (LANES, LANES), 1)
+    earlier = jnp.where(row < lane, 1.0, 0.0).astype(BF16)
+    for f in range(FACES):
+        for partner in range(4):
+            scratch[4 * f + partner : 4 * f + partner + 1, :] = jnp.where(groups[f] == partner, 1.0, 0.0)
+    members = scratch[0:16, :]
+    before = matmul(members, earlier)
+    totals = jnp.sum(members, axis=1, keepdims=True)
+    starts = [64.0 * partner for partner in range(4)]
+    places = []
+    for f in range(FACES):
+        place = jnp.full((1, LANES), -1.0, F32)
+        for partner in range(4):
+            i = 4 * f + partner
+            place = jnp.where(groups[f] == partner, before[i : i + 1, :] + starts[partner], place)
+            starts[partner] = starts[partner] + totals[i : i + 1, :]
         places.append(place)
     return places
 
@@ -303,9 +327,7 @@
 
 def make_send_index(devices, neighbour, face_kind, index, flip, spare):
     groups, _, _ = partner_groups(devices, neighbour, face_kind)
-    element = lax.broadcasted_iota(jnp.int32, (1, LANES), 1)
-    keys = [(element + f * LANES).astype(F32) for f in range(FACES)]
-    places = group_places(groups, keys, flip)
+    places = send_places(groups, flip)
     for tile, (element, face) in enumerate(columns_of(places, spare)):
         index[2 * tile : 2 * tile + 1, :] = element
         index[2 * tile + 1 : 2 * tile + 2, :] = face
@@ -422,16 +444,6 @@
     r.packs[2:3, :] = jnp.bitwise_and(rank, PACK - 1)
     lane = lax.broadcasted_iota(jnp.int32, (1, LANES), 1)
     kinds = r.cluster[...]
-    for f in range(FACES):
-        r.source_cluster[f : f + 1, :] = take_lanes(kinds, r.index[8 + f : 9 + f, :])
-    got = [r.index[f : f + 1, :].astype(F32) for f in range(FACES)]
-    for tile, (element, _) in enumerate(columns_of(got, r.flips.at[10])):
-        kind = take_lanes(kinds, element)
-        for side in range(2):
-            width = 32 if tile else 64
-            parts = [turn_lanes(kind, width * j - 64 * side) for j in range(LANES // width)]
-            first = 2 * tile + side
-            r.column_cluster[first : first + 1, :] = choose(parts, lane, width)
     for tile in range(2):
         element = r.send_index[2 * tile : 2 * tile + 1, :]
         face = r.send_index[2 * tile + 1 : 2 * tile + 2, :]
@@ -449,6 +461,21 @@
                 r.send_packs[first : first + 1, :] = value
 
 
+def make_targets(r):
+    kinds = r.cluster[...]
+    lane = lax.broadcasted_iota(jnp.int32, (1, LANES), 1)
+    for f in range(FACES):
+        r.source_cluster[f : f + 1, :] = take_lanes(kinds, r.index[8 + f : 9 + f, :])
+    got = [r.index[f : f + 1, :].astype(F32) for f in range(FACES)]
+    for tile, (element, _) in enumerate(columns_of(got, r.flip)):
+        kind = take_lanes(kinds, element)
+        for side in range(2):
+            width = 32 if tile else 64
+            parts = [turn_lanes(kind, width * j - 64 * side) for j in range(LANES // width)]
+            first = 2 * tile + side
+            r.column_cluster[first : first + 1, :] = choose(parts, lane, width)
+
+
 def pack_flux(flux, element, packed):
     lane = lax.broadcasted_iota(jnp.int32, (FACES, LANES), 1)
     face = lax.broadcasted_iota(jnp.int32, (FACES, LANES), 0)
@@ -476,30 +503,36 @@
     lane = lax.broadcasted_iota(jnp.int32, (FACE_PAD, LANES), 1)
     nothing = jnp.zeros((FACE_PAD, LANES), F32)
     for k in range(PACKS):
+        group = [total[q] if q < QUANTITIES else nothing for q in range(GROUPS * k, GROUPS * (k + 1))]
+        turned = [turn_lanes(value, PACK * shift) for shift, value in enumerate(rotated_by_copy(group, lane))]
+        placed = rotated_by_copy(turned, lane)
         for f in range(FACES):
-            parts = []
-            for j in range(GROUPS):
-                q = GROUPS * k + j
-                parts.append(turn_lanes(total[q], PACK * (j - f)) if q < QUANTITIES else nothing)
-            lift_in[f * FACE_PAD : (f + 1) * FACE_PAD, lanes_of(k)] = choose(parts, lane, PACK)
+            lift_in[f * FACE_PAD : (f + 1) * FACE_PAD, lanes_of(k)] = placed[(GROUPS - f) % GROUPS]
     return [tall_faces(lift_in[:, lanes_of(k)]) for k in range(PACKS)]
 
 
-def packed_fields(r, block, base, ahead, gathered, flux, where, lift_in, work):
-    near_refs = (r.got_a, r.got_x) if block == 0 else (r.sum_a, r.sum_x)
-    far_refs = (r.got_y, r.got_z) if block == 0 else (r.sum_y, r.sum_z)
-    place = where[0:1, :]
-    near = jnp.bitwise_and(place, 63)
-    far = jnp.bitwise_and(place, PACK - 1)
+def received_piece(refs, place, p):
+    near, far = jnp.bitwise_and(place, 63), jnp.bitwise_and(place, PACK - 1)
+    got = [take_lanes(ref[rows_of(p // 2), :], near + 64 * (p % 2)) for ref in refs[:2]]
+    got += [take_lanes(ref[rows_of(p // 4), :], far + PACK * (p % 4)) for ref in refs[2:]]
+    got = jnp.where(place < 128, jnp.where(place < 64, got[0], got[1]), jnp.where(place < 192, got[2], got[3]))
+    return jnp.where(place >= 0, got, 0.0)
+
+
+def flux_sum(flux, pieces):
     total = [None] * QUANTITIES
     for p in range(QUANTITIES):
-        got = [take_lanes(ref[rows_of(p // 2), :], near + 64 * (p % 2)) for ref in near_refs]
-        got += [take_lanes(ref[rows_of(p // 4), :], far + PACK * (p % 4)) for ref in far_refs]
-        remote = jnp.where(place < 64, got[0], jnp.where(place < 128, got[1], jnp.where(place < 192, got[2], got[3])))
-        piece = gathered[rows_of(p), :] + jnp.where(place >= 0, remote, 0.0)
         for q in range(QUANTITIES):
-            term = flux[q, p : p + 1, :] * piece
+            term = flux(q, p) * pieces[p]
             total[q] = term if total[q] is None else total[q] + term
+    return total
+
+
+def packed_fields(r, block, base, ahead, gathered, flux, where, lift_in, work):
+    refs = [getattr(r, ("sum_" if block else "got_") + name) for name in "axyz"]
+    place = where[0:1, :]
+    pieces = [gathered[rows_of(p), :] + received_piece(refs, place, p) for p in range(QUANTITIES)]
+    total = flux_sum(lambda q, p: flux[q, p : p + 1, :], pieces)
     lifted = matmul_each(r.lift_w[:, :192], spread_faces(total, lift_in), 1)
     for k in range(PACKS):
         work[:, lanes_of(k)] = ahead[:, lanes_of(k)] - lifted[k][48:176, :]
@@ -509,6 +542,12 @@
 def packed_derivatives(terms, deriv_w, work):
     for k in range(PACKS):
         work[:, lanes_of(k)] = matmul(deriv_w[...], tall_basis(terms[k]))
+
+
+def rotated_by_copy(values, lane):
+    odd, high = jnp.bitwise_and(lane, PACK) != 0, lane >= 2 * PACK
+    step = [jnp.where(odd, values[(i + 1) % GROUPS], values[i]) for i in range(GROUPS)]
+    return [jnp.where(high, step[(i + 2) % GROUPS], step[i]) for i in range(GROUPS)]
 
 
 def gather_copies(values):
@@ -517,21 +556,14 @@
         value = values[0]
         rolled = [pltpu.roll(value, PACK * shift, 1) for shift in (1, 2, 3)]
         return jnp.where(lane < PACK, (value + rolled[0]) + (rolled[1] + rolled[2]), 0.0)
-    parts = []
-    for shift in range(GROUPS):
-        mixed = choose([values[(copy + shift) % GROUPS] for copy in range(GROUPS)], lane, PACK)
-        parts.append(turn_lanes(mixed, PACK * shift))
+    mixed = rotated_by_copy(values, lane)
+    parts = [turn_lanes(mixed[shift], PACK * shift) for shift in range(GROUPS)]
     return (parts[0] + parts[1]) + (parts[2] + parts[3])
 
 
-def packed_star(star, work, follow=None):
-    result = []
-    for k in range(PACKS):
-        quantities = range(GROUPS * k, min(GROUPS * (k + 1), QUANTITIES))
-        result.append(gather_copies(star_tile(star, work, quantities, PACKS)))
-        if follow is not None:
-            follow(k, result[k])
-    return result
+def packed_star(star, work, k):
+    quantities = range(GROUPS * k, min(GROUPS * (k + 1), QUANTITIES))
+    return gather_copies(star_tile(star, work, quantities, PACKS))
 
 
 def packed_faces(integrals, turn_w, where, put):
@@ -571,14 +603,13 @@
     first = [None] * len(blocks)
     second = None
     for k in range(ORDER):
-        for b, block in enumerate(blocks):
-            if k:
+        for i in range(PACKS if k else 0):
+            for b, block in enumerate(blocks):
                 work, other = (block.work, block.spare) if k % 2 else (block.spare, block.work)
-
-                def follow(i, value, other=other):
-                    other[:, lanes_of(i)] = matmul(r.deriv_w[...], tall_basis(value))
-
-                terms[b] = packed_star(block.star, work, follow if k < ORDER - 1 else None)
+                terms[b][i] = packed_star(block.star, work, i)
+                if k < ORDER - 1:
+                    other[:, lanes_of(i)] = matmul(r.deriv_w[...], tall_basis(terms[b][i]))
+        for b in range(len(blocks)):
             first[b] = add_terms(first[b], terms[b], 1.0 / math.factorial(k + 1))
         if slot == 2:
             second = add_terms(second, terms[1], (2.0 ** (k + 1) - 1.0) / math.factorial(k + 1))
@@ -622,9 +653,11 @@
     r.orientation_out[...] = r.orientation[...]
     r.cluster_out[...] = r.cluster[...].reshape(1, LANES)
     r.far_out[...] = r.neighbour_face[...]
-    make_send_index(devices, r.neighbour, r.face_kind, r.send_index, r.flip, r.flap)
-    make_faces(r.proj, r.orient, r.frame, r.proj_w, r.turn_w, r.flop)
-    predict(r.taylor, r.star, r.deriv_w, (r.spare, r.work))
+    between = {
+        1: lambda: make_send_index(devices, r.neighbour, r.face_kind, r.send_index, r.flip, r.flap),
+        2: lambda: make_faces(r.proj, r.orient, r.frame, r.proj_w, r.turn_w, r.flop),
+    }
+    predict(r.taylor, r.star, r.deriv_w, (r.spare, r.work), between)
     span = lax.shift_left(jnp.ones_like(r.cluster_out[...]), r.cluster_out[...]).astype(F32)
     for q in range(QUANTITIES):
         r.step[q] = step_integral(r.taylor, q, span)
@@ -637,8 +670,7 @@
 
 
 def last_kernel(r):
-    add_received(r)
-    unpack_receives([r.sum_a, r.sum_x, r.sum_y, r.sum_z], r.near, r.far)
+    unpack_receives([getattr(r, name) for name in RECEIVED], r.near, r.far)
 
     def keep(f, value):
         r.collected[f] = value
@@ -682,13 +714,12 @@
             value = jnp.where(cluster == 1, unpack_quantity(packed(getattr(r, name + "1")), q, rank), value)
         return value
 
-    sums = r.sums
-    for g in range(FACES):
+    sums = r.sums if slot else r.faces
+    if slot == 1:
+        make_targets(r)
+    for g in range(FACES if slot else 0):
         reset = r.source_cluster[g : g + 1, :] <= (0 if slot % 2 else 1)
         for q in range(QUANTITIES):
-            if slot == 0:
-                sums[g, rows_of(q), :] = r.faces[g, rows_of(q), :]
-                continue
             value = jnp.where(started, unpacked("faces", q, g), r.later[g, rows_of(q), :])
             sums[g, rows_of(q), :] = value + jnp.where(reset, 0.0, r.old_sums[g, rows_of(q), :])
     if slot:
@@ -707,6 +738,12 @@
                 value = jnp.where(face == g, take_lanes(sums[g], lane), 0.0)
                 total = value if total is None else total + value
             r.gathered[f] = total
+        unpack_receives([r.old_a, r.old_x, r.old_y, r.old_z], r.near, r.far)
+
+        def keep(f, value):
+            r.gathered[f] = value
+
+        add_remote(r.index, r.near, r.far, r.gathered, keep)
     if slot == 0:
         fields = [r.taylor[0, q] for q in range(QUANTITIES)]
         steps = [r.step[q] for q in range(QUANTITIES)]
@@ -855,15 +892,14 @@
         {**some(sends, "taylor", "step", "faces"),
          **some(v, "star", "orientation", "cluster", "flux_local", "flux_neigh", "face_kind", "neighbour",
                 "neighbour_face", "update", "lift_mat", "deriv_w", "proj_w", "turn_w", "send_index")},
-        dict(base=STATE, sums=TURNED, source_cluster=ints(FACES), column_cluster=ints(4),
-             flux_own=shape_of(flux_local), later1=TURNED, update_w=SQUARE, lift_w=shape(176, 256), index=ints(24), packs=ints(8),
+        dict(base=STATE, flux_own=shape_of(flux_local), later1=TURNED, update_w=SQUARE, lift_w=shape(176, 256), index=ints(24), packs=ints(8),
              send_packs=ints(12), where0=ints(8), star0=PACKED_STAR, flux0=PACKED_FLUX,
              base0=PACKED, ahead0=AHEAD, gathered0=TILE, **LATER_SENDS),
-        dict(work=WORK, lift_in=LIFT_IN, flips=shape(11, LANES, LANES)),
+        dict(work=WORK, lift_in=LIFT_IN, flips=shape(10, LANES, LANES)),
         50_000_000,
     )
     v.update(kept)
-    v.update(taylor=sends["taylor"])
+    v.update(taylor=sends["taylor"], sums=sends["faces"])
     for slot in range(1, SLOTS):
         numbers = (0, 1) if slot == 2 else (0,)
         per_block = [name + str(b) for b in numbers for name in ("base", "ahead", "gathered", "flux", "star", "where")]
@@ -892,10 +928,9 @@
             ins.update({"older_" + name: v["old_" + name] for name in "axyz"})
         ins.update(old_base=v["base"], old_sums=v["sums"], later=v["later%d" % slot])
         ins.update(
-            some(v, "star", "cluster", "flux_own", "proj_w", "update_w", "lift_w", "packs", "source_cluster",
-                 "column_cluster")
+            some(v, "star", "cluster", "flux_own", "proj_w", "update_w", "lift_w", "packs")
         )
-        results = dict(base=STATE, **OLD)
+        results = dict(base=STATE, **(OLD if slot < 3 else {}))
         scratch = dict(work=WORK, lift_in=LIFT_IN)
         if slot < 3:
             ins.update(some(v, "send_index", "deriv_w", "where0"))
@@ -903,8 +938,12 @@
         else:
             ins.update(some(v, "index"))
             results.update(gathered=TURNED)
-            scratch.update(sums=TURNED)
+            scratch.update(sums=TURNED, near=TILE, far=TILE, **OLD)
+        if slot > 1:
+            ins.update(some(v, "source_cluster", "column_cluster"))
         if slot == 1:
+            scratch.update(flip=SQUARE)
+            results.update(source_cluster=ints(FACES), column_cluster=ints(4))
             ins.update(some(v, "flux_neigh", "orientation", "index", "turn_w", "taylor"))
             results.update(later2=TURNED, later3=TURNED, base1=PACKED, ahead1=AHEAD, gathered1=TILE, where1=ints(8), star1=PACKED_STAR,
                            flux1=PACKED_FLUX)
@@ -922,9 +961,9 @@
     return call(
         last_kernel,
         "finish",
-        {**receives, **some(v, *OLD, "base", "gathered", "flux_neigh", "lift_w", "index")},
+        {**receives, **some(v, "base", "gathered", "flux_neigh", "lift_w", "index")},
         dict(out=shape(*dofs.shape)),
-        dict(**SUMS, near=TILE, far=TILE, collected=TURNED, lift_in=LIFT_IN),
+        dict(near=TILE, far=TILE, collected=TURNED, lift_in=LIFT_IN),
         10_000_000,
     )["out"]
 

time: 48.9 us -> 48.5 us (level)
  transfers between devices with their start and end apart: 16 -> 16, of which waited for: 4 -> 4; matrix products, arithmetic and copies ran while one was open for 0% -> 0% of each run, Pallas kernels for 17% -> 18%
where the time goes in v4:
time: 48.5 us; the launch traced here: 48.4 us
  starting transfers between devices  25.2 us (52%)
  Pallas kernels  19.6 us (40%)
  waiting for transfers between devices  2.37 us (5%)
  local copies, waits for them, and re-layouts  1.04 us (2%)
    ppermute x16, starting transfers between devices, exchange(): lax.ppermute(sends[NAMES[partner]], 'dom', pairs)  25.2 us
    pallas_call x10, Pallas kernels, call(): pl.pallas_call(run, out_shape=list(outs.values()), in_specs=[VMEM] * len(...  19.6 us
    ppermute x16, waiting for transfers between devices, exchange(): lax.ppermute(sends[NAMES[partner]], 'dom', pairs)  2.37 us
    unnamed x28, local copies, waits for them, and re-layouts  1.04 us
  transfers between devices with their start and end apart: 16, of which 4 were waited for; matrix products, arithmetic and copies ran while one was open for 0% of the time, Pallas kernels for 18%

profile of v4, /device:TPU:0, one launch (start us, length us, event | category | flops | bytes accessed | tf_op | source)
XLA Modules:
  0.0 48.4 jit_solution(8508540781540371108)
XLA Ops:
  0.1 0.0 copy-start.9
  0.1 0.7 %copy-done.8 = f32[3,15,15]{2,1,0:T(8,128)S(1)} copy-done((f32[3,15,15]{2,1,0:T(8,128)S(1)}, f32[3,15,15]{2,1,0:T(8,128)}, u32[]{:S(2)}) %copy-start.8) | copy-done | bytes 2724
  0.7 0.0 copy-done.7
  0.8 0.1 copy-done.4
  0.9 0.1 copy-done
  1.0 0.1 copy-done.2
  1.1 0.0 copy-start.5
  1.1 2.9 %start.1 = (f32[128,128]{1,0:T(8,128)S(1)}, s32[4,128]{1,0:T(4,128)S(1)}, f32[64,128]{1,0:T(8,128)S(1)}, f32[192,128]{1,0:T(8,128)S(1)}, s32[8,128]{1,0:T(8,128)...) custom-call(f32[128,128]{1,0:T(8,128)S(1)} %frame.1.refs_0_, ...), custom_call_target="tpu_custom_call" | custom-call | flops 100000000 | bytes 2155720 | tf_op jit(solution)/shard_map/start/pallas_call | solution.py:845
  4.0 3.0 %collective-permute-start = (f32[80,128]{1,0:T(8,128)S(1)}, f32[80,128]{1,0:T(8,128)S(1)}, u32[]{:S(2)}, u32[]{:S(2)}) collective-permute-start(f32[80,128]{1,0:T(8,128)S(1)} %get-tuple-element.105), channel_id=1, source_target_pairs={{0,2},{1,31},{2,4},{3,1},{4,6},{5,3},{6,8},{7,5},{8,10},{9,7},{10,... | collective-permute-start | bytes 122888 | tf_op jit(solution)/shard_map/ppermute | solution.py:43
  7.0 3.7 %collective-permute-start.1 = (f32[80,128]{1,0:T(8,128)S(1)}, f32[80,128]{1,0:T(8,128)S(1)}, u32[]{:S(2)}, u32[]{:S(2)}) collective-permute-start(f32[80,128]{1,0:T(8,128)S(1)} %get-tuple-element.106), channel_id=1, source_target_pairs={{0,31},{1,2},{2,1},{3,4},{4,3},{5,6},{6,5},{7,8},{8,7},{9,10},{10,... | collective-permute-start | bytes 122888 | tf_op jit(solution)/shard_map/ppermute | solution.py:43
  10.7 1.4 %collective-permute-start.2 = (f32[80,128]{1,0:T(8,128)S(1)}, f32[80,128]{1,0:T(8,128)S(1)}, u32[]{:S(2)}, u32[]{:S(2)}) collective-permute-start(f32[80,128]{1,0:T(8,128)S(1)} %get-tuple-element.107), channel_id=1, source_target_pairs={{0,30},{1,3},{2,0},{3,5},{4,2},{5,7},{6,4},{7,9},{8,6},{9,11},{10,... | collective-permute-start | bytes 122888 | tf_op jit(solution)/shard_map/ppermute | solution.py:43
  12.2 2.3 %beside0.1 = (f32[9,40,128]{2,1,0:T(8,128)S(1)}, f32[9,9,4,128]{3,2,1,0:T(4,128)S(1)}, f32[4,144,128]{2,1,0:T(8,128)S(1)}, f32[128,128]{1,0:T(8,128)S(1)}, f32[1...) custom-call(f32[5,9,40,128]{3,2,1,0:T(8,128)S(1)} %get-tuple-element, ...), custom_call_target="tpu_custom_call" | custom-call | flops 50000000 | bytes 3585596 | tf_op jit(solution)/shard_map/beside0/pallas_call | solution.py:845
  14.5 0.3 collective-permute-done.2.refs_2_.refs_5_
  14.7 2.0 %slot1.1 = (f32[3,40,128]{2,1,0:T(8,128)S(1)}, f32[3,40,128]{2,1,0:T(8,128)S(1)}, f32[4,48,128]{2,1,0:T(8,128)S(1)}, f32[80,128]{1,0:T(8,128)S(1)}, f32[80,128]{...) custom-call(f32[80,128]{1,0:T(8,128)S(1)} %collective-permute-done.refs_0_.refs_3_, ...), custom_call_target="tpu_custom_call" | custom-call | flops 100000000 | bytes 1481728 | tf_op jit(solution)/shard_map/slot1/pallas_call | solution.py:845
  16.8 2.4 %collective-permute-start.4 = (f32[80,128]{1,0:T(8,128)S(1)}, f32[80,128]{1,0:T(8,128)S(1)}, u32[]{:S(2)}, u32[]{:S(2)}) collective-permute-start(f32[80,128]{1,0:T(8,128)S(1)} %get-tuple-element.131), channel_id=1, source_target_pairs={{0,2},{1,31},{2,4},{3,1},{4,6},{5,3},{6,8},{7,5},{8,10},{9,7},{10,... | collective-permute-start | bytes 122888 | tf_op jit(solution)/shard_map/ppermute | solution.py:43
  19.2 0.8 %collective-permute-start.5 = (f32[80,128]{1,0:T(8,128)S(1)}, f32[80,128]{1,0:T(8,128)S(1)}, u32[]{:S(2)}, u32[]{:S(2)}) collective-permute-start(f32[80,128]{1,0:T(8,128)S(1)} %get-tuple-element.132), channel_id=1, source_target_pairs={{0,31},{1,2},{2,1},{3,4},{4,3},{5,6},{6,5},{7,8},{8,7},{9,10},{10,... | collective-permute-start | bytes 122888 | tf_op jit(solution)/shard_map/ppermute | solution.py:43
  20.0 2.4 %collective-permute-start.6 = (f32[80,128]{1,0:T(8,128)S(1)}, f32[80,128]{1,0:T(8,128)S(1)}, u32[]{:S(2)}, u32[]{:S(2)}) collective-permute-start(f32[80,128]{1,0:T(8,128)S(1)} %get-tuple-element.133), channel_id=1, source_target_pairs={{0,30},{1,3},{2,0},{3,5},{4,2},{5,7},{6,4},{7,9},{8,6},{9,11},{10,... | collective-permute-start | bytes 122888 | tf_op jit(solution)/shard_map/ppermute | solution.py:43
  22.4 2.4 %beside1.1 = (f32[9,40,128]{2,1,0:T(8,128)S(1)}, f32[80,128]{1,0:T(8,128)S(1)}, f32[80,128]{1,0:T(8,128)S(1)}, f32[80,128]{1,0:T(8,128)S(1)}, f32[80,128]{1,0:T(...) custom-call(f32[3,40,128]{2,1,0:T(8,128)S(1)} %get-tuple-element.135, ...), custom_call_target="tpu_custom_call" | custom-call | flops 50000000 | bytes 5157888 | tf_op jit(solution)/shard_map/beside1/pallas_call | solution.py:845
  24.8 1.4 %collective-permute-done.5.refs_1_ = f32[80,128]{1,0:T(8,128)S(1)} collective-permute-done((f32[80,128]{1,0:T(8,128)S(1)}, f32[80,128]{1,0:T(8,128)S(1)}, u32[]{:S(2)}, u32[]{:S(2)}) %collective-permute-start.5) | collective-permute-done | bytes 40992 | tf_op jit(solution)/shard_map/ppermute | solution.py:43
  26.2 2.8 %slot2.1 = (f32[3,40,128]{2,1,0:T(8,128)S(1)}, f32[3,40,128]{2,1,0:T(8,128)S(1)}, f32[4,48,128]{2,1,0:T(8,128)S(1)}, f32[3,40,128]{2,1,0:T(8,128)S(1)}, f32[3,40...) custom-call(f32[80,128]{1,0:T(8,128)S(1)} %collective-permute-done.4, ...), custom_call_target="tpu_custom_call" | custom-call | flops 100000000 | bytes 2510848 | tf_op jit(solution)/shard_map/slot2/pallas_call | solution.py:845
  29.0 0.4 collective-permute-start.8
  29.4 1.8 %collective-permute-start.9 = (f32[80,128]{1,0:T(8,128)S(1)}, f32[80,128]{1,0:T(8,128)S(1)}, u32[]{:S(2)}, u32[]{:S(2)}) collective-permute-start(f32[80,128]{1,0:T(8,128)S(1)} %get-tuple-element.162), channel_id=1, source_target_pairs={{0,31},{1,2},{2,1},{3,4},{4,3},{5,6},{6,5},{7,8},{8,7},{9,10},{10,... | collective-permute-start | bytes 122888 | tf_op jit(solution)/shard_map/ppermute | solution.py:43
  31.3 3.4 %collective-permute-start.10 = (f32[80,128]{1,0:T(8,128)S(1)}, f32[80,128]{1,0:T(8,128)S(1)}, u32[]{:S(2)}, u32[]{:S(2)}) collective-permute-start(f32[80,128]{1,0:T(8,128)S(1)} %get-tuple-element.163), channel_id=1, source_target_pairs={{0,30},{1,3},{2,0},{3,5},{4,2},{5,7},{6,4},{7,9},{8,6},{9,11},{10,... | collective-permute-start | bytes 122888 | tf_op jit(solution)/shard_map/ppermute | solution.py:43
  34.7 2.2 %beside2.1 = (f32[9,40,128]{2,1,0:T(8,128)S(1)}, f32[80,128]{1,0:T(8,128)S(1)}, f32[80,128]{1,0:T(8,128)S(1)}, f32[80,128]{1,0:T(8,128)S(1)}, f32[80,128]{1,0:T(...) custom-call(f32[3,40,128]{2,1,0:T(8,128)S(1)} %get-tuple-element.165, ...), custom_call_target="tpu_custom_call" | custom-call | flops 50000000 | bytes 3921920 | tf_op jit(solution)/shard_map/beside2/pallas_call | solution.py:845
  36.9 0.2 collective-permute-done.8.refs_0_.refs_3_
  37.1 2.0 %slot3.1 = (f32[3,40,128]{2,1,0:T(8,128)S(1)}, f32[3,40,128]{2,1,0:T(8,128)S(1)}, f32[4,48,128]{2,1,0:T(8,128)S(1)}, f32[80,128]{1,0:T(8,128)S(1)}, f32[80,128]{...) custom-call(f32[80,128]{1,0:T(8,128)S(1)} %collective-permute-done.8.refs_0_.refs_3_, ...), custom_call_target="tpu_custom_call" | custom-call | flops 100000000 | bytes 1481728 | tf_op jit(solution)/shard_map/slot3/pallas_call | solution.py:845
  39.1 0.1 collective-permute-start.12
  39.2 2.8 %collective-permute-start.13 = (f32[80,128]{1,0:T(8,128)S(1)}, f32[80,128]{1,0:T(8,128)S(1)}, u32[]{:S(2)}, u32[]{:S(2)}) collective-permute-start(f32[80,128]{1,0:T(8,128)S(1)} %get-tuple-element.190), channel_id=1, source_target_pairs={{0,31},{1,2},{2,1},{3,4},{4,3},{5,6},{6,5},{7,8},{8,7},{9,10},{10,... | collective-permute-start | bytes 122888 | tf_op jit(solution)/shard_map/ppermute | solution.py:43
  42.0 2.8 %collective-permute-start.14 = (f32[80,128]{1,0:T(8,128)S(1)}, f32[80,128]{1,0:T(8,128)S(1)}, u32[]{:S(2)}, u32[]{:S(2)}) collective-permute-start(f32[80,128]{1,0:T(8,128)S(1)} %get-tuple-element.191), channel_id=1, source_target_pairs={{0,30},{1,3},{2,0},{3,5},{4,2},{5,7},{6,4},{7,9},{8,6},{9,11},{10,... | collective-permute-start | bytes 122888 | tf_op jit(solution)/shard_map/ppermute | solution.py:43
  44.8 1.7 %beside3.1 = (f32[9,40,128]{2,1,0:T(8,128)S(1)}, f32[4,144,128]{2,1,0:T(8,128)S(1)}) custom-call(f32[3,40,128]{2,1,0:T(8,128)S(1)} %get-tuple-element.193.refs_0_, f32[3,40,128]{2,1,0:T(8,128)S(1)} %get-tuple-element.194.refs_1_, f32[4,48,128]{2,1,0:T(8,128)S(1)} %get-tuple-element.195.refs_2_, f32[80,128]{1,0:T(8,128)S(1)} %collective-permute-done.8.refs_0_.refs_3_, ...), custom_call_target="tpu_custom_call" | custom-call | flops 50000000 | bytes 2392064 | tf_op jit(solution)/shard_map/beside3/pallas_call | solution.py:845
  46.5 0.5 collective-permute-done.12.refs_0_
  47.0 1.4 %finish.1 = f32[9,35,128]{2,1,0:T(8,128)} custom-call(f32[80,128]{1,0:T(8,128)S(1)} %collective-permute-done.12.refs_0_, f32[80,128]{1,0:T(8,128)S(1)} %collective-permute-done.13.refs_1_, f32[80,128]{1,0:T(8,128)S(1)} %collective-permute-done.14.refs_2_, f32[80,128]{1,0:T(8,128)S(1)} %collective-permute-done.15.refs_3_, ...), custom_call_target="tpu_custom_call" | custom-call | flops 10000000 | bytes 1162752 | tf_op jit(solution)/shard_map/finish/pallas_call | solution.py:845
  (38 shorter events, 0.1 us)
Async XLA Ops:
  0.0 0.7 %copy-start.8 = (f32[3,15,15]{2,1,0:T(8,128)S(1)}, f32[3,15,15]{2,1,0:T(8,128)}, u32[]{:S(2)}) copy-start(f32[3,15,15]{2,1,0:T(8,128)} %refs_8_.2) | copy-start | bytes 8104
  0.0 0.8 %copy-start.7 = (f32[4,15,35]{2,0,1:T(4,128)S(1)}, f32[4,15,35]{2,0,1:T(4,128)}, u32[]{:S(2)}) copy-start(f32[4,15,35]{2,0,1:T(4,128)} %param.25) | copy-start | bytes 25204
  0.0 0.9 %copy-start.4 = (f32[3,35,35]{2,1,0:T(8,128)S(1)}, f32[3,35,35]{2,1,0:T(8,128)}, u32[]{:S(2)}) copy-start(f32[3,35,35]{2,1,0:T(8,128)} %refs_6_.1) | copy-start | bytes 44104
  0.0 1.0 %copy-start = (f32[3,9,9,128]{3,0,2,1:T(4,128)S(1)}, f32[3,9,9,128]{3,0,2,1:T(4,128)}, u32[]{:S(2)}) copy-start(f32[3,9,9,128]{3,0,2,1:T(4,128)} %param.15) | copy-start | bytes 373252
  0.0 1.1 %copy-start.2 = (f32[9,35,128]{2,1,0:T(8,128)S(1)}, f32[9,35,128]{2,1,0:T(8,128)}, u32[]{:S(2)}) copy-start(f32[9,35,128]{2,1,0:T(8,128)} %refs_9_.2) | copy-start | bytes 483844
  0.0 1.1 %copy-start.10 = (s32[4,128]{1,0:T(4,128)S(1)}, s32[4,128]{1,0:T(4,128)}, u32[]{:S(2)}) copy-start(s32[4,128]{1,0:T(4,128)} %refs_8_.3) | copy-start | bytes 6148
  0.0 1.1 %copy-start.11 = (s32[4,128]{1,0:T(4,128)S(1)}, s32[4,128]{1,0:T(4,128)}, u32[]{:S(2)}) copy-start(s32[4,128]{1,0:T(4,128)} %refs_2_.1) | copy-start | bytes 6148
  0.0 1.0 %copy-start.12 = (s32[4,128]{1,0:T(4,128)S(1)}, s32[4,128]{1,0:T(4,128)}, u32[]{:S(2)}) copy-start(s32[4,128]{1,0:T(4,128)} %refs_4_.1) | copy-start | bytes 6148
  0.1 1.0 %copy-start.9 = (s32[4,128]{1,0:T(4,128)S(1)}, s32[4,128]{1,0:T(4,128)}, u32[]{:S(2)}) copy-start(s32[4,128]{1,0:T(4,128)} %refs_9_.3) | copy-start | bytes 6148
  0.1 1.0 %copy-start.13 = (s32[128]{0:T(128)S(1)}, s32[128]{0:T(128)}, u32[]{:S(2)}) copy-start(s32[128]{0:T(128)} %refs_5_.1) | copy-start | bytes 1540
  1.1 11.1 %copy-start.1 = (f32[4,9,9,128]{3,0,2,1:T(4,128)S(1)}, f32[4,9,9,128]{3,0,2,1:T(4,128)}, u32[]{:S(2)}) copy-start(f32[4,9,9,128]{3,0,2,1:T(4,128)} %param.17) | copy-start | bytes 497668
  1.1 11.1 %copy-start.3 = (f32[4,9,9,128]{3,0,2,1:T(4,128)S(1)}, f32[4,9,9,128]{3,0,2,1:T(4,128)}, u32[]{:S(2)}) copy-start(f32[4,9,9,128]{3,0,2,1:T(4,128)} %param.16) | copy-start | bytes 497668
  1.1 11.1 %copy-start.5 = (f32[3,35,35]{2,1,0:T(8,128)S(1)}, f32[3,35,35]{2,1,0:T(8,128)}, u32[]{:S(2)}) copy-start(f32[3,35,35]{2,1,0:T(8,128)} %refs_11_.1) | copy-start | bytes 44104
  4.0 8.2 %copy-start.6 = (f32[4,35,15]{1,0,2:T(4,128)S(1)}, f32[4,35,15]{1,0,2:T(4,128)}, u32[]{:S(2)}) copy-start(f32[4,35,15]{1,0,2:T(4,128)} %param.26) | copy-start | bytes 25204
  4.0 10.4 %collective-permute-start = (f32[80,128]{1,0:T(8,128)S(1)}, f32[80,128]{1,0:T(8,128)S(1)}, u32[]{:S(2)}, u32[]{:S(2)}) collective-permute-start(f32[80,128]{1,0:T(8,128)S(1)} %get-tuple-element.105), channel_id=1, source_target_pairs={{0,2},{1,31},{2,4},{3,1},{4,6},{5,3},{6,8},{7,5},{8,10},{9,7},{10,... | collective-permute-start | bytes 122888 | tf_op jit(solution)/shard_map/ppermute | solution.py:43
  7.0 7.4 %collective-permute-start.1 = (f32[80,128]{1,0:T(8,128)S(1)}, f32[80,128]{1,0:T(8,128)S(1)}, u32[]{:S(2)}, u32[]{:S(2)}) collective-permute-start(f32[80,128]{1,0:T(8,128)S(1)} %get-tuple-element.106), channel_id=1, source_target_pairs={{0,31},{1,2},{2,1},{3,4},{4,3},{5,6},{6,5},{7,8},{8,7},{9,10},{10,... | collective-permute-start | bytes 122888 | tf_op jit(solution)/shard_map/ppermute | solution.py:43
  10.7 4.0 %collective-permute-start.2 = (f32[80,128]{1,0:T(8,128)S(1)}, f32[80,128]{1,0:T(8,128)S(1)}, u32[]{:S(2)}, u32[]{:S(2)}) collective-permute-start(f32[80,128]{1,0:T(8,128)S(1)} %get-tuple-element.107), channel_id=1, source_target_pairs={{0,30},{1,3},{2,0},{3,5},{4,2},{5,7},{6,4},{7,9},{8,6},{9,11},{10,... | collective-permute-start | bytes 122888 | tf_op jit(solution)/shard_map/ppermute | solution.py:43
  12.2 2.6 %collective-permute-start.3 = (f32[80,128]{1,0:T(8,128)S(1)}, f32[80,128]{1,0:T(8,128)S(1)}, u32[]{:S(2)}, u32[]{:S(2)}) collective-permute-start(f32[80,128]{1,0:T(8,128)S(1)} %get-tuple-element.108), channel_id=1, source_target_pairs={{0,1},{1,0},{2,3},{3,2},{4,5},{5,4},{6,7},{7,6},{8,9},{9,8},{10,11... | collective-permute-start | bytes 122888 | tf_op jit(solution)/shard_map/ppermute | solution.py:43
  16.8 8.1 %collective-permute-start.4 = (f32[80,128]{1,0:T(8,128)S(1)}, f32[80,128]{1,0:T(8,128)S(1)}, u32[]{:S(2)}, u32[]{:S(2)}) collective-permute-start(f32[80,128]{1,0:T(8,128)S(1)} %get-tuple-element.131), channel_id=1, source_target_pairs={{0,2},{1,31},{2,4},{3,1},{4,6},{5,3},{6,8},{7,5},{8,10},{9,7},{10,... | collective-permute-start | bytes 122888 | tf_op jit(solution)/shard_map/ppermute | solution.py:43
  19.2 7.0 %collective-permute-start.5 = (f32[80,128]{1,0:T(8,128)S(1)}, f32[80,128]{1,0:T(8,128)S(1)}, u32[]{:S(2)}, u32[]{:S(2)}) collective-permute-start(f32[80,128]{1,0:T(8,128)S(1)} %get-tuple-element.132), channel_id=1, source_target_pairs={{0,31},{1,2},{2,1},{3,4},{4,3},{5,6},{6,5},{7,8},{8,7},{9,10},{10,... | collective-permute-start | bytes 122888 | tf_op jit(solution)/shard_map/ppermute | solution.py:43
  20.0 6.2 %collective-permute-start.6 = (f32[80,128]{1,0:T(8,128)S(1)}, f32[80,128]{1,0:T(8,128)S(1)}, u32[]{:S(2)}, u32[]{:S(2)}) collective-permute-start(f32[80,128]{1,0:T(8,128)S(1)} %get-tuple-element.133), channel_id=1, source_target_pairs={{0,30},{1,3},{2,0},{3,5},{4,2},{5,7},{6,4},{7,9},{8,6},{9,11},{10,... | collective-permute-start | bytes 122888 | tf_op jit(solution)/shard_map/ppermute | solution.py:43
  22.4 3.8 %collective-permute-start.7 = (f32[80,128]{1,0:T(8,128)S(1)}, f32[80,128]{1,0:T(8,128)S(1)}, u32[]{:S(2)}, u32[]{:S(2)}) collective-permute-start(f32[80,128]{1,0:T(8,128)S(1)} %get-tuple-element.134), channel_id=1, source_target_pairs={{0,1},{1,0},{2,3},{3,2},{4,5},{5,4},{6,7},{7,6},{8,9},{9,8},{10,11... | collective-permute-start | bytes 122888 | tf_op jit(solution)/shard_map/ppermute | solution.py:43
  29.0 8.1 %collective-permute-start.8 = (f32[80,128]{1,0:T(8,128)S(1)}, f32[80,128]{1,0:T(8,128)S(1)}, u32[]{:S(2)}, u32[]{:S(2)}) collective-permute-start(f32[80,128]{1,0:T(8,128)S(1)} %get-tuple-element.161), channel_id=1, source_target_pairs={{0,2},{1,31},{2,4},{3,1},{4,6},{5,3},{6,8},{7,5},{8,10},{9,7},{10,... | collective-permute-start | bytes 122888 | tf_op jit(solution)/shard_map/ppermute | solution.py:43
  29.4 7.7 %collective-permute-start.9 = (f32[80,128]{1,0:T(8,128)S(1)}, f32[80,128]{1,0:T(8,128)S(1)}, u32[]{:S(2)}, u32[]{:S(2)}) collective-permute-start(f32[80,128]{1,0:T(8,128)S(1)} %get-tuple-element.162), channel_id=1, source_target_pairs={{0,31},{1,2},{2,1},{3,4},{4,3},{5,6},{6,5},{7,8},{8,7},{9,10},{10,... | collective-permute-start | bytes 122888 | tf_op jit(solution)/shard_map/ppermute | solution.py:43
  31.3 5.8 %collective-permute-start.10 = (f32[80,128]{1,0:T(8,128)S(1)}, f32[80,128]{1,0:T(8,128)S(1)}, u32[]{:S(2)}, u32[]{:S(2)}) collective-permute-start(f32[80,128]{1,0:T(8,128)S(1)} %get-tuple-element.163), channel_id=1, source_target_pairs={{0,30},{1,3},{2,0},{3,5},{4,2},{5,7},{6,4},{7,9},{8,6},{9,11},{10,... | collective-permute-start | bytes 122888 | tf_op jit(solution)/shard_map/ppermute | solution.py:43
  34.7 2.4 %collective-permute-start.11 = (f32[80,128]{1,0:T(8,128)S(1)}, f32[80,128]{1,0:T(8,128)S(1)}, u32[]{:S(2)}, u32[]{:S(2)}) collective-permute-start(f32[80,128]{1,0:T(8,128)S(1)} %get-tuple-element.164), channel_id=1, source_target_pairs={{0,1},{1,0},{2,3},{3,2},{4,5},{5,4},{6,7},{7,6},{8,9},{9,8},{10,11... | collective-permute-start | bytes 122888 | tf_op jit(solution)/shard_map/ppermute | solution.py:43
  39.1 7.8 %collective-permute-start.12 = (f32[80,128]{1,0:T(8,128)S(1)}, f32[80,128]{1,0:T(8,128)S(1)}, u32[]{:S(2)}, u32[]{:S(2)}) collective-permute-start(f32[80,128]{1,0:T(8,128)S(1)} %get-tuple-element.189), channel_id=1, source_target_pairs={{0,2},{1,31},{2,4},{3,1},{4,6},{5,3},{6,8},{7,5},{8,10},{9,7},{10,... | collective-permute-start | bytes 122888 | tf_op jit(solution)/shard_map/ppermute | solution.py:43
  39.2 7.7 %collective-permute-start.13 = (f32[80,128]{1,0:T(8,128)S(1)}, f32[80,128]{1,0:T(8,128)S(1)}, u32[]{:S(2)}, u32[]{:S(2)}) collective-permute-start(f32[80,128]{1,0:T(8,128)S(1)} %get-tuple-element.190), channel_id=1, source_target_pairs={{0,31},{1,2},{2,1},{3,4},{4,3},{5,6},{6,5},{7,8},{8,7},{9,10},{10,... | collective-permute-start | bytes 122888 | tf_op jit(solution)/shard_map/ppermute | solution.py:43
  42.0 5.0 %collective-permute-start.14 = (f32[80,128]{1,0:T(8,128)S(1)}, f32[80,128]{1,0:T(8,128)S(1)}, u32[]{:S(2)}, u32[]{:S(2)}) collective-permute-start(f32[80,128]{1,0:T(8,128)S(1)} %get-tuple-element.191), channel_id=1, source_target_pairs={{0,30},{1,3},{2,0},{3,5},{4,2},{5,7},{6,4},{7,9},{8,6},{9,11},{10,... | collective-permute-start | bytes 122888 | tf_op jit(solution)/shard_map/ppermute | solution.py:43
  44.8 2.1 %collective-permute-start.15 = (f32[80,128]{1,0:T(8,128)S(1)}, f32[80,128]{1,0:T(8,128)S(1)}, u32[]{:S(2)}, u32[]{:S(2)}) collective-permute-start(f32[80,128]{1,0:T(8,128)S(1)} %get-tuple-element.192), channel_id=1, source_target_pairs={{0,1},{1,0},{2,3},{3,2},{4,5},{5,4},{6,7},{7,6},{8,9},{9,8},{10,11... | collective-permute-start | bytes 122888 | tf_op jit(solution)/shard_map/ppermute | solution.py:43
